TPU v7x, 32 devices: a whole 2x2x4 slice. The times are simulated.
32 devices in a mesh: dom: 8 (over z, y), feat: 4 (over x, core).
Axes of the slice: x: 2, y: 2, z: 4, core: 2. Of those that a mesh axis runs over, the one named last changes fastest.
Arguments:
- features: float32 [16384, 100], P('dom', 'feat'), may hold values from -6 to 6
- inner_adj: int32 [16384, 2048], P('dom'), may hold values 0 or 1
- bound_adj: int32 [16384, 256], P('dom'), may hold values 0 or 1
- keep_slots: int32 [8, 256], P('dom'), may hold values 0 or 1
- send_index: int32 [8, 8, 32], P('dom'), may hold values from 0 to 2047
- labels: int32 [16384], P('dom'), may hold values from 0 to 46
- train_mask: int32 [16384], P('dom'), may hold values from 0 to 1
- w_in: float32 [2, 100, 256], P(None, 'feat'), may hold values from -0.4375 to 0.4375
- w_mid: float32 [2, 256, 256], P(None, 'feat'), may hold values from -0.25 to 0.25
- w_out: float32 [2, 256, 47], P(None, 'feat'), may hold values from -0.75 to 0.75
- norm_params: float32 [2, 2, 256], P(None, None, 'feat'), as said below
- m_in: float32 [2, 100, 256], P(None, 'feat'), may hold values from -0.00030517578 to 0.00030517578
- m_mid: float32 [2, 256, 256], P(None, 'feat'), may hold values from -0.00030517578 to 0.00030517578
- m_out: float32 [2, 256, 47], P(None, 'feat'), may hold values from -0.00030517578 to 0.00030517578
- m_norms: float32 [2, 2, 256], P(None, None, 'feat'), may hold values from -0.00061035156 to 0.00061035156
- v_in: float32 [2, 100, 256], P(None, 'feat'), may hold values from 2.4112654e-10 to 3.8580246e-09
- v_mid: float32 [2, 256, 256], P(None, 'feat'), may hold values from 2.4112654e-10 to 3.8580246e-09
- v_out: float32 [2, 256, 47], P(None, 'feat'), may hold values from 2.4112654e-10 to 3.8580246e-09
- v_norms: float32 [2, 2, 256], P(None, None, 'feat'), may hold values from 9.645061e-10 to 1.44675925e-08
Outputs:
- loss_sum: float32 [], replicated
- train_count: float32 [], replicated
- grad_norm: float32 [], replicated
- new_in: float32 [2, 100, 256], P(None, 'feat')
- new_mid: float32 [2, 256, 256], P(None, 'feat')
- new_out: float32 [2, 256, 47], P(None, 'feat')
- new_norms: float32 [2, 2, 256], P(None, None, 'feat')
- first_in: float32 [2, 100, 256], P(None, 'feat')
- first_mid: float32 [2, 256, 256], P(None, 'feat')
- first_out: float32 [2, 256, 47], P(None, 'feat')
- first_norms: float32 [2, 2, 256], P(None, None, 'feat')
- second_in: float32 [2, 100, 256], P(None, 'feat')
- second_mid: float32 [2, 256, 256], P(None, 'feat')
- second_out: float32 [2, 256, 47], P(None, 'feat')
- second_norms: float32 [2, 2, 256], P(None, None, 'feat')
- copy_in: bfloat16 [2, 100, 256], P(None, 'feat')
- copy_mid: bfloat16 [2, 256, 256], P(None, 'feat')
- copy_out: bfloat16 [2, 256, 47], P(None, 'feat')
Inputs may be any that keep to these rules, and one draw needn't show every extreme that they name: `norm_params`: gains positive.
All inputs are finite; a program needn't handle non-finite values. No bound on the sum of `inner_adj` or of `bound_adj` or of `keep_slots` on one device may be relied on, other than what follows from the above.
Results may differ from a plain program's by a relative error of at most 0.004.
Values may be sent and summed in bfloat16 or wider, within the bound.
No kernel may reach another device: no remote copies, remote signals or barrier semaphores. Data moves between devices by JAX's collectives and lax.ppermute only.
A program may use at most 128 MiB of HBM per device.

v0:
```python
import jax
import jax.numpy as jnp
from jax import lax
from jax.sharding import PartitionSpec as P

HID = 256
STEP = 5


NORM_EPS = 1e-05
PEN_WEIGHT = 0.001
CLIP_LEVEL = 0.01
RATE = 0.05
BETA_ONE = 0.5
BETA_TWO = 0.5
ADAM_EPS = 1e-08
DECAY = 0.01


def matmul(first_op, second_op):
    return jnp.dot(first_op, second_op, preferred_element_type=jnp.float32)


def contract_rows(first_op, second_op):
    return lax.dot_general(
        first_op, second_op, (((0,), (0,)), ((), ())), preferred_element_type=jnp.float32
    )


def contract_last(first_op, second_op):
    return lax.dot_general(
        first_op, second_op, (((1,), (1,)), ((), ())), preferred_element_type=jnp.float32
    )


def halo_rows(values, send_rows):
    outgoing = values[send_rows]
    incoming = lax.all_to_all(outgoing, "dom", split_axis=0, concat_axis=0, tiled=True)
    return incoming.reshape(-1, values.shape[1])


def halo_back(grads, send_rows, node_count):
    feat_width = grads.shape[1]
    outgoing = grads.reshape(send_rows.shape[0], send_rows.shape[1], feat_width)
    incoming = lax.all_to_all(outgoing, "dom", split_axis=0, concat_axis=0, tiled=True)
    flat_rows = incoming.reshape(-1, feat_width).astype(jnp.float32)
    return jnp.zeros((node_count, feat_width), jnp.float32).at[send_rows.reshape(-1)].add(flat_rows)


def linear(h_low, mean_low, weight, split):
    w_low = weight.astype(jnp.bfloat16)
    partial_out = matmul(h_low, w_low[0]) + matmul(mean_low, w_low[1])
    if split:
        result = lax.psum_scatter(partial_out, "feat", scatter_dimension=1, tiled=True)
    else:
        result = lax.psum(partial_out, "feat")
    return result


def forward_layer(hidden, weight, gain, shift, graph_data, send_rows):
    adj_low, edge_low, inv_deg = graph_data
    h_low = hidden.astype(jnp.bfloat16)
    halo_in = halo_rows(h_low, send_rows)
    summed = matmul(adj_low, h_low) + matmul(edge_low, halo_in)
    mean_low = (summed * inv_deg[:, None]).astype(jnp.bfloat16)
    joined = linear(h_low, mean_low, weight, gain is not None)
    if gain is None:
        return (joined, (h_low, mean_low))
    moments = lax.psum((jnp.sum(joined, 1), jnp.sum(joined * joined, 1)), "feat")
    center = moments[0] / HID
    inv_std = lax.rsqrt(moments[1] / HID - center * center + NORM_EPS)
    x_hat = (joined - center[:, None]) * inv_std[:, None]
    normed = x_hat * gain + shift
    return (jax.nn.silu(normed), (h_low, mean_low, x_hat, inv_std, normed))


def norm_back(grad_out, gain, x_hat, inv_std, normed):
    sig_gate = jax.nn.sigmoid(normed)
    grad_pre = grad_out * sig_gate * (1.0 + normed * (1.0 - sig_gate))
    grad_gain = jnp.sum(grad_pre * x_hat, 0)
    grad_shift = jnp.sum(grad_pre, 0)
    grad_x = grad_pre * gain
    moments = lax.psum((jnp.sum(grad_x, 1), jnp.sum(grad_x * x_hat, 1)), "feat")
    grad_in = inv_std[:, None] * (
        grad_x - moments[0][:, None] / HID - x_hat * moments[1][:, None] / HID
    )
    grad_full = lax.all_gather(grad_in.astype(jnp.bfloat16), "feat", axis=1, tiled=True)
    return (grad_full, grad_gain, grad_shift)


def linear_back(grad_full, h_low, mean_low, weight):
    w_low = weight.astype(jnp.bfloat16)
    grad_w = jnp.stack([contract_rows(h_low, grad_full), contract_rows(mean_low, grad_full)])
    return (grad_w, contract_last(grad_full, w_low[0]), contract_last(grad_full, w_low[1]))


def graph_back(grad_mean, graph_data, send_rows):
    adj_low, edge_low, inv_deg = graph_data
    grad_sum = (grad_mean * inv_deg[:, None]).astype(jnp.bfloat16)
    own_part = contract_rows(adj_low, grad_sum)
    halo_grad = contract_rows(edge_low, grad_sum).astype(jnp.bfloat16)
    return own_part + halo_back(halo_grad, send_rows, adj_low.shape[0])


def adam_step(param, grad, first, second):
    first_new = BETA_ONE * first + (1.0 - BETA_ONE) * grad
    second_new = BETA_TWO * second + (1.0 - BETA_TWO) * grad * grad
    first_hat = first_new / (1.0 - BETA_ONE**STEP)
    second_hat = second_new / (1.0 - BETA_TWO**STEP)
    fresh = param - RATE * (first_hat / (jnp.sqrt(second_hat) + ADAM_EPS) + DECAY * param)
    return (fresh, first_new, second_new)


def shards(
    features,
    inner_adj,
    bound_adj,
    keep_slots,
    send_index,
    labels,
    train_mask,
    w_in,
    w_mid,
    w_out,
    norm_params,
    m_in,
    m_mid,
    m_out,
    m_norms,
    v_in,
    v_mid,
    v_out,
    v_norms,
):
    send_rows = send_index[0]
    edge_int = bound_adj * keep_slots
    degree = (jnp.sum(inner_adj, 1) + jnp.sum(edge_int, 1)).astype(jnp.float32)
    inv_deg = 1.0 / jnp.maximum(degree, 1.0)
    edge_f = edge_int.astype(jnp.float32)
    edge_low = edge_int.astype(jnp.bfloat16)
    graph_data = (inner_adj.astype(jnp.bfloat16), edge_low, inv_deg)
    hidden_one, saved_one = forward_layer(
        features, w_in, norm_params[0, 0], norm_params[0, 1], graph_data, send_rows
    )
    hidden_two, saved_two = forward_layer(
        hidden_one, w_mid, norm_params[1, 0], norm_params[1, 1], graph_data, send_rows
    )
    logits, saved_head = forward_layer(hidden_two, w_out, None, None, graph_data, send_rows)
    row_top = jnp.max(logits, 1, keepdims=True)
    shifted = jnp.exp(logits - row_top)
    row_total = jnp.sum(shifted, 1)
    log_total = row_top[:, 0] + jnp.log(row_total)
    classes = lax.broadcasted_iota(jnp.int32, logits.shape, 1)
    one_hot = (classes == labels[:, None]).astype(jnp.float32)
    target = jnp.sum(logits * one_hot, 1)
    weights = train_mask.astype(jnp.float32)
    pred_low = logits.astype(jnp.bfloat16)
    halo_pred = halo_rows(pred_low, send_rows)
    pred_f = pred_low.astype(jnp.float32)
    halo_f = halo_pred.astype(jnp.float32)
    row_deg = jnp.sum(edge_f, 1)
    col_deg = jnp.sum(edge_f, 0)
    cross_term = contract_last(pred_low, halo_pred)
    penalty = jnp.sum(row_deg * jnp.sum(pred_f * pred_f, 1)) - 2.0 * jnp.sum(edge_f * cross_term)
    penalty = penalty + jnp.sum(col_deg * jnp.sum(halo_f * halo_f, 1))
    totals = lax.psum((jnp.sum(weights * (log_total - target)), penalty, jnp.sum(weights)), "dom")
    loss_sum = totals[0] + PEN_WEIGHT * totals[1]
    count_all = totals[2]
    scale_pen = 2.0 * PEN_WEIGHT / count_all
    grad_ce = weights[:, None] * (shifted / row_total[:, None] - one_hot) / count_all
    grad_own = scale_pen * (row_deg[:, None] * pred_f - matmul(edge_low, halo_pred))
    grad_halo = scale_pen * (col_deg[:, None] * halo_f - contract_rows(edge_low, pred_low))
    returned = halo_back(grad_halo.astype(jnp.bfloat16), send_rows, logits.shape[0])
    grad_logits = (grad_ce + grad_own + returned).astype(jnp.bfloat16)
    grad_head, grad_h, grad_mean = linear_back(grad_logits, saved_head[0], saved_head[1], w_out)
    grad_hidden = grad_h + graph_back(grad_mean, graph_data, send_rows)
    grad_full, gain_two, shift_two = norm_back(
        grad_hidden, norm_params[1, 0], saved_two[2], saved_two[3], saved_two[4]
    )
    grad_second, grad_h, grad_mean = linear_back(grad_full, saved_two[0], saved_two[1], w_mid)
    grad_hidden = grad_h + graph_back(grad_mean, graph_data, send_rows)
    grad_full, gain_one, shift_one = norm_back(
        grad_hidden, norm_params[0, 0], saved_one[2], saved_one[3], saved_one[4]
    )
    grad_first, unused_h, unused_mean = linear_back(grad_full, saved_one[0], saved_one[1], w_in)
    grad_norms = jnp.stack([jnp.stack([gain_one, shift_one]), jnp.stack([gain_two, shift_two])])
    grad_first, grad_second, grad_head, grad_norms = [
        lax.psum(item, "dom") for item in (grad_first, grad_second, grad_head, grad_norms)
    ]
    local_sq = jnp.sum(grad_first * grad_first) + jnp.sum(grad_second * grad_second)
    local_sq = local_sq + jnp.sum(grad_head * grad_head) + jnp.sum(grad_norms * grad_norms)
    grad_norm = jnp.sqrt(lax.psum(local_sq, "feat"))
    factor = jnp.minimum(1.0, CLIP_LEVEL / (grad_norm + 1e-06))
    res_in = adam_step(w_in, grad_first * factor, m_in, v_in)
    res_mid = adam_step(w_mid, grad_second * factor, m_mid, v_mid)
    res_out = adam_step(w_out, grad_head * factor, m_out, v_out)
    res_norm = adam_step(norm_params, grad_norms * factor, m_norms, v_norms)
    return (
        loss_sum,
        count_all,
        grad_norm,
        res_in[0],
        res_mid[0],
        res_out[0],
        res_norm[0],
        res_in[1],
        res_mid[1],
        res_out[1],
        res_norm[1],
        res_in[2],
        res_mid[2],
        res_out[2],
        res_norm[2],
        res_in[0].astype(jnp.bfloat16),
        res_mid[0].astype(jnp.bfloat16),
        res_out[0].astype(jnp.bfloat16),
    )


def solution(mesh):
    placed = (
        P("dom", "feat"),
        P("dom", None),
        P("dom", None),
        P("dom", None),
        P("dom", None, None),
        P("dom"),
        P("dom"),
        P(None, "feat", None),
        P(None, "feat", None),
        P(None, "feat", None),
        P(None, None, "feat"),
        P(None, "feat", None),
        P(None, "feat", None),
        P(None, "feat", None),
        P(None, None, "feat"),
        P(None, "feat", None),
        P(None, "feat", None),
        P(None, "feat", None),
        P(None, None, "feat"),
    )
    return jax.shard_map(
        shards,
        mesh=mesh,
        in_specs=placed,
        out_specs=(
            P(),
            P(),
            P(),
            P(None, "feat", None),
            P(None, "feat", None),
            P(None, "feat", None),
            P(None, None, "feat"),
            P(None, "feat", None),
            P(None, "feat", None),
            P(None, "feat", None),
            P(None, None, "feat"),
            P(None, "feat", None),
            P(None, "feat", None),
            P(None, "feat", None),
            P(None, None, "feat"),
            P(None, "feat", None),
            P(None, "feat", None),
            P(None, "feat", None),
        ),
        check_vma=False,
    )
```

profile of v0, /device:TPU:0, one launch (start us, length us, event | category | flops | bytes accessed | tf_op | source)
XLA Modules:
  0.0 519.0 jit_solution(5677527865139728592)
XLA Ops:
  10.8 7.3 %all-to-all-start = ((bf16[8,2,400]{2,1,0:T(2,128)(2,1)}), bf16[8,2,400]{2,1,0:T(2,128)(2,1)S(1)}, u32[]{:S(2)}, u32[]{:S(2)}) async-start(bf16[8,2,400]{2,1,0:T(2,128)(2,1)} %reshape.231), calls=%async_computation | async-start | bytes 32768 | tf_op jit(solution)/shard_map/all_to_all | solution.py:38
  20.8 13.5 %fusion.41 = (s32[2048]{0:T(1024)S(1)}, bf16[2048,2048]{1,0:T(8,128)(2,1)S(1)}) fusion(s32[2048,2048]{1,0:T(8,128)} %param.20), kind=kLoop, calls=%fused_computation.151 | loop fusion | flops 8386560 | bytes 25174016 | tf_op jit(solution)/shard_map/reduce_sum | solution.py:137
  34.3 2.6 fusion.42
  40.3 3.4 convolution_add_fusion.1
  45.8 30.9 %reduce-scatter.3.cloned.1.call-done = f32[2048,64]{0,1:T(8,128)} async-done(((f32[2048,256]{0,1:T(8,128)}), f32[2048,64]{0,1:T(8,128)}) %reduce-scatter.3.cloned.1.call-update) | async-done | bytes 524304 | tf_op jit(solution)/shard_map/reduce_scatter | solution.py:54
  77.8 10.1 %all-reduce.4 = (f32[2048]{0:T(1024)S(1)}, f32[2048]{0:T(1024)S(1)}) all-reduce(f32[2048]{0:T(1024)S(1)} %get-tuple-element.85, f32[2048]{0:T(1024)S(1)} %get-tuple-element.84), channel_id=1, replica_groups=mesh['dom'=8,'feat'=4] {'feat'}, use_global_device_ids=true, to_apply=%region_6.0 | all-reduce | flops 4096 | bytes 32768 | tf_op jit(solution)/shard_map/psum | solution.py:69
  90.9 6.8 %convolution_bitcast_fusion.3 = f32[2048,64]{0,1:T(8,128)} fusion(bf16[2048,64]{0,1:T(8,128)(2,1)S(1)} %multiply_convert_fusion.4, bf16[2048,2048]{1,0:T(8,128)(2,1)} %copy-done), kind=kOutput, calls=%fused_computation.19 | convolution fusion | flops 536870912 | bytes 9175040 | tf_op jit(solution)/shard_map/dot_general | solution.py:21
  97.7 2.6 gather_fusion.1
  101.9 5.6 %all-to-all-start.1 = ((bf16[8,2,1024]{2,1,0:T(2,128)(2,1)}), bf16[8,2,1024]{2,1,0:T(2,128)(2,1)}, u32[]{:S(2)}, u32[]{:S(2)}) async-start(bf16[8,2,1024]{2,1,0:T(2,128)(2,1)} %reshape.233), calls=%async_computation.2 | async-start | bytes 65536 | tf_op jit(solution)/shard_map/all_to_all | solution.py:38
  107.6 2.6 fusion.27
  110.2 4.2 all-to-all-done.1
  117.4 3.4 convolution_add_fusion
  123.4 26.5 %reduce-scatter.5.cloned.1.call-done = f32[2048,64]{0,1:T(8,128)} async-done(((f32[2048,256]{0,1:T(8,128)}), f32[2048,64]{0,1:T(8,128)}) %reduce-scatter.5.cloned.1.call-update) | async-done | bytes 524304 | tf_op jit(solution)/shard_map/reduce_scatter | solution.py:54
  151.0 10.3 %all-reduce.3 = (f32[2048]{0:T(1024)S(1)}, f32[2048]{0:T(1024)S(1)}) all-reduce(f32[2048]{0:T(1024)S(1)} %get-tuple-element.83, f32[2048]{0:T(1024)S(1)} %get-tuple-element.82), channel_id=1, replica_groups=mesh['dom'=8,'feat'=4] {'feat'}, use_global_device_ids=true, to_apply=%region_11.12 | all-reduce | flops 4096 | bytes 32768 | tf_op jit(solution)/shard_map/psum | solution.py:69
  164.2 6.8 %convolution_bitcast_fusion.2 = f32[2048,64]{0,1:T(8,128)} fusion(bf16[2048,64]{0,1:T(8,128)(2,1)S(1)} %multiply_convert_fusion.3, bf16[2048,2048]{1,0:T(8,128)(2,1)} %copy-done), kind=kOutput, calls=%fused_computation.17 | convolution fusion | flops 536870912 | bytes 9175040 | tf_op jit(solution)/shard_map/dot_general | solution.py:21
  171.1 2.6 gather_fusion.2
  175.2 5.5 %all-to-all-start.2 = ((bf16[8,2,1024]{2,1,0:T(2,128)(2,1)}), bf16[8,2,1024]{2,1,0:T(2,128)(2,1)}, u32[]{:S(2)}, u32[]{:S(2)}) async-start(bf16[8,2,1024]{2,1,0:T(2,128)(2,1)} %reshape.235), calls=%async_computation.4 | async-start | bytes 65536 | tf_op jit(solution)/shard_map/all_to_all | solution.py:38
  182.5 5.1 all-to-all-done.2
  194.7 28.4 %all-reduce.9.cloned.1.call-done = f32[2048,47]{0,1:T(8,128)} async-done(((f32[2048,47]{0,1:T(8,128)}), f32[2048,47]{0,1:T(8,128)}) %all-reduce.9.cloned.1.call-update) | async-done | bytes 385040 | tf_op jit(solution)/shard_map/psum | solution.py:56
  224.8 2.6 fusion.14
  229.3 2.6 gather_fusion.3
  233.5 5.5 %all-to-all-start.3 = ((bf16[8,2,752]{2,1,0:T(2,128)(2,1)}), bf16[8,2,752]{2,1,0:T(2,128)(2,1)}, u32[]{:S(2)}, u32[]{:S(2)}) async-start(bf16[8,2,752]{2,1,0:T(2,128)(2,1)} %reshape.237), calls=%async_computation.5 | async-start | bytes 49152 | tf_op jit(solution)/shard_map/all_to_all | solution.py:38
  240.4 22.5 %psum.126 = f32[]{:T(128)} all-reduce(f32[]{:T(128)} %get-tuple-element.88), channel_id=1, replica_groups=mesh['dom'=8,'feat'=4] {'dom'}, use_global_device_ids=true, to_apply=%region_27.28 | all-reduce | flops 1 | bytes 8 | tf_op jit(solution)/shard_map/psum | solution.py:166
  271.5 4.0 all-to-all-start.4
  275.5 3.0 fusion.8
  278.5 2.3 copy.98
  283.6 4.3 scatter_custom_fusion
  295.4 4.6 all-to-all-start.5
  300.0 5.9 %fusion = f32[2048,64]{0,1:T(8,128)} fusion(f32[2048,64]{0,1:T(8,128)} %fusion.29, bf16[2048,64]{0,1:T(8,128)(2,1)} %copy-done.11, bf16[2048,2048]{1,0:T(8,128)(2,1)} %copy-done), kind=kOutput, calls=%fused_computation.14 | convolution fusion | flops 537001984 | bytes 9699328 | tf_op jit(solution)/shard_map/dot_general | solution.py:25
  305.9 2.4 copy.101
  309.8 4.3 scatter_custom_fusion.1
  314.1 2.3 copy.102
  316.4 3.2 multiply_reduce_fusion.1
  319.6 11.4 %all-reduce.2 = (f32[2048]{0:T(1024)}, f32[2048]{0:T(1024)}) all-reduce(f32[2048]{0:T(1024)} %get-tuple-element.77, f32[2048]{0:T(1024)} %get-tuple-element.78), channel_id=1, replica_groups=mesh['dom'=8,'feat'=4] {'feat'}, use_global_device_ids=true, to_apply=%region_33.34 | all-reduce | flops 4096 | bytes 32768 | tf_op jit(solution)/shard_map/psum | solution.py:83
  331.7 2.1 multiply_convert_fusion.2
  334.1 17.1 %all-gather.3.cloned.1.call-done = bf16[2048,256]{0,1:T(8,128)(2,1)} async-done(((bf16[2048,64]{0,1:T(8,128)(2,1)}), bf16[2048,256]{0,1:T(8,128)(2,1)}) %all-gather.3.cloned.1.call-update) | async-done | bytes 1048592 | tf_op jit(solution)/shard_map/all_gather | solution.py:87
  352.7 5.9 %convolution_bitcast_fusion = f32[2048,64]{0,1:T(8,128)} fusion(bf16[2048,64]{0,1:T(8,128)(2,1)S(1)} %fusion.6, bf16[2048,2048]{1,0:T(8,128)(2,1)} %copy-done), kind=kOutput, calls=%fused_computation.12 | convolution fusion | flops 536870912 | bytes 9175040 | tf_op jit(solution)/shard_map/dot_general | solution.py:25
  364.2 5.5 %all-to-all-start.6 = ((bf16[8,2,1024]{2,1,0:T(2,128)(2,1)}), bf16[8,2,1024]{2,1,0:T(2,128)(2,1)}, u32[]{:S(2)}, u32[]{:S(2)}) async-start(bf16[8,2,1024]{2,1,0:T(2,128)(2,1)} %reshape.243), calls=%async_computation.8 | async-start | bytes 65536 | tf_op jit(solution)/shard_map/all_to_all | solution.py:45
  369.8 2.2 convolution_add_fusion.2
  372.0 2.5 copy.104
  377.4 4.2 scatter_custom_fusion.2
  383.1 2.6 multiply_reduce_fusion.2
  385.7 11.8 %all-reduce.1 = (f32[2048]{0:T(1024)}, f32[2048]{0:T(1024)}) all-reduce(f32[2048]{0:T(1024)} %get-tuple-element.75, f32[2048]{0:T(1024)} %get-tuple-element.79), channel_id=1, replica_groups=mesh['dom'=8,'feat'=4] {'feat'}, use_global_device_ids=true, to_apply=%region_38.39 | all-reduce | flops 4096 | bytes 32768 | tf_op jit(solution)/shard_map/psum | solution.py:83
  402.6 2.4 fusion.13
  409.9 21.1 %all-reduce.11.cloned.1.call-done = f32[2,64,256]{2,1,0:T(8,128)} async-done(((f32[2,64,256]{2,1,0:T(8,128)}), f32[2,64,256]{2,1,0:T(8,128)}) %all-reduce.11.cloned.1.call-update) | async-done | bytes 131088 | tf_op jit(solution)/shard_map/psum | solution.py:188
  432.6 15.9 %all-gather.5.cloned.1.call-done = bf16[2048,256]{0,1:T(8,128)(2,1)} async-done(((bf16[2048,64]{0,1:T(8,128)(2,1)}), bf16[2048,256]{0,1:T(8,128)(2,1)}) %all-gather.5.cloned.1.call-update) | async-done | bytes 1048592 | tf_op jit(solution)/shard_map/all_gather | solution.py:87
  451.7 38.4 %all-reduce.12 = (f32[]{:T(128)}, f32[]{:T(128)}, f32[2,25,256]{2,1,0:T(8,128)S(1)}, f32[2,64,47]{1,2,0:T(8,128)S(1)}, f32[2,2,64]{2,1,0:T(2,128)S(1)}) all-reduce(f32[]{:T(128)} %get-tuple-element.89, f32[]{:T(128)S(6)} %add.252, f32[2,25,256]{2,1,0:T(8,128)S(1)} %pad_maximum_fusion.1, ...), channel_id=1, replica_groups=mesh['dom'=8,'feat'=4] {'dom'}, use_global_device_ids=true, to_apply=%region_17.18 | all-reduce | flops 19074 | bytes 152592 | tf_op jit(solution)/shard_map/psum | solution.py:166
  494.6 6.5 %psum.135 = f32[]{:T(128)} all-reduce(f32[]{:T(128)S(6)} %add.262), channel_id=1, replica_groups=mesh['dom'=8,'feat'=4] {'feat'}, use_global_device_ids=true, to_apply=%region_51.52 | all-reduce | flops 1 | bytes 8 | tf_op jit(solution)/shard_map/psum | solution.py:192
  (199 shorter events, 97.7 us)
Async XLA Ops:
  8.0 12.8 %copy-start.30 = (s32[1024]{0:T(1024)}, s32[1024]{0:T(1024)S(1)}, u32[]{:S(2)}) copy-start(s32[1024]{0:T(1024)S(1)} %pad_clamp_fusion) | copy-start | bytes 12292
  9.2 25.1 %copy-start.4 = (bf16[2048,25]{1,0:T(8,128)(2,1)}, bf16[2048,25]{1,0:T(8,128)(2,1)S(1)}, u32[]{:S(2)}) copy-start(bf16[2048,25]{1,0:T(8,128)(2,1)S(1)} %copy.89) | copy-start | bytes 307204
  10.8 27.4 %all-to-all-start = ((bf16[8,2,400]{2,1,0:T(2,128)(2,1)}), bf16[8,2,400]{2,1,0:T(2,128)(2,1)S(1)}, u32[]{:S(2)}, u32[]{:S(2)}) async-start(bf16[8,2,400]{2,1,0:T(2,128)(2,1)} %reshape.231), calls=%async_computation | async-start | bytes 32768 | tf_op jit(solution)/shard_map/all_to_all | solution.py:38
  18.1 58.6 %reduce-scatter.3.cloned.1.call-start = ((), (), s32[]{:S(2)}) async-start(), calls=%async_computation.9 | async-start | bytes 2621440 | tf_op jit(solution)/shard_map/reduce_scatter | solution.py:54
  19.0 15.3 %copy-start.27 = (bf16[2,25,256]{2,1,0:T(8,128)(2,1)}, bf16[2,25,256]{2,1,0:T(8,128)(2,1)S(1)}, u32[]{:S(2)}) copy-start(bf16[2,25,256]{2,1,0:T(8,128)(2,1)S(1)} %copy.148) | copy-start | bytes 76804
  34.3 3.6 copy-start
  34.3 3.6 copy-start.1
  34.3 3.5 copy-start.37
  43.7 1.5 copy-start.39
  89.9 17.7 %copy-start.9 = (bf16[2048,64]{0,1:T(8,128)(2,1)}, bf16[2048,64]{0,1:T(8,128)(2,1)S(1)}, u32[]{:S(2)}) copy-start(bf16[2048,64]{0,1:T(8,128)(2,1)S(1)} %multiply_convert_fusion.4) | copy-start | bytes 786436
  101.9 12.4 %all-to-all-start.1 = ((bf16[8,2,1024]{2,1,0:T(2,128)(2,1)}), bf16[8,2,1024]{2,1,0:T(2,128)(2,1)}, u32[]{:S(2)}, u32[]{:S(2)}) async-start(bf16[8,2,1024]{2,1,0:T(2,128)(2,1)} %reshape.233), calls=%async_computation.2 | async-start | bytes 65536 | tf_op jit(solution)/shard_map/all_to_all | solution.py:38
  107.5 42.3 %reduce-scatter.5.cloned.1.call-start = ((), (), s32[]{:S(2)}) async-start(), calls=%async_computation.10 | async-start | bytes 2621440 | tf_op jit(solution)/shard_map/reduce_scatter | solution.py:54
  120.8 1.4 copy-start.21
  175.2 12.3 %all-to-all-start.2 = ((bf16[8,2,1024]{2,1,0:T(2,128)(2,1)}), bf16[8,2,1024]{2,1,0:T(2,128)(2,1)}, u32[]{:S(2)}, u32[]{:S(2)}) async-start(bf16[8,2,1024]{2,1,0:T(2,128)(2,1)} %reshape.235), calls=%async_computation.4 | async-start | bytes 65536 | tf_op jit(solution)/shard_map/all_to_all | solution.py:38
  180.8 42.4 %all-reduce.9.cloned.1.call-start = ((), (), s32[]{:S(2)}) async-start(), calls=%async_computation.11 | async-start | bytes 786432 | tf_op jit(solution)/shard_map/psum | solution.py:56
  189.1 2.3 copy-start.15
  233.5 30.0 %all-to-all-start.3 = ((bf16[8,2,752]{2,1,0:T(2,128)(2,1)}), bf16[8,2,752]{2,1,0:T(2,128)(2,1)}, u32[]{:S(2)}, u32[]{:S(2)}) async-start(bf16[8,2,752]{2,1,0:T(2,128)(2,1)} %reshape.237), calls=%async_computation.5 | async-start | bytes 49152 | tf_op jit(solution)/shard_map/all_to_all | solution.py:38
  271.5 10.6 %all-to-all-start.4 = ((bf16[8,2,752]{2,1,0:T(2,128)(2,1)}), bf16[8,2,752]{2,1,0:T(2,128)(2,1)}, u32[]{:S(2)}, u32[]{:S(2)}) async-start(bf16[8,2,752]{2,1,0:T(2,128)(2,1)} %reshape.239), calls=%async_computation.6 | async-start | bytes 49152 | tf_op jit(solution)/shard_map/all_to_all | solution.py:45
  287.9 2.4 copy-start.19
  295.4 12.9 %all-to-all-start.5 = ((bf16[8,2,1024]{2,1,0:T(2,128)(2,1)}), bf16[8,2,1024]{2,1,0:T(2,128)(2,1)}, u32[]{:S(2)}, u32[]{:S(2)}) async-start(bf16[8,2,1024]{2,1,0:T(2,128)(2,1)} %reshape.241), calls=%async_computation.7 | async-start | bytes 65536 | tf_op jit(solution)/shard_map/all_to_all | solution.py:45
  300.0 51.2 %all-gather.3.cloned.1.call-start = ((), (), s32[]{:S(2)}) async-start(), calls=%async_computation.12 | async-start | bytes 1310720 | tf_op jit(solution)/shard_map/all_gather | solution.py:87
  333.8 97.2 %all-reduce.11.cloned.1.call-start = ((), (), s32[]{:S(2)}) async-start(), calls=%async_computation.14 | async-start | bytes 262144 | tf_op jit(solution)/shard_map/psum | solution.py:188
  352.7 6.8 %copy-start.2 = (bf16[2048,256]{0,1:T(8,128)(2,1)S(1)}, bf16[2048,256]{0,1:T(8,128)(2,1)}, u32[]{:S(2)}) copy-start(bf16[2048,256]{0,1:T(8,128)(2,1)} %all-gather.3.cloned.1.call-done) | copy-start | bytes 3145732
  352.7 6.8 %copy-start.14 = (bf16[2048,64]{0,1:T(8,128)(2,1)S(1)}, bf16[2048,64]{0,1:T(8,128)(2,1)}, u32[]{:S(2)}) copy-start(bf16[2048,64]{0,1:T(8,128)(2,1)} %copy-done.13) | copy-start | bytes 786436
  358.6 1.4 copy-start.10
  359.5 10.2 %copy-start.3 = (bf16[2048,256]{0,1:T(8,128)(2,1)S(1)}, bf16[2048,256]{0,1:T(8,128)(2,1)}, u32[]{:S(2)}) copy-start(bf16[2048,256]{0,1:T(8,128)(2,1)} %all-gather.3.cloned.1.call-done) | copy-start | bytes 3145732
  364.2 12.3 %all-to-all-start.6 = ((bf16[8,2,1024]{2,1,0:T(2,128)(2,1)}), bf16[8,2,1024]{2,1,0:T(2,128)(2,1)}, u32[]{:S(2)}, u32[]{:S(2)}) async-start(bf16[8,2,1024]{2,1,0:T(2,128)(2,1)} %reshape.243), calls=%async_computation.8 | async-start | bytes 65536 | tf_op jit(solution)/shard_map/all_to_all | solution.py:45
  369.7 78.7 %all-gather.5.cloned.1.call-start = ((), (), s32[]{:S(2)}) async-start(), calls=%async_computation.13 | async-start | bytes 1310720 | tf_op jit(solution)/shard_map/all_gather | solution.py:87
  371.9 11.1 %copy-start.8 = (f32[2048,64]{0,1:T(8,128)S(1)}, f32[2048,64]{0,1:T(8,128)}, u32[]{:S(2)}) copy-start(f32[2048,64]{0,1:T(8,128)} %reduce-scatter.3.cloned.1.call-done) | copy-start | bytes 1572868
  372.0 11.2 %copy-start.24 = (f32[2048]{0:T(1024)S(1)}, f32[2048]{0:T(1024)}, u32[]{:S(2)}) copy-start(f32[2048]{0:T(1024)} %copy-done.23) | copy-start | bytes 24580
  385.7 21.8 %copy-start.7 = (bf16[2048,47]{1,0:T(8,128)(2,1)S(1)}, bf16[2048,47]{1,0:T(8,128)(2,1)}, u32[]{:S(2)}) copy-start(bf16[2048,47]{1,0:T(8,128)(2,1)} %copy-done.6) | copy-start | bytes 577540
  400.2 6.1 %copy-start.38 = (f32[256]{0:T(256)S(1)}, f32[256]{0:T(256)}, u32[]{:S(2)}) copy-start(f32[256]{0:T(256)} %get-tuple-element.72) | copy-start | bytes 3076
  400.2 9.0 %copy-start.41 = (f32[64]{0:T(128)S(1)}, f32[64]{0:T(128)}, u32[]{:S(2)}) copy-start(f32[64]{0:T(128)} %get-tuple-element.76) | copy-start | bytes 772
  400.2 9.0 %copy-start.42 = (f32[64]{0:T(128)S(1)}, f32[64]{0:T(128)}, u32[]{:S(2)}) copy-start(f32[64]{0:T(128)} %get-tuple-element.81) | copy-start | bytes 772
  402.6 45.8 %copy-start.5 = (bf16[2048,25]{1,0:T(8,128)(2,1)S(1)}, bf16[2048,25]{1,0:T(8,128)(2,1)}, u32[]{:S(2)}) copy-start(bf16[2048,25]{1,0:T(8,128)(2,1)} %copy-done.4) | copy-start | bytes 307204
  408.8 93.0 %copy-start.22 = (f32[2,64,47]{1,0,2:T(2,128)S(1)}, f32[2,64,47]{1,0,2:T(2,128)}, u32[]{:S(2)}) copy-start(f32[2,64,47]{1,0,2:T(2,128)} %param.28) | copy-start | bytes 72196
  408.8 93.0 %copy-start.33 = (f32[2,64,47]{1,0,2:T(2,128)S(1)}, f32[2,64,47]{1,0,2:T(2,128)}, u32[]{:S(2)}) copy-start(f32[2,64,47]{1,0,2:T(2,128)} %param.32) | copy-start | bytes 72196
  408.8 93.0 %copy-start.34 = (f32[2,64,47]{1,0,2:T(2,128)S(1)}, f32[2,64,47]{1,0,2:T(2,128)}, u32[]{:S(2)}) copy-start(f32[2,64,47]{1,0,2:T(2,128)} %param.36) | copy-start | bytes 72196
  409.1 95.3 %copy-start.20 = (f32[2,25,256]{2,0,1:T(2,128)S(1)}, f32[2,25,256]{2,0,1:T(2,128)}, u32[]{:S(2)}) copy-start(f32[2,25,256]{2,0,1:T(2,128)} %param.26) | copy-start | bytes 153604
  409.1 95.3 %copy-start.31 = (f32[2,25,256]{2,0,1:T(2,128)S(1)}, f32[2,25,256]{2,0,1:T(2,128)}, u32[]{:S(2)}) copy-start(f32[2,25,256]{2,0,1:T(2,128)} %param.30) | copy-start | bytes 153604
  409.1 95.3 %copy-start.32 = (f32[2,25,256]{2,0,1:T(2,128)S(1)}, f32[2,25,256]{2,0,1:T(2,128)}, u32[]{:S(2)}) copy-start(f32[2,25,256]{2,0,1:T(2,128)} %param.34) | copy-start | bytes 153604
  432.5 75.9 %copy-start.40 = (f32[2,2,64]{2,1,0:T(2,128)S(1)}, f32[2,2,64]{2,1,0:T(2,128)}, u32[]{:S(2)}) copy-start(f32[2,2,64]{2,1,0:T(2,128)} %param.29) | copy-start | bytes 3076
  432.5 75.9 %copy-start.43 = (f32[2,2,64]{2,1,0:T(2,128)S(1)}, f32[2,2,64]{2,1,0:T(2,128)}, u32[]{:S(2)}) copy-start(f32[2,2,64]{2,1,0:T(2,128)} %param.33) | copy-start | bytes 3076
  432.5 75.9 %copy-start.44 = (f32[2,2,64]{2,1,0:T(2,128)S(1)}, f32[2,2,64]{2,1,0:T(2,128)}, u32[]{:S(2)}) copy-start(f32[2,2,64]{2,1,0:T(2,128)} %param.37) | copy-start | bytes 3076
  432.5 76.6 %copy-start.17 = (f32[2,64,256]{2,1,0:T(8,128)S(1)}, f32[2,64,256]{2,1,0:T(8,128)}, u32[]{:S(2)}) copy-start(f32[2,64,256]{2,1,0:T(8,128)} %param.27) | copy-start | bytes 393220
  432.5 76.6 %copy-start.18 = (f32[2,64,256]{2,1,0:T(8,128)S(1)}, f32[2,64,256]{2,1,0:T(8,128)}, u32[]{:S(2)}) copy-start(f32[2,64,256]{2,1,0:T(8,128)} %all-reduce.11.cloned.1.call-done) | copy-start | bytes 393220
  432.5 76.6 %copy-start.28 = (f32[2,64,256]{2,1,0:T(8,128)S(1)}, f32[2,64,256]{2,1,0:T(8,128)}, u32[]{:S(2)}) copy-start(f32[2,64,256]{2,1,0:T(8,128)} %param.31) | copy-start | bytes 393220
  432.6 76.6 %copy-start.29 = (f32[2,64,256]{2,1,0:T(8,128)S(1)}, f32[2,64,256]{2,1,0:T(8,128)}, u32[]{:S(2)}) copy-start(f32[2,64,256]{2,1,0:T(8,128)} %param.35) | copy-start | bytes 393220
  (10 other events, 7.8 us)
Sparse Core Ops, SparseCore 0:
  43.8 32.7 reduce-scatter.2
  121.0 28.8 reduce-scatter.4
  193.2 29.9 all-reduce.8
  334.0 17.1 all-gather.2
  361.2 69.6 all-reduce.10
  432.4 15.9 all-gather.4
where the time goes:
time: 523 us; the launch traced here: 519 us
  waiting for transfers between devices  153 us (29%)
  blocking collectives  111 us (21%)
  matrix products  67.5 us (13%)
  other arithmetic  62.9 us (12%)
  local copies, waits for them, and re-layouts  62.3 us (12%)
  starting transfers between devices  38.5 us (7%)
  between operations  24.3 us (5%)
    psum x2, blocking collectives, shards(): lax.psum((jnp.sum(weights * (log_total - target)), penalty, jnp.sum(weigh...  60.9 us
    reduce_scatter x2, waiting for transfers between devices, linear(): lax.psum_scatter(partial_out, 'feat', scatter_dimension=1, tiled=True)  57.4 us
    dot_general x13, matrix products, matmul(): return jnp.dot(first_op, second_op, preferred_element_type=jnp.float32)  38.1 us
    all_gather x2, waiting for transfers between devices, norm_back(): lax.all_gather(grad_in.astype(jnp.bfloat16), 'feat', axis=1, tiled=True)  32.9 us
    unnamed x115, local copies, waits for them, and re-layouts  31.8 us
    psum x1, waiting for transfers between devices, linear(): result = lax.psum(partial_out, 'feat')  28.4 us
    all_to_all x4, starting transfers between devices, halo_rows(): lax.all_to_all(outgoing, 'dom', split_axis=0, concat_axis=0, tiled=True)  24 us
    psum x2, blocking collectives, norm_back(): moments = lax.psum((jnp.sum(grad_x, 1), jnp.sum(grad_x * x_hat, 1)), 'feat')  23.2 us
  transfers between devices with their start and end apart: 13, of which 10 were waited for; matrix products, arithmetic and copies ran while one was open for 14% of the time, Pallas kernels for 0%

commit v1 on v0

v1 whole, which is shorter than its diff:
```python
import functools

import jax
import jax.numpy as jnp
from jax import lax
from jax.experimental import pallas as pl
from jax.experimental.pallas import tpu as pltpu
from jax.sharding import PartitionSpec as P

HID = 256
STEP = 5

NORM_EPS = 1e-05
PEN_WEIGHT = 0.001
CLIP_LEVEL = 0.01
RATE = 0.05
BETA_ONE = 0.5
BETA_TWO = 0.5
ADAM_EPS = 1e-08
DECAY = 0.01

BF = jnp.bfloat16
F32 = jnp.float32
LANE = 128
FEAT_PAD = 32
MIB = 1 << 20
CONVERT_TILE = 256

VMEM = pl.BlockSpec(memory_space=pltpu.VMEM)
SMEM = pl.BlockSpec(memory_space=pltpu.SMEM)
ANY = pl.BlockSpec(memory_space=pl.ANY)


def dot_nn(a, b):
    return jnp.dot(a, b, preferred_element_type=F32)


def dot_tn(a, b):
    return lax.dot_general(a, b, (((0,), (0,)), ((), ())), preferred_element_type=F32)


def dot_nt(a, b):
    return lax.dot_general(a, b, (((1,), (1,)), ((), ())), preferred_element_type=F32)


def iota(shape, axis):
    return lax.broadcasted_iota(jnp.int32, shape, axis)


def place(rows, cols, shift, turned=False):
    dims = (cols, rows) if turned else (rows, cols)
    return (iota(dims, int(turned)) + shift == iota(dims, int(not turned))).astype(F32).astype(BF)


def widen(x):
    return x.astype(F32)


def bf_parts(x, count):
    parts = []
    for _ in range(count):
        part = x.astype(BF)
        parts.append(part)
        x = x - widen(part)
    return parts


def rows_of(i, tile):
    return pl.ds(pl.multiple_of(i * tile, tile), tile)


def call(kernel, outs, *args, mib=24, flops=0, smem_in=(), any_in=(), smem_out=(), scratch=()):
    size = sum(a.size * a.dtype.itemsize for a in (*args, *outs))
    return pl.pallas_call(
        kernel,
        out_shape=outs,
        in_specs=[SMEM if i in smem_in else ANY if i in any_in else VMEM for i in range(len(args))],
        out_specs=[SMEM if i in smem_out else VMEM for i in range(len(outs))],
        scratch_shapes=list(scratch),
        cost_estimate=pl.CostEstimate(flops=flops, bytes_accessed=size // 4, transcendentals=0),
        compiler_params=pltpu.CompilerParams(vmem_limit_bytes=mib * MIB),
    )(*args)


def shape(*dims, dtype=F32):
    return jax.ShapeDtypeStruct(dims, dtype)


def pack_kernel(idx_ref, feat_ref, w_in_ref, w_mid_ref, w_out_ref, norm_ref, at_ref, sel_ref, pack_ref, at_out):
    at_out[0] = at_ref[0]
    slots, nodes = sel_ref.shape
    parts, each = idx_ref.shape[1:]
    eye = iota((each, each), 0) == iota((each, each), 1)
    for p in range(parts):
        column = jnp.sum(jnp.where(eye, idx_ref[0, p : p + 1, :].astype(F32), 0.0), 1, keepdims=True)
        hot = iota((each, nodes), 1) == column.astype(jnp.int32)
        sel_ref[p * each : (p + 1) * each, :] = hot.astype(F32).astype(BF)

    width, share = feat_ref.shape[0], w_mid_ref.shape[1]
    rows = dot_nn(place(FEAT_PAD, width, 0), feat_ref[...].astype(BF))
    ones = iota((FEAT_PAD, nodes), 0) == FEAT_PAD - 1
    blocks = [jnp.zeros((FEAT_PAD, HID), F32) for _ in range(3)]
    for layer in range(2):
        for p, part in enumerate(bf_parts(norm_ref[layer], 3)):
            part = dot_nn(part, place(share, HID, 0)).astype(BF)
            blocks[p] = blocks[p] + dot_nn(place(2, FEAT_PAD, NORM_AT + 2 * layer, turned=True), part)
    blocks.append(jnp.zeros((FEAT_PAD, nodes - 3 * HID), F32))
    pack_ref[0:FEAT_PAD, :] = (jnp.where(ones, 1.0, rows) + jnp.concatenate(blocks, 1)).astype(BF)
    for k in range(2):
        for r in range(0, share, 16):
            b = (k * share + r) // 16
            pack_ref[MID_AT : MID_AT + 16, b * HID : (b + 1) * HID] = w_mid_ref[k, r : r + 16, :].astype(BF)
        spread = dot_nn(place(FEAT_PAD, width, 0), w_in_ref[:, k, :].astype(BF)).astype(BF)
        for r in range(0, FEAT_PAD, 16):
            b = (share + k * FEAT_PAD + r) // 16
            pack_ref[OUT_AT : OUT_AT + 16, b * HID : (b + 1) * HID] = spread[r : r + 16, :]
        classes = w_out_ref.shape[0]
        turned = dot_tn(w_out_ref[:, k, :].astype(BF), place(classes, LANE, 0)).astype(BF)
        for r in range(0, share, 16):
            b = r // 16
            pack_ref[OUT_AT : OUT_AT + 16, b * HID + k * LANE : b * HID + (k + 1) * LANE] = turned[r : r + 16, :]


MID_AT = FEAT_PAD
OUT_AT = FEAT_PAD + 16
NORM_AT = FEAT_PAD - 6
PACK_ROWS = FEAT_PAD + 32


def convert_kernel(adj_ref, bound_ref, keep_ref, after_ref, adj_out, edge_out):
    del after_ref
    adj_out[...] = adj_ref[...].astype(F32).astype(BF)
    edge_out[...] = (bound_ref[...] * keep_ref[...]).astype(F32).astype(BF)


def convert(adj, bound, keep, after):
    rows, nodes = adj.shape
    halo = bound.shape[1]

    def tile(width):
        return pl.BlockSpec((CONVERT_TILE, width), lambda i: (i, 0))

    return pl.pallas_call(
        convert_kernel,
        grid=(rows // CONVERT_TILE,),
        in_specs=[tile(nodes), tile(halo), pl.BlockSpec((1, halo), lambda i: (0, 0)), pl.BlockSpec(memory_space=pl.ANY)],
        out_specs=[tile(nodes), tile(halo)],
        out_shape=[shape(rows, nodes, dtype=BF), shape(rows, halo, dtype=BF)],
        cost_estimate=pl.CostEstimate(flops=0, bytes_accessed=6 * MIB, transcendentals=0),
        compiler_params=pltpu.CompilerParams(vmem_limit_bytes=16 * MIB),
    )(adj, bound, keep, after)


def spread_kernel(packed_ref, sel_ref, after_ref, ft_ref, send_ref):
    del after_ref
    feats = packed_ref.shape[0]
    row = iota((FEAT_PAD, ft_ref.shape[1]), 0)
    for f in range(feats):
        rows = widen(packed_ref[f, 0:FEAT_PAD, :])
        keep = (row < NORM_AT) | (row == FEAT_PAD - 1)
        ft_ref[f * FEAT_PAD : (f + 1) * FEAT_PAD, :] = jnp.where(keep, rows, 0.0).astype(BF)
    send_ref[...] = dot_nt(sel_ref[...], ft_ref[...]).astype(BF)


def place_back(share, f):
    row, col = iota((HID, HID), 0), iota((HID, HID), 1)
    return ((row + f * share == col) & (row < share)).astype(F32).astype(BF)


def unpack(packed_ref, win_ref, wmid_ref, wout_ref, norm_ref):
    feats = packed_ref.shape[0]
    share = HID // feats
    norms = jnp.zeros((8, HID), F32)
    pick = place(8, FEAT_PAD, NORM_AT)
    for f in range(feats):
        for k in range(2):
            for r in range(0, share, 16):
                b = (k * share + r) // 16
                wmid_ref[k, f * share + r : f * share + r + 16, :] = packed_ref[f, MID_AT : MID_AT + 16, b * HID : (b + 1) * HID]
                b = r // 16
                wout_ref[k, f * share + r : f * share + r + 16, :] = packed_ref[
                    f, OUT_AT : OUT_AT + 16, b * HID + k * LANE : b * HID + (k + 1) * LANE
                ]
            for r in range(0, FEAT_PAD, 16):
                b = (share + k * FEAT_PAD + r) // 16
                win_ref[k, f * FEAT_PAD + r : f * FEAT_PAD + r + 16, :] = packed_ref[
                    f, OUT_AT : OUT_AT + 16, b * HID : (b + 1) * HID
                ]
        for p in range(3):
            part = dot_nn(pick, packed_ref[f, 0:FEAT_PAD, p * HID : (p + 1) * HID]).astype(BF)
            norms = norms + dot_nn(part, place_back(share, f))
    norm_ref[...] = norms


TILE = 1024


def both(x):
    return jnp.concatenate([x, x], 1)


def loop(count, tile, body, carry=0):
    return lax.fori_loop(0, count // tile, lambda i, c: body(rows_of(i, tile), c), carry)


def norm_forward(joined, norm_ref, layer):
    center = jnp.sum(joined, 1, keepdims=True) * (1.0 / HID)
    spread = jnp.sum(joined * joined, 1, keepdims=True) * (1.0 / HID) - center * center
    inv_std = lax.rsqrt(spread + NORM_EPS)
    x_hat = (joined - center) * inv_std
    normed = x_hat * norm_ref[2 * layer : 2 * layer + 1, :] + norm_ref[2 * layer + 1 : 2 * layer + 2, :]
    gate = 0.5 * jnp.tanh(0.5 * normed) + 0.5
    return inv_std, x_hat, normed * gate, gate * (1.0 + normed * (1.0 - gate))


def keep_norm(s, parts, xhat_ref, slope_ref, istd_ref, h_ref):
    inv_std, x_hat, hidden, slope = parts
    xhat_ref[s, :] = x_hat
    slope_ref[s, :] = slope
    istd_ref[s, :] = jnp.broadcast_to(inv_std, (x_hat.shape[0], LANE))
    h_ref[s, :] = hidden.astype(BF)


def first_kernel(adj_ref, edge_ref, recv_ref, packed_ref, ft_ref, sel_ref,
                 row_ref, col_ref, wmid_ref, wout_ref, norm_ref,
                 mean_ref, xhat_ref, slope_ref, istd_ref, h_ref, invd_ref, send_ref, win_ref):
    nodes, halo = edge_ref.shape
    unpack(packed_ref, win_ref, wmid_ref, wout_ref, norm_ref)

    row_ref[...] = dot_nn(edge_ref[...], jnp.ones((halo, LANE), BF))
    col_ref[...] = dot_tn(edge_ref[...], jnp.ones((nodes, LANE), BF))

    def gather(s, _):
        summed = dot_nt(adj_ref[s, :], ft_ref[...]) + dot_nn(edge_ref[s, :], recv_ref[...])
        inv_deg = 1.0 / jnp.maximum(summed[:, LANE - 1 : LANE], 1.0)
        invd_ref[s, :] = jnp.broadcast_to(inv_deg, summed.shape)
        mean_ref[s, :] = (summed * inv_deg).astype(BF)
        return 0

    loop(nodes, TILE, gather)

    def apply(s, _):
        joined = dot_tn(ft_ref[:, s], win_ref[0]) + dot_nn(mean_ref[s, :], win_ref[1])
        keep_norm(s, norm_forward(joined, norm_ref, 0), xhat_ref, slope_ref, istd_ref, h_ref)
        return 0

    loop(nodes, TILE, apply)
    send_ref[...] = dot_nn(sel_ref[...], h_ref[...]).astype(BF)


def gather_mean(adj_ref, hin_ref, edge_ref, halo_ref, invd_ref, mean_ref):
    def gather(s, _):
        summed = dot_nn(adj_ref[s, :], hin_ref[...]) + dot_nn(edge_ref[s, :], halo_ref[...])
        mean_ref[s, :] = (summed * both(invd_ref[s, :])).astype(BF)
        return 0

    loop(adj_ref.shape[0], TILE, gather)


def second_kernel(adj_ref, edge_ref, halo_ref, hin_ref, w_ref, norm_ref, invd_ref, sel_ref,
                  mean_ref, xhat_ref, slope_ref, istd_ref, h_ref, send_ref):
    gather_mean(adj_ref, hin_ref, edge_ref, halo_ref, invd_ref, mean_ref)

    def apply(s, _):
        joined = dot_nn(hin_ref[s, :], w_ref[0]) + dot_nn(mean_ref[s, :], w_ref[1])
        keep_norm(s, norm_forward(joined, norm_ref, 1), xhat_ref, slope_ref, istd_ref, h_ref)
        return 0

    loop(adj_ref.shape[0], TILE, apply)
    send_ref[...] = dot_nn(sel_ref[...], h_ref[...]).astype(BF)


def split_count(x):
    high = jnp.floor(x * (1.0 / 256.0))
    return high, x - 256.0 * high


def head_kernel(adj_ref, edge_ref, halo_ref, hin_ref, w_ref, invd_ref, sel_ref, mask_ref, col_ref,
                mean_ref, logit_ref, pred_ref, cross_ref, mine_ref, send_ref):
    gather_mean(adj_ref, hin_ref, edge_ref, halo_ref, invd_ref, mean_ref)

    def apply(s, _):
        logits = dot_nn(hin_ref[s, :], w_ref[0]) + dot_nn(mean_ref[s, :], w_ref[1])
        logit_ref[s, :] = logits
        pred_ref[s, :] = logits.astype(BF)
        return 0

    loop(adj_ref.shape[0], TILE, apply)
    mine = dot_nn(sel_ref[...], pred_ref[...])
    mine_ref[...] = mine
    cross = dot_tn(edge_ref[...], pred_ref[...])
    cross_ref[...] = cross
    high, low = bf_parts(cross, 2)
    count = jnp.sum(mask_ref[...].astype(F32), keepdims=True)
    lane = iota(mine.shape, 1)
    count_high, count_low = split_count(count)
    col_high, col_low = split_count(col_ref[...])
    extra = jnp.where(lane == 64, count_high, 0.0) + jnp.where(lane == 65, count_low, 0.0)
    extra = extra + jnp.where(lane == 66, col_high, 0.0) + jnp.where(lane == 67, col_low, 0.0)
    send_ref[:, 0:LANE] = (mine + pltpu.roll(widen(low), 64, 1)).astype(BF)
    send_ref[:, LANE:] = (widen(high) + extra).astype(BF)


def spread_row(values, row):
    pick = (iota(values.shape, 0) == row).astype(F32).astype(BF)
    return dot_tn(values.astype(F32).astype(BF), pick)


def logit_grad_kernel(logit_ref, label_ref, mask_ref, row_ref, pred_ref, edge_ref, recv_ref, mine_ref, cross_ref, col_ref,
                      sel_ref, w_ref, invd_ref,
                      grad_ref, gs_ref, send_ref, loss_ref, hp_ref, ret_ref, lab_ref, wgt_ref, *, classes, each):
    slots = mine_ref.shape[0]
    nodes = logit_ref.shape[0]
    first, second = widen(recv_ref[:, 0:LANE]), widen(recv_ref[:, LANE:])
    lane = iota((slots, LANE), 1)
    low_half = lane < 64
    halo_pred = jnp.where(low_half, first, 0.0)
    back_cross = jnp.where(low_half, second + pltpu.roll(first, 64, 1), 0.0)
    count = 256.0 * jnp.sum(jnp.where(lane == 64, second, 0.0), keepdims=True)
    count = (count + jnp.sum(jnp.where(lane == 65, second, 0.0), keepdims=True)) * (1.0 / each)
    col_back = 256.0 * second[:, 66:67] + second[:, 67:68]
    scale = 2.0 * PEN_WEIGHT / count
    inv_count = 1.0 / count
    hp_ref[...] = halo_pred.astype(BF)
    ret_ref[...] = (scale * (col_back * mine_ref[...] - back_cross)).astype(BF)
    pen = jnp.sum(col_ref[...] * (halo_pred * halo_pred), keepdims=True)
    pen = pen - 2.0 * jnp.sum(halo_pred * cross_ref[...], keepdims=True)
    for r in range(nodes // LANE):
        lab_ref[r * LANE : (r + 1) * LANE, :] = spread_row(label_ref[...], r)
        wgt_ref[r * LANE : (r + 1) * LANE, :] = spread_row(mask_ref[...], r)

    def body(s, carry):
        ce_sum, pen_sum = carry
        logits = logit_ref[s, :]
        lane = iota(logits.shape, 1)
        real = lane < classes
        top = jnp.max(jnp.where(real, logits, -jnp.inf), 1, keepdims=True)
        shifted = jnp.where(real, jnp.exp(jnp.where(real, logits - top, 0.0)), 0.0)
        total = jnp.sum(shifted, 1, keepdims=True)
        hot = (lane.astype(F32) == lab_ref[s, :]).astype(F32)
        target = jnp.sum(logits * hot, 1, keepdims=True)
        weight = wgt_ref[s, :]
        ce_sum = ce_sum + jnp.sum(weight[:, 0:1] * (top + jnp.log(total) - target), keepdims=True)
        pred = widen(pred_ref[s, :])
        drawn = row_ref[s, :] * pred
        pen_sum = pen_sum + jnp.sum(drawn * pred, keepdims=True)
        own = drawn - dot_nn(edge_ref[s, :], hp_ref[...])
        back = dot_tn(sel_ref[:, s], ret_ref[...])
        grad = ((inv_count * weight) * (shifted * (1.0 / total) - hot) + scale * own + back).astype(BF)
        grad_ref[s, :] = grad
        gs_ref[s, :] = (dot_nt(grad, w_ref[1]) * both(invd_ref[s, :])).astype(BF)
        return ce_sum, pen_sum

    zero = jnp.zeros((1, 1), F32)
    ce_sum, pen_sum = loop(nodes, TILE, body, (zero, zero))
    row = iota((8, LANE), 0)
    loss_ref[...] = (jnp.where(row == 0, ce_sum, 0.0) + jnp.where(row == 1, pen + pen_sum, 0.0)
                     + jnp.where(row == 2, count, 0.0))
    send_ref[...] = dot_tn(edge_ref[...], gs_ref[...]).astype(BF)


BACK_TILE = 512


def layer_back(adj_ref, gs_ref, grad_ref, w_ref, sel_ref, halo_ref, slope_ref, xhat_ref, istd_ref, norm_ref, layer, own_ref, gj_ref):
    nodes = adj_ref.shape[0]

    def pull(s, _):
        own_ref[s, :] = (dot_tn(adj_ref[:, s], gs_ref[...]) + dot_nt(grad_ref[s, :], w_ref[0])
                         + dot_tn(sel_ref[:, s], halo_ref[...]))
        return 0

    loop(nodes, BACK_TILE, pull)

    def body(s, carry):
        gain_sum, bias_sum = carry
        grad_pre = own_ref[s, :] * slope_ref[s, :]
        x_hat = xhat_ref[s, :]
        grad_x = grad_pre * norm_ref[2 * layer : 2 * layer + 1, :]
        mean_one = jnp.sum(grad_x, 1, keepdims=True) * (1.0 / HID)
        mean_two = jnp.sum(grad_x * x_hat, 1, keepdims=True) * (1.0 / HID)
        gj_ref[s, :] = (both(istd_ref[s, :]) * (grad_x - mean_one - x_hat * mean_two)).astype(BF)
        gain_sum = gain_sum + jnp.sum(grad_pre * x_hat, 0, keepdims=True)
        bias_sum = bias_sum + jnp.sum(grad_pre, 0, keepdims=True)
        return gain_sum, bias_sum

    zero = jnp.zeros((1, HID), F32)
    return loop(nodes, TILE, body, (zero, zero))


def second_back_kernel(adj_ref, gsin_ref, grad_ref, wout_ref, recv_ref, sel_ref, slope_ref, xhat_ref, istd_ref, norm_ref, w_ref,
                       invd_ref, edge_ref, h_two_ref, mean_head_ref, h_one_ref, mean_two_ref, at_ref,
                       gj_ref, gs_ref, send_ref, sums_ref, own_ref, full_ref, head_ref, *, each):
    gain_sum, bias_sum = layer_back(
        adj_ref, gsin_ref, grad_ref, wout_ref, sel_ref, recv_ref, slope_ref, xhat_ref, istd_ref, norm_ref, 1, own_ref, gj_ref
    )
    row = iota((8, HID), 0)
    sums_ref[...] = jnp.where(row == 2, gain_sum, 0.0) + jnp.where(row == 3, bias_sum, 0.0)

    def body(s, _):
        gs_ref[s, :] = (dot_nt(gj_ref[s, :], w_ref[1]) * both(invd_ref[s, :])).astype(BF)
        return 0

    loop(adj_ref.shape[0], TILE, body)
    parts = send_ref.shape[0]
    send_ref[:, 0:each, :] = dot_tn(edge_ref[...], gs_ref[...]).astype(BF).reshape(parts, each, HID)
    head_ref[:, 0:LANE] = dot_tn(h_two_ref[...], grad_ref[...])
    head_ref[:, LANE:] = dot_tn(mean_head_ref[...], grad_ref[...])
    full_ref[0] = dot_tn(h_one_ref[...], gj_ref[...])
    full_ref[1] = dot_tn(mean_two_ref[...], gj_ref[...])
    share = HID // FEATS
    start = at_ref[0] * share
    for q in range(parts):
        if q * 16 < 2 * share:
            k, r = divmod(q * 16, share)
            send_ref[q, each : each + 16, :] = full_ref[k, pl.ds(pl.multiple_of(start + r, 16), 16), :].astype(BF)
            rows = head_ref[pl.ds(pl.multiple_of(start + q * 8, 8), 8), :]
            high, low = bf_parts(rows, 2)
            send_ref[q, each + 16 : each + 32, :] = jnp.concatenate([widen(high), widen(low)], 0).astype(BF)
        else:
            send_ref[q, each : each + 32, :] = jnp.zeros((32, HID), BF)


FEATS = 4


def first_back_kernel(adj_ref, gsin_ref, grad_ref, w_ref, recv_ref, sel_ref, slope_ref, xhat_ref, istd_ref, norm_ref,
                      ft_ref, mean_ref, loss_ref, sums_ref, at_ref,
                      send_ref, gj_ref, own_ref, full_ref, halo_ref, *, each):
    parts = recv_ref.shape[0]
    halo_ref[...] = recv_ref[:, 0:each, :].reshape(halo_ref.shape)
    gain_sum, bias_sum = layer_back(
        adj_ref, gsin_ref, grad_ref, w_ref, sel_ref, halo_ref, slope_ref, xhat_ref, istd_ref, norm_ref, 0, own_ref, gj_ref
    )
    row = iota((8, HID), 0)
    sums = sums_ref[...] + jnp.where(row == 0, gain_sum, 0.0) + jnp.where(row == 1, bias_sum, 0.0)
    full_ref[0] = dot_nn(ft_ref[...], gj_ref[...])
    full_ref[1] = dot_tn(mean_ref[...], gj_ref[...])
    at = rows_of(at_ref[0], FEAT_PAD)
    mid = jnp.zeros((16, HID), F32)
    out = jnp.zeros((16, HID), F32)
    for q in range(parts):
        mid = mid + widen(recv_ref[q, each : each + 16, :])
        out = out + widen(recv_ref[q, each + 16 : each + 32, :])
    out = out + pltpu.roll(out, 8, 0)
    mid_high, mid_low = bf_parts(mid, 2)
    out_high, out_low = bf_parts(out, 2)
    out = jnp.where(iota((16, HID), 0) < 8, widen(out_high), widen(out_low))
    high, low = bf_parts(sums, 2)
    lane = iota((8, HID), 1)
    tail = jnp.zeros((8, HID), F32)
    for which in range(2):
        for p, part in enumerate(bf_parts(jnp.broadcast_to(loss_ref[which : which + 1, 0:1], (8, HID)), 3)):
            tail = tail + jnp.where((lane == p) & (row == which), widen(part), 0.0)
    message = jnp.concatenate(
        [full_ref[0, at, :], full_ref[1, at, :], jnp.where(row < 4, widen(high), 0.0) + pltpu.roll(widen(low), 4, 0), tail,
         widen(mid_high), widen(mid_low), out], 0
    ).astype(BF)
    for q in range(parts):
        send_ref[q] = message


NORM_ROW = 2 * FEAT_PAD
CHUNK_ROW = NORM_ROW + 16
MESSAGE_ROWS = CHUNK_ROW + 48


def total_kernel(recv_ref, grads_ref, mid_ref, out_ref, square_ref, *, width):
    parts = recv_ref.shape[0]
    grads = jnp.zeros((CHUNK_ROW, HID), F32)
    for q in range(parts):
        grads = grads + widen(recv_ref[q, 0:CHUNK_ROW, :])
    norms = grads[NORM_ROW : NORM_ROW + 8, :]
    norms = jnp.where(iota((8, HID), 0) < 4, norms + pltpu.roll(norms, 4, 0), 0.0)
    grads_ref[...] = grads
    grads_ref[NORM_ROW : NORM_ROW + 8, :] = norms
    for q in range(mid_ref.shape[0] // 16):
        at = CHUNK_ROW
        mid_ref[q * 16 : q * 16 + 16, :] = widen(recv_ref[q, at : at + 16, :]) + widen(recv_ref[q, at + 16 : at + 32, :])
        rows = widen(recv_ref[q, at + 32 : at + 48, :])
        out_ref[q * 8 : q * 8 + 8, :] = rows[0:8, :] + rows[8:16, :]
    weight_row = (iota((NORM_ROW, HID), 0) & (FEAT_PAD - 1)) < width
    first = jnp.where(weight_row, grads[0:NORM_ROW, :], 0.0)
    square = jnp.sum(first * first, keepdims=True)
    square = square + jnp.sum(mid_ref[...] * mid_ref[...], keepdims=True)
    square = square + jnp.sum(out_ref[...] * out_ref[...], keepdims=True)
    row = iota((8, LANE), 0)
    square_ref[...] = jnp.where(row == 1, jnp.sum(norms * norms, keepdims=True), square)


def adam(param, grad, first, second):
    first_new = BETA_ONE * first + (1.0 - BETA_ONE) * grad
    second_new = BETA_TWO * second + (1.0 - BETA_TWO) * grad * grad
    first_hat = first_new / (1.0 - BETA_ONE**STEP)
    second_hat = second_new / (1.0 - BETA_TWO**STEP)
    fresh = param - RATE * (first_hat / (jnp.sqrt(second_hat) + ADAM_EPS) + DECAY * param)
    return fresh, first_new, second_new


def update_kernel(grads_ref, gmid_ref, gout_ref, sq0_ref, sq1_ref, sq2_ref, sq3_ref, loss_ref,
                  w_in, w_mid, w_out, norm, m_in, m_mid, m_out, m_norm, v_in, v_mid, v_out, v_norm, at_ref,
                  loss_out, count_out, gnorm_out,
                  nw_in, nw_mid, nw_out, nnorm, nm_in, nm_mid, nm_out, nm_norm, nv_in, nv_mid, nv_out, nv_norm,
                  c_in, c_mid, c_out):
    tail = jnp.sum(grads_ref[NORM_ROW + 8 : NORM_ROW + 16, :], 1, keepdims=True)
    loss_out[...] = tail[0:1] + PEN_WEIGHT * tail[1:2]
    count_out[...] = loss_ref[2:3, 0:1]
    square = (sq0_ref[0:1, 0:1] + sq1_ref[0:1, 0:1]) + (sq2_ref[0:1, 0:1] + sq3_ref[0:1, 0:1])
    grad_norm = jnp.sqrt(square + sq0_ref[1:2, 0:1])
    gnorm_out[...] = grad_norm
    factor = jnp.minimum(1.0, CLIP_LEVEL / (grad_norm + 1e-06))

    def step(index, grad, w, m, v, nw, nm, nv, copy):
        fresh, first, second = adam(w[index], grad * factor, m[index], v[index])
        nw[index], nm[index], nv[index] = fresh, first, second
        if copy is not None:
            copy[index] = fresh.astype(BF)

    every = slice(None)
    width, _, share = w_in.shape[0], 2, w_mid.shape[1]
    classes = w_out.shape[0]
    for k in range(2):
        step((every, k, every), grads_ref[k * FEAT_PAD : k * FEAT_PAD + width, :], w_in, m_in, v_in, nw_in, nm_in, nv_in, c_in)
        step(k, gmid_ref[k * share : (k + 1) * share, :], w_mid, m_mid, v_mid, nw_mid, nm_mid, nv_mid, c_mid)
        turned = jnp.transpose(gout_ref[:, k * LANE : (k + 1) * LANE])[0:classes, :]
        step((every, k, every), turned, w_out, m_out, v_out, nw_out, nm_out, nv_out, c_out)
    whole = grads_ref[NORM_ROW : NORM_ROW + 8, :]
    mine = jnp.zeros((8, share), F32)
    for f in range(HID // share):
        mine = mine + jnp.where(at_ref[0] == f, whole[:, f * share : (f + 1) * share], 0.0)
    for layer in range(2):
        step(layer, mine[2 * layer : 2 * layer + 2, :], norm, m_norm, v_norm, nnorm, nm_norm, nv_norm, None)


def exchange(x, parts):
    return lax.all_to_all(x.reshape(parts, -1, x.shape[-1]), "dom", split_axis=0, concat_axis=0, tiled=True)


def native(w_in, w_mid, w_out, norm):
    return (jnp.transpose(w_in, (1, 0, 2)), w_mid, jnp.transpose(w_out, (2, 0, 1)), norm)


def restore(w_in, w_mid, w_out, *norm):
    return (jnp.transpose(w_in, (1, 0, 2)), w_mid, jnp.transpose(w_out, (1, 2, 0)), *norm)


def shards(
    features,
    inner_adj,
    bound_adj,
    keep_slots,
    send_index,
    labels,
    train_mask,
    w_in,
    w_mid,
    w_out,
    norm_params,
    m_in,
    m_mid,
    m_out,
    m_norms,
    v_in,
    v_mid,
    v_out,
    v_norms,
    *,
    parts,
    feats,
):
    nodes = features.shape[0]
    each = send_index.shape[2]
    halo = parts * each
    classes = w_out.shape[2]
    share = w_mid.shape[1]
    width = features.shape[1]
    run = functools.partial(call, mib=24 if parts <= 16 else 48)
    labels = labels.reshape(nodes // LANE, LANE)
    mask = train_mask.reshape(nodes // LANE, LANE)
    params = native(w_in, w_mid, w_out, norm_params)
    firsts = native(m_in, m_mid, m_out, m_norms)
    seconds = native(v_in, v_mid, v_out, v_norms)
    feat_at = lax.axis_index("feat").astype(jnp.int32).reshape(1)

    def bf(*dims):
        return shape(*dims, dtype=BF)

    sel, packed, at = run(
        pack_kernel, [bf(halo, nodes), bf(PACK_ROWS, nodes), shape(1, dtype=jnp.int32)],
        send_index, features.T, *params, feat_at, smem_in=(6,), smem_out=(2,),
    )
    packed = lax.all_gather(packed, "feat", axis=0)
    adj, edge = convert(inner_adj, bound_adj, keep_slots, packed)
    ft, send = run(spread_kernel, [bf(feats * FEAT_PAD, nodes), bf(halo, LANE)], packed, sel, adj, any_in=(2,))
    recv = exchange(send, parts).reshape(halo, LANE)
    (row_deg, col_deg, wmid, wout, norms,
     mean_one, xhat_one, slope_one, istd_one, h_one, inv_deg, send) = run(
        first_kernel,
        [shape(nodes, LANE), shape(halo, LANE), bf(2, HID, HID), bf(2, HID, LANE), shape(8, HID),
         bf(nodes, LANE), shape(nodes, HID), shape(nodes, HID), shape(nodes, LANE), bf(nodes, HID), shape(nodes, LANE), bf(halo, HID)],
        adj, edge, recv, packed, ft, sel,
        scratch=[pltpu.VMEM((2, feats * FEAT_PAD, HID), BF)],
    )
    halo_one = exchange(send, parts).reshape(halo, HID)
    mean_two, xhat_two, slope_two, istd_two, h_two, send = run(
        second_kernel,
        [bf(nodes, HID), shape(nodes, HID), shape(nodes, HID), shape(nodes, LANE), bf(nodes, HID), bf(halo, HID)],
        adj, edge, halo_one, h_one, wmid, norms, inv_deg, sel,
    )
    halo_two = exchange(send, parts).reshape(halo, HID)
    mean_head, logits, pred, cross, mine, send = run(
        head_kernel,
        [bf(nodes, HID), shape(nodes, LANE), bf(nodes, LANE), shape(halo, LANE), shape(halo, LANE), bf(halo, HID)],
        adj, edge, halo_two, h_two, wout, inv_deg, sel, mask, col_deg,
    )
    recv = exchange(send, parts).reshape(halo, HID)
    grad, grad_sum, send, losses = run(
        functools.partial(logit_grad_kernel, classes=classes, each=each),
        [bf(nodes, LANE), bf(nodes, HID), bf(halo, HID), shape(8, LANE)],
        logits, labels, mask, row_deg, pred, edge, recv, mine, cross, col_deg, sel, wout, inv_deg,
        scratch=[pltpu.VMEM((halo, LANE), BF), pltpu.VMEM((halo, LANE), BF), pltpu.VMEM((nodes, LANE), F32), pltpu.VMEM((nodes, LANE), F32)],
    )
    recv = exchange(send, parts).reshape(halo, HID)
    joined_two, grad_sum, send, norm_sums = run(
        functools.partial(second_back_kernel, each=each),
        [bf(nodes, HID), bf(nodes, HID), bf(parts, each + 32, HID), shape(8, HID)],
        adj, grad_sum, grad, wout, recv, sel, slope_two, xhat_two, istd_two, norms, wmid, inv_deg, edge,
        h_two, mean_head, h_one, mean_two, at, smem_in=(17,),
        scratch=[pltpu.VMEM((nodes, HID), F32), pltpu.VMEM((2, HID, HID), F32), pltpu.VMEM((HID, HID), F32)],
    )
    recv = exchange(send, parts)
    send, = run(
        functools.partial(first_back_kernel, each=each), [bf(parts, MESSAGE_ROWS, HID)],
        adj, grad_sum, joined_two, wmid, recv, sel, slope_one, xhat_one, istd_one, norms, ft, mean_one, losses, norm_sums, at,
        smem_in=(14,),
        scratch=[pltpu.VMEM((nodes, HID), BF), pltpu.VMEM((nodes, HID), F32), pltpu.VMEM((2, feats * FEAT_PAD, HID), F32),
                 pltpu.VMEM((halo, HID), BF)],
    )
    recv = exchange(send, parts)
    grads, gmid, gout, square = run(
        functools.partial(total_kernel, width=width),
        [shape(CHUNK_ROW, HID), shape(2 * share, HID), shape(share, HID), shape(8, LANE)], recv,
    )
    squares = [square]
    for k in range(1, feats):
        squares.append(lax.ppermute(square, "feat", [(s, s ^ k) for s in range(feats)]))
    outs = [shape(1, 1)] * 3 + [shape(*p.shape) for p in params] * 3 + [bf(*p.shape) for p in params[:3]]
    result = run(update_kernel, outs, grads, gmid, gout, *squares, losses, *params, *firsts, *seconds, at, smem_in=(20,))
    return (
        tuple(r.reshape(()) for r in result[:3])
        + restore(*result[3:7]) + restore(*result[7:11]) + restore(*result[11:15]) + restore(*result[15:])
    )


def solution(mesh):
    weight = P(None, "feat", None)
    norm = P(None, None, "feat")
    placed = (
        P("dom", "feat"), P("dom", None), P("dom", None), P("dom", None), P("dom", None, None), P("dom"), P("dom"),
    ) + (weight, weight, weight, norm) * 3
    return jax.shard_map(
        functools.partial(shards, parts=mesh.shape["dom"], feats=mesh.shape["feat"]),
        mesh=mesh,
        in_specs=placed,
        out_specs=(P(), P(), P()) + (weight, weight, weight, norm) * 3 + (weight,) * 3,
        check_vma=False,
    )
```

time: 523 us -> 165 us (0.32)
  waiting for transfers between devices: 153 us -> 21.4 us
  matrix products: 67.5 us -> 0 us
  other arithmetic: 62.9 us -> 0 us
  local copies, waits for them, and re-layouts: 62.3 us -> 14.1 us
  Pallas kernels: 0 us -> 37.9 us
  starting transfers between devices: 38.5 us -> 1.96 us
  blocking collectives: 111 us -> 74.8 us
  between operations: 24.3 us -> 14.3 us
    psum x7 -> x0, blocking collectives: 111 us -> none  [the longest x2 60.9 us: shards(): lax.psum((jnp.sum(weights * (log_total - target)), penalty, jnp.sum(weigh...]
    all_to_all x0 -> x7, blocking collectives: none -> 74.8 us  [exchange(): lax.all_to_all(x.reshape(parts, -1, x.shape[-1]), 'dom', split_axis=0, co...]
    dot_general x29 -> x0, matrix products: 67.5 us -> none  [the longest x13 38.1 us: matmul(): return jnp.dot(first_op, second_op, preferred_element_type=jnp.float32)]
    reduce_scatter x2 -> x0, waiting for transfers between devices: 57.4 us -> none  [linear(): lax.psum_scatter(partial_out, 'feat', scatter_dimension=1, tiled=True)]
    psum x2 -> x0, waiting for transfers between devices: 49.5 us -> none  [the longest x1 28.4 us: linear(): result = lax.psum(partial_out, 'feat')]
    all_to_all x7 -> x0, starting transfers between devices: 38 us -> none  [the longest x4 24 us: halo_rows(): lax.all_to_all(outgoing, 'dom', split_axis=0, concat_axis=0, tiled=True)]
    pallas_call x0 -> x11, Pallas kernels: none -> 37.9 us  [the longest x10 36.8 us: call(): pl.pallas_call(kernel, out_shape=outs, in_specs=[SMEM if i in smem_in els...]
    reduce_sum x16 -> x0, other arithmetic: 33.8 us -> none  [the longest x2 13.9 us: shards(): degree = (jnp.sum(inner_adj, 1) + jnp.sum(edge_int, 1)).astype(jnp.float32)]
  transfers between devices with their start and end apart: 13 -> 4, of which waited for: 10 -> 3; matrix products, arithmetic and copies ran while one was open for 14% -> 0% of each run, Pallas kernels for 0% -> 0%
where the time goes in v1:
time: 165 us
  blocking collectives  74.8 us (45%)
  Pallas kernels  37.9 us (23%)
  waiting for transfers between devices  21.4 us (13%)
  between operations  14.3 us (9%)
  local copies, waits for them, and re-layouts  14.1 us (9%)
  starting transfers between devices  1.96 us (1%)
    all_to_all x7, blocking collectives, exchange(): lax.all_to_all(x.reshape(parts, -1, x.shape[-1]), 'dom', split_axis=0, co...  74.8 us
    pallas_call x10, Pallas kernels, call(): pl.pallas_call(kernel, out_shape=outs, in_specs=[SMEM if i in smem_in els...  36.8 us
    all_gather x1, waiting for transfers between devices, shards(): packed = lax.all_gather(packed, 'feat', axis=0)  19.6 us
    unnamed x48, local copies, waits for them, and re-layouts  14.1 us
  transfers between devices with their start and end apart: 4, of which 3 were waited for; matrix products, arithmetic and copies ran while one was open for 0% of the time, Pallas kernels for 0%

profile of v1, /device:TPU:0, one launch (start us, length us, event | category | flops | bytes accessed | tf_op | source)
XLA Modules:
  0.0 164.5 jit_solution(14100341065627294094)
XLA Ops:
  7.2 0.0 all-gather.3.cloned.1.call-start
  7.2 0.0 copy-start.3
  7.3 0.9 copy-done.3
  8.1 0.9 copy-done.5
  9.1 0.8 copy-done.6
  9.9 0.8 copy-done.8
  10.7 0.7 copy-done.18
  11.4 0.7 copy-done.20
  12.1 1.3 shard_map.322
  13.3 0.0 all-gather.3.cloned.1.call-update
  13.4 19.6 %all-gather.3.cloned.1.call-done = bf16[256,2048]{1,0:T(8,128)(2,1)} async-done(((bf16[64,2048]{1,0:T(8,128)(2,1)}), bf16[256,2048]{1,0:T(8,128)(2,1)}) %all-gather.3.cloned.1.call-update) | async-done | bytes 1048592 | tf_op jit(solution)/shard_map/all_gather | solution.py:592
  32.9 5.8 %copy-done = s32[2048,2048]{1,0:T(8,128)S(1)} copy-done((s32[2048,2048]{1,0:T(8,128)S(1)}, s32[2048,2048]{1,0:T(8,128)}, u32[]{:S(2)}) %copy-start) | copy-done | bytes 16777240
  38.7 1.2 copy-done.1
  39.9 1.6 copy-done.2
  41.5 0.7 copy-done.23
  42.2 1.1 shard_map.323
  43.3 0.4 shard_map.324
  43.8 12.2 %all_to_all.35 = bf16[8,32,128]{2,1,0:T(8,128)(2,1)S(1)} all-to-all(bf16[8,32,128]{2,1,0:T(8,128)(2,1)S(1)} %bitcast.49), channel_id=1, replica_groups=mesh['dom'=8,'feat'=4] {'dom'}, dimensions={0} | all-to-all | bytes 131072 | tf_op jit(solution)/shard_map/all_to_all | solution.py:536
  56.0 6.1 %shard_map.325 = (f32[2048,128]{1,0:T(8,128)S(1)}, f32[256,128]{1,0:T(8,128)S(1)}, bf16[2,256,256]{2,1,0:T(8,128)(2,1)S(1)}, bf16[2,256,128]{2,1,0:T(8,128)(2,1)...) custom-call(bf16[2048,2048]{1,0:T(8,128)(2,1)S(1)} %get-tuple-elemen, ...), custom_call_target="tpu_custom_call" | custom-call | bytes 5425152 | tf_op jit(solution)/shard_map/pallas_call | solution.py:74
  62.1 9.7 %all_to_all.36 = bf16[8,32,256]{2,1,0:T(8,128)(2,1)S(1)} all-to-all(bf16[8,32,256]{2,1,0:T(8,128)(2,1)S(1)} %bitcast.45), channel_id=1, replica_groups=mesh['dom'=8,'feat'=4] {'dom'}, dimensions={0} | all-to-all | bytes 262144 | tf_op jit(solution)/shard_map/all_to_all | solution.py:536
  71.8 5.1 %shard_map.326 = (bf16[2048,256]{1,0:T(8,128)(2,1)S(1)}, f32[2048,256]{1,0:T(8,128)S(1)}, f32[2048,256]{1,0:T(8,128)S(1)}, f32[2048,128]{1,0:T(8,128)S(1)}, bf16...) custom-call(bf16[2048,2048]{1,0:T(8,128)(2,1)S(1)} %get-tuple-element.80.after_ref.adj_ref, ...), custom_call_target="tpu_custom_call" | custom-call | bytes 5113856 | tf_op jit(solution)/shard_map/pallas_call | solution.py:74
  76.9 9.7 %all_to_all.37 = bf16[8,32,256]{2,1,0:T(8,128)(2,1)S(1)} all-to-all(bf16[8,32,256]{2,1,0:T(8,128)(2,1)S(1)} %bitcast.47), channel_id=1, replica_groups=mesh['dom'=8,'feat'=4] {'dom'}, dimensions={0} | all-to-all | bytes 262144 | tf_op jit(solution)/shard_map/all_to_all | solution.py:536
  86.6 0.0 copy-done.16
  86.6 4.5 %shard_map.327 = (bf16[2048,256]{1,0:T(8,128)(2,1)S(1)}, f32[2048,128]{1,0:T(8,128)S(1)}, bf16[2048,128]{1,0:T(8,128)(2,1)S(1)}, f32[256,128]{1,0:T(8,128)S(1)},...) custom-call(bf16[2048,2048]{1,0:T(8,128)(2,1)S(1)} %get-tuple-element.80.after_ref.adj_ref, ...), custom_call_target="tpu_custom_call" | custom-call | bytes 3999744 | tf_op jit(solution)/shard_map/pallas_call | solution.py:74
  91.1 9.7 %all_to_all.38 = bf16[8,32,256]{2,1,0:T(8,128)(2,1)S(1)} all-to-all(bf16[8,32,256]{2,1,0:T(8,128)(2,1)S(1)} %bitcast.48), channel_id=1, replica_groups=mesh['dom'=8,'feat'=4] {'dom'}, dimensions={0} | all-to-all | bytes 262144 | tf_op jit(solution)/shard_map/all_to_all | solution.py:536
  100.8 3.2 %shard_map.328 = (bf16[2048,128]{1,0:T(8,128)(2,1)S(1)}, bf16[2048,256]{1,0:T(8,128)(2,1)S(1)}, bf16[256,256]{1,0:T(8,128)(2,1)S(1)}, f32[8,128]{1,0:T(8,128)S(1)}) custom-call(f32[2048,128]{1,0:T(8,128)S(1)} %get-tuple-element.94.logit_ref, s32[16,128]{1,0:T(8,128)S(1)} %bitcast.56, s32[16,128]{1,0:T(8,128)S(1)} %bitcast.55, ...), custom_call_target="tpu_custom_call" | custom-call | bytes 2036736 | tf_op jit(solution)/shard_map/pallas_call | solution.py:74
  104.0 9.7 %all_to_all.39 = bf16[8,32,256]{2,1,0:T(8,128)(2,1)S(1)} all-to-all(bf16[8,32,256]{2,1,0:T(8,128)(2,1)S(1)} %bitcast.46), channel_id=1, replica_groups=mesh['dom'=8,'feat'=4] {'dom'}, dimensions={0} | all-to-all | bytes 262144 | tf_op jit(solution)/shard_map/all_to_all | solution.py:536
  113.8 7.8 %shard_map.329 = (bf16[2048,256]{1,0:T(8,128)(2,1)S(1)}, bf16[2048,256]{1,0:T(8,128)(2,1)S(1)}, bf16[8,64,256]{2,1,0:T(8,128)(2,1)S(1)}, f32[8,256]{1,0:T(8,128)S(1)}) custom-call(bf16[2048,2048]{1,0:T(8,128)(2,1)S(1)} %get-tuple-element.80.after_ref.adj_ref, bf16[2048,256]{1,0:T(8,128)(2,1)S(1)} %get-tuple-element.100.gsin_ref, ...), custom_call_target="tpu_custom_call" | custom-call | bytes 6361089 | tf_op jit(solution)/shard_map/pallas_call | solution.py:74
  121.5 10.6 %all_to_all.40.recv_ref = bf16[8,64,256]{2,1,0:T(8,128)(2,1)S(1)} all-to-all(bf16[8,64,256]{2,1,0:T(8,128)(2,1)S(1)} %get-tuple-element.111), channel_id=1, replica_groups=mesh['dom'=8,'feat'=4] {'dom'}, dimensions={0} | all-to-all | bytes 524288 | tf_op jit(solution)/shard_map/all_to_all | solution.py:536
  132.2 0.0 copy-start.11
  132.2 0.0 copy-start.12
  132.2 0.0 copy-start.13
  132.2 0.0 copy-start.14
  132.2 0.0 copy-start.15
  132.2 0.0 copy-start.19
  132.2 0.0 copy-start.21
  132.3 0.0 copy-start.22
  132.3 6.2 %shard_map.330 = bf16[8,128,256]{2,1,0:T(8,128)(2,1)S(1)} custom-call(bf16[2048,2048]{1,0:T(8,128)(2,1)S(1)} %get-tuple-element.80.after_ref.adj_ref, bf16[2048,256]{1,0:T(8,128)(2,1)S(1)} %get-tuple-element.109.gsin_ref, bf16[2048,256]{1,0:T(8,128)(2,1)S(1)} %get-tuple-element.110.grad_ref, bf16[2,256,256]{2,1,0:T(8,128)(2,1)S(1)} %get-tuple-element.87.w_ref, ...), custom_call_target="tpu_custom_call" | custom-call | bytes 4723713 | tf_op jit(solution)/shard_map/pallas_call | solution.py:74
  138.4 13.0 %all_to_all.41.recv_ref = bf16[8,128,256]{2,1,0:T(8,128)(2,1)S(1)} all-to-all(bf16[8,128,256]{2,1,0:T(8,128)(2,1)S(1)} %shard_map.330), channel_id=1, replica_groups=mesh['dom'=8,'feat'=4] {'dom'}, dimensions={0} | all-to-all | bytes 1048576 | tf_op jit(solution)/shard_map/all_to_all | solution.py:536
  151.5 0.2 shard_map.331
  151.7 0.1 collective-permute-start.2
  151.8 0.6 collective-permute-start.1
  152.4 1.2 collective-permute-start
  153.6 1.2 collective-permute-done.2.sq3_ref
  154.8 0.7 collective-permute-done.1.sq2_ref
  155.4 0.0 collective-permute-done.sq1_ref
  155.4 0.0 copy-done.7
  155.6 2.1 %shard_map.332 = (f32[1,1]{1,0:T(1,128)}, f32[1,1]{1,0:T(1,128)}, f32[1,1]{1,0:T(1,128)}, f32[25,2,256]{2,1,0:T(2,128)}, f32[2,64,256]{2,1,0:T(8,128)}, /*index=...) custom-call(f32[80,256]{1,0:T(8,128)S(1)} %get-tuple-element.118.gra, ...), custom_call_target="tpu_custom_call" | custom-call | bytes 411588 | tf_op jit(solution)/shard_map/pallas_call | solution.py:74
  (27 shorter events, 0.0 us)
Async XLA Ops:
  7.2 25.7 %all-gather.3.cloned.1.call-start = ((), (), s32[]{:S(2)}) async-start(), calls=%async_computation.7 | async-start | bytes 1310720 | tf_op jit(solution)/shard_map/all_gather | solution.py:592
  7.2 0.9 copy-start.3
  8.1 0.9 copy-start.5
  9.1 0.8 copy-start.6
  9.9 0.8 copy-start.8
  10.7 0.7 copy-start.18
  11.4 0.7 copy-start.20
  32.9 5.8 %copy-start = (s32[2048,2048]{1,0:T(8,128)S(1)}, s32[2048,2048]{1,0:T(8,128)}, u32[]{:S(2)}) copy-start(s32[2048,2048]{1,0:T(8,128)} %adj_ref.1) | copy-start | bytes 50331652
  38.7 1.2 copy-start.1
  39.9 1.6 copy-start.2
  41.5 0.7 copy-start.23
  71.8 14.8 %copy-start.16 = (s32[2048]{0:T(1024)S(1)}, s32[2048]{0:T(1024)}, u32[]{:S(2)}) copy-start(s32[2048]{0:T(1024)} %param.25) | copy-start | bytes 24580
  86.6 14.2 %copy-start.17 = (s32[2048]{0:T(1024)S(1)}, s32[2048]{0:T(1024)}, u32[]{:S(2)}) copy-start(s32[2048]{0:T(1024)} %param.24) | copy-start | bytes 24580
  132.2 23.3 %copy-start.4 = (f32[2,64,256]{2,1,0:T(8,128)S(1)}, f32[2,64,256]{2,1,0:T(8,128)}, u32[]{:S(2)}) copy-start(f32[2,64,256]{2,1,0:T(8,128)} %w_mid.1) | copy-start | bytes 393220
  132.2 23.3 %copy-start.7 = (f32[2,25,256]{2,0,1:T(2,128)S(1)}, f32[2,25,256]{2,0,1:T(2,128)}, u32[]{:S(2)}) copy-start(f32[2,25,256]{2,0,1:T(2,128)} %param.26) | copy-start | bytes 153604
  132.2 23.3 %copy-start.9 = (f32[2,64,47]{1,0,2:T(2,128)S(1)}, f32[2,64,47]{1,0,2:T(2,128)}, u32[]{:S(2)}) copy-start(f32[2,64,47]{1,0,2:T(2,128)} %param.28) | copy-start | bytes 72196
  132.2 23.3 %copy-start.10 = (f32[2,64,256]{2,1,0:T(8,128)S(1)}, f32[2,64,256]{2,1,0:T(8,128)}, u32[]{:S(2)}) copy-start(f32[2,64,256]{2,1,0:T(8,128)} %m_mid.1) | copy-start | bytes 393220
  132.2 23.3 %copy-start.11 = (f32[2,64,256]{2,1,0:T(8,128)S(1)}, f32[2,64,256]{2,1,0:T(8,128)}, u32[]{:S(2)}) copy-start(f32[2,64,256]{2,1,0:T(8,128)} %v_mid.1) | copy-start | bytes 393220
  132.2 23.3 %copy-start.12 = (f32[2,25,256]{2,0,1:T(2,128)S(1)}, f32[2,25,256]{2,0,1:T(2,128)}, u32[]{:S(2)}) copy-start(f32[2,25,256]{2,0,1:T(2,128)} %param.30) | copy-start | bytes 153604
  132.2 23.3 %copy-start.13 = (f32[2,25,256]{2,0,1:T(2,128)S(1)}, f32[2,25,256]{2,0,1:T(2,128)}, u32[]{:S(2)}) copy-start(f32[2,25,256]{2,0,1:T(2,128)} %param.34) | copy-start | bytes 153604
  132.2 23.3 %copy-start.14 = (f32[2,64,47]{1,0,2:T(2,128)S(1)}, f32[2,64,47]{1,0,2:T(2,128)}, u32[]{:S(2)}) copy-start(f32[2,64,47]{1,0,2:T(2,128)} %param.32) | copy-start | bytes 72196
  132.2 23.3 %copy-start.15 = (f32[2,64,47]{1,0,2:T(2,128)S(1)}, f32[2,64,47]{1,0,2:T(2,128)}, u32[]{:S(2)}) copy-start(f32[2,64,47]{1,0,2:T(2,128)} %param.36) | copy-start | bytes 72196
  132.2 23.3 %copy-start.19 = (f32[2,2,64]{2,1,0:T(2,128)S(1)}, f32[2,2,64]{2,1,0:T(2,128)}, u32[]{:S(2)}) copy-start(f32[2,2,64]{2,1,0:T(2,128)} %norm.1) | copy-start | bytes 3076
  132.2 23.3 %copy-start.21 = (f32[2,2,64]{2,1,0:T(2,128)S(1)}, f32[2,2,64]{2,1,0:T(2,128)}, u32[]{:S(2)}) copy-start(f32[2,2,64]{2,1,0:T(2,128)} %m_norm.1) | copy-start | bytes 3076
  132.3 23.3 %copy-start.22 = (f32[2,2,64]{2,1,0:T(2,128)S(1)}, f32[2,2,64]{2,1,0:T(2,128)}, u32[]{:S(2)}) copy-start(f32[2,2,64]{2,1,0:T(2,128)} %v_norm.1) | copy-start | bytes 3076
  151.7 3.1 %collective-permute-start.2 = (f32[8,128]{1,0:T(8,128)S(1)}, f32[8,128]{1,0:T(8,128)S(1)}, u32[]{:S(2)}, u32[]{:S(2)}) collective-permute-start(f32[8,128]{1,0:T(8,128)S(1)} %get-tuple-element.121.sq0_ref), channel_id=1, source_target_pairs={{0,3},{1,2},{2,1},{3,0},{4,7},{5,6},{6,5},{7,4},{8,11},{9,10},{10,... | collective-permute-start | bytes 12296 | tf_op jit(solution)/shard_map/ppermute | solution.py:646
  151.8 3.7 %collective-permute-start.1 = (f32[8,128]{1,0:T(8,128)S(1)}, f32[8,128]{1,0:T(8,128)S(1)}, u32[]{:S(2)}, u32[]{:S(2)}) collective-permute-start(f32[8,128]{1,0:T(8,128)S(1)} %get-tuple-element.121.sq0_ref), channel_id=1, source_target_pairs={{0,2},{1,3},{2,0},{3,1},{4,6},{5,7},{6,4},{7,5},{8,10},{9,11},{10,... | collective-permute-start | bytes 12296 | tf_op jit(solution)/shard_map/ppermute | solution.py:646
  152.4 3.0 %collective-permute-start = (f32[8,128]{1,0:T(8,128)S(1)}, f32[8,128]{1,0:T(8,128)S(1)}, u32[]{:S(2)}, u32[]{:S(2)}) collective-permute-start(f32[8,128]{1,0:T(8,128)S(1)} %get-tuple-element.121.sq0_ref), channel_id=1, source_target_pairs={{0,1},{1,0},{2,3},{3,2},{4,5},{5,4},{6,7},{7,6},{8,9},{9,8},{10,11... | collective-permute-start | bytes 12296 | tf_op jit(solution)/shard_map/ppermute | solution.py:646
Sparse Core Ops, SparseCore 0:
  13.5 19.4 all-gather.2

commit v2 on v1

--- a/solution.py
+++ b/solution.py
@@ -29,6 +29,7 @@
 VMEM = pl.BlockSpec(memory_space=pltpu.VMEM)
 SMEM = pl.BlockSpec(memory_space=pltpu.SMEM)
 ANY = pl.BlockSpec(memory_space=pl.ANY)
+HBM = pl.BlockSpec(memory_space=pltpu.HBM)
 
 
 def dot_nn(a, b):
@@ -65,16 +66,20 @@
     return parts
 
 
+def both(x):
+    return jnp.concatenate([x, x], 1)
+
+
 def rows_of(i, tile):
     return pl.ds(pl.multiple_of(i * tile, tile), tile)
 
 
-def call(kernel, outs, *args, mib=24, flops=0, smem_in=(), any_in=(), smem_out=(), scratch=()):
+def call(kernel, outs, *args, mib=24, flops=0, smem_in=(), any_in=(), hbm_in=(), smem_out=(), scratch=()):
     size = sum(a.size * a.dtype.itemsize for a in (*args, *outs))
     return pl.pallas_call(
         kernel,
         out_shape=outs,
-        in_specs=[SMEM if i in smem_in else ANY if i in any_in else VMEM for i in range(len(args))],
+        in_specs=[SMEM if i in smem_in else ANY if i in any_in else HBM if i in hbm_in else VMEM for i in range(len(args))],
         out_specs=[SMEM if i in smem_out else VMEM for i in range(len(outs))],
         scratch_shapes=list(scratch),
         cost_estimate=pl.CostEstimate(flops=flops, bytes_accessed=size // 4, transcendentals=0),
@@ -86,17 +91,19 @@
     return jax.ShapeDtypeStruct(dims, dtype)
 
 
-def pack_kernel(idx_ref, feat_ref, w_in_ref, w_mid_ref, w_out_ref, norm_ref, at_ref, sel_ref, pack_ref, at_out):
+def pack_kernel(feat_hbm, w_in_hbm, w_mid_hbm, w_out_hbm, norm_hbm, at_ref, pack_ref, at_out,
+                feat_ref, w_in_ref, w_mid_ref, w_out_ref, norm_ref, sems):
+    sources = (feat_hbm, w_mid_hbm, w_in_hbm, w_out_hbm, norm_hbm)
+    targets = (feat_ref, w_mid_ref, w_in_ref, w_out_ref, norm_ref)
+    copies = [pltpu.make_async_copy(src, dst, sems.at[i]) for i, (src, dst) in enumerate(zip(sources, targets))]
+    for copy in copies:
+        copy.start()
     at_out[0] = at_ref[0]
-    slots, nodes = sel_ref.shape
-    parts, each = idx_ref.shape[1:]
-    eye = iota((each, each), 0) == iota((each, each), 1)
-    for p in range(parts):
-        column = jnp.sum(jnp.where(eye, idx_ref[0, p : p + 1, :].astype(F32), 0.0), 1, keepdims=True)
-        hot = iota((each, nodes), 1) == column.astype(jnp.int32)
-        sel_ref[p * each : (p + 1) * each, :] = hot.astype(F32).astype(BF)
-
+    for copy in copies:
+        copy.wait()
+    nodes = feat_ref.shape[1]
     width, share = feat_ref.shape[0], w_mid_ref.shape[1]
+    classes = w_out_ref.shape[0]
     rows = dot_nn(place(FEAT_PAD, width, 0), feat_ref[...].astype(BF))
     ones = iota((FEAT_PAD, nodes), 0) == FEAT_PAD - 1
     blocks = [jnp.zeros((FEAT_PAD, HID), F32) for _ in range(3)]
@@ -105,98 +112,127 @@
             part = dot_nn(part, place(share, HID, 0)).astype(BF)
             blocks[p] = blocks[p] + dot_nn(place(2, FEAT_PAD, NORM_AT + 2 * layer, turned=True), part)
     blocks.append(jnp.zeros((FEAT_PAD, nodes - 3 * HID), F32))
-    pack_ref[0:FEAT_PAD, :] = (jnp.where(ones, 1.0, rows) + jnp.concatenate(blocks, 1)).astype(BF)
+    rows = (jnp.where(ones, 1.0, rows) + jnp.concatenate(blocks, 1)).astype(BF)
+    at = 0
+    for b in range(nodes // HID):
+        pack_ref[at : at + FEAT_PAD, :] = rows[:, b * HID : (b + 1) * HID]
+        at += FEAT_PAD
     for k in range(2):
-        for r in range(0, share, 16):
-            b = (k * share + r) // 16
-            pack_ref[MID_AT : MID_AT + 16, b * HID : (b + 1) * HID] = w_mid_ref[k, r : r + 16, :].astype(BF)
-        spread = dot_nn(place(FEAT_PAD, width, 0), w_in_ref[:, k, :].astype(BF)).astype(BF)
-        for r in range(0, FEAT_PAD, 16):
-            b = (share + k * FEAT_PAD + r) // 16
-            pack_ref[OUT_AT : OUT_AT + 16, b * HID : (b + 1) * HID] = spread[r : r + 16, :]
-        classes = w_out_ref.shape[0]
-        turned = dot_tn(w_out_ref[:, k, :].astype(BF), place(classes, LANE, 0)).astype(BF)
-        for r in range(0, share, 16):
-            b = r // 16
-            pack_ref[OUT_AT : OUT_AT + 16, b * HID + k * LANE : b * HID + (k + 1) * LANE] = turned[r : r + 16, :]
-
-
-MID_AT = FEAT_PAD
-OUT_AT = FEAT_PAD + 16
+        pack_ref[at : at + share, :] = w_mid_ref[k].astype(BF)
+        at += share
+    for k in range(2):
+        pack_ref[at : at + FEAT_PAD, :] = dot_nn(place(FEAT_PAD, width, 0), w_in_ref[:, k, :].astype(BF)).astype(BF)
+        at += FEAT_PAD
+    turned = jnp.zeros((2 * CLASS_HALF, LANE), F32)
+    for k in range(2):
+        grown = dot_nn(place(classes, 2 * CLASS_HALF, 0, turned=True), w_out_ref[:, k, :].astype(BF)).astype(BF)
+        turned = turned + dot_nn(grown, place(share, LANE, k * share))
+    turned = turned.astype(BF)
+    for half in range(2):
+        pack_ref[at : at + CLASS_HALF, half * LANE : (half + 1) * LANE] = turned[half * CLASS_HALF : (half + 1) * CLASS_HALF, :]
+
+
 NORM_AT = FEAT_PAD - 6
-PACK_ROWS = FEAT_PAD + 32
-
-
-def convert_kernel(adj_ref, bound_ref, keep_ref, after_ref, adj_out, edge_out):
+CLASS_HALF = 32
+
+
+def pack_rows(nodes, share):
+    return nodes // HID * FEAT_PAD + 2 * share + 2 * FEAT_PAD + CLASS_HALF
+
+
+def convert_kernel(adj_hbm, bound_hbm, keep_hbm, idx_hbm, adj_ref, edge_ref, row_ref, col_ref, sel_ref,
+                   adj_buf, bound_buf, keep_ref, idx_ref, sems, small_sems):
+    slots, nodes = sel_ref.shape
+    parts, each = idx_ref.shape[1:]
+    steps = nodes // CONVERT_TILE
+
+    def fetch(step, slot):
+        s = rows_of(step, CONVERT_TILE)
+        return (pltpu.make_async_copy(adj_hbm.at[s], adj_buf.at[slot], sems.at[0, slot]),
+                pltpu.make_async_copy(bound_hbm.at[s], bound_buf.at[slot], sems.at[1, slot]))
+
+    small = (pltpu.make_async_copy(idx_hbm, idx_ref, small_sems.at[0]), pltpu.make_async_copy(keep_hbm, keep_ref, small_sems.at[1]))
+    for copy in small:
+        copy.start()
+    for step in range(CONVERT_SLOTS):
+        for copy in fetch(step, step):
+            copy.start()
+    for copy in small:
+        copy.wait()
+    eye = iota((each, each), 0) == iota((each, each), 1)
+    for p in range(parts):
+        column = jnp.sum(jnp.where(eye, idx_ref[0, p : p + 1, :].astype(F32), 0.0), 1, keepdims=True)
+        hot = iota((each, nodes), 1) == column.astype(jnp.int32)
+        sel_ref[p * each : (p + 1) * each, :] = hot.astype(F32).astype(BF)
+
+    def body(step, _):
+        slot = lax.rem(step, CONVERT_SLOTS)
+        s = rows_of(step, CONVERT_TILE)
+        for copy in fetch(step, slot):
+            copy.wait()
+        adj_ref[s, :] = adj_buf[slot].astype(F32).astype(BF)
+        edge = (bound_buf[slot] * keep_ref[...]).astype(F32).astype(BF)
+        edge_ref[s, :] = edge
+        row_ref[s, :] = dot_nn(edge, jnp.ones((slots, LANE), BF))
+        col_ref[...] += dot_tn(edge, jnp.ones((CONVERT_TILE, LANE), BF))
+
+        @pl.when(step + CONVERT_SLOTS < steps)
+        def _():
+            for copy in fetch(step + CONVERT_SLOTS, slot):
+                copy.start()
+
+        return 0
+
+    col_ref[...] = jnp.zeros(col_ref.shape, F32)
+    lax.fori_loop(0, steps, body, 0)
+
+
+CONVERT_SLOTS = 4
+
+
+def spread_kernel(own_ref, core_ref, chip_ref, far_ref, sel_ref, after_ref, at_ref, ft_ref, send_ref):
     del after_ref
-    adj_out[...] = adj_ref[...].astype(F32).astype(BF)
-    edge_out[...] = (bound_ref[...] * keep_ref[...]).astype(F32).astype(BF)
-
-
-def convert(adj, bound, keep, after):
-    rows, nodes = adj.shape
-    halo = bound.shape[1]
-
-    def tile(width):
-        return pl.BlockSpec((CONVERT_TILE, width), lambda i: (i, 0))
-
-    return pl.pallas_call(
-        convert_kernel,
-        grid=(rows // CONVERT_TILE,),
-        in_specs=[tile(nodes), tile(halo), pl.BlockSpec((1, halo), lambda i: (0, 0)), pl.BlockSpec(memory_space=pl.ANY)],
-        out_specs=[tile(nodes), tile(halo)],
-        out_shape=[shape(rows, nodes, dtype=BF), shape(rows, halo, dtype=BF)],
-        cost_estimate=pl.CostEstimate(flops=0, bytes_accessed=6 * MIB, transcendentals=0),
-        compiler_params=pltpu.CompilerParams(vmem_limit_bytes=16 * MIB),
-    )(adj, bound, keep, after)
-
-
-def spread_kernel(packed_ref, sel_ref, after_ref, ft_ref, send_ref):
-    del after_ref
-    feats = packed_ref.shape[0]
-    row = iota((FEAT_PAD, ft_ref.shape[1]), 0)
-    for f in range(feats):
-        rows = widen(packed_ref[f, 0:FEAT_PAD, :])
-        keep = (row < NORM_AT) | (row == FEAT_PAD - 1)
-        ft_ref[f * FEAT_PAD : (f + 1) * FEAT_PAD, :] = jnp.where(keep, rows, 0.0).astype(BF)
+    row = iota((FEAT_PAD, HID), 0)
+    keep = (row < NORM_AT) | (row == FEAT_PAD - 1)
+    for k, packed_ref in enumerate((own_ref, core_ref, chip_ref, far_ref)):
+        at = rows_of(at_ref[0] ^ k, FEAT_PAD)
+        for b in range(ft_ref.shape[1] // HID):
+            rows = widen(packed_ref[b * FEAT_PAD : (b + 1) * FEAT_PAD, :])
+            ft_ref[at, b * HID : (b + 1) * HID] = jnp.where(keep, rows, 0.0).astype(BF)
     send_ref[...] = dot_nt(sel_ref[...], ft_ref[...]).astype(BF)
 
 
-def place_back(share, f):
-    row, col = iota((HID, HID), 0), iota((HID, HID), 1)
-    return ((row + f * share == col) & (row < share)).astype(F32).astype(BF)
-
-
-def unpack(packed_ref, win_ref, wmid_ref, wout_ref, norm_ref):
-    feats = packed_ref.shape[0]
-    share = HID // feats
+def unpack(packed_refs, at_ref, win_ref, wmid_ref, wout_ref, norm_ref):
+    share = HID // len(packed_refs)
     norms = jnp.zeros((8, HID), F32)
-    pick = place(8, FEAT_PAD, NORM_AT)
-    for f in range(feats):
+    heads = [jnp.zeros((2 * CLASS_HALF, HID), F32) for _ in range(2)]
+    for offset, packed_ref in enumerate(packed_refs):
+        f = at_ref[0] ^ offset
+        at = packed_ref.shape[0] - 2 * share - 2 * FEAT_PAD - CLASS_HALF
         for k in range(2):
-            for r in range(0, share, 16):
-                b = (k * share + r) // 16
-                wmid_ref[k, f * share + r : f * share + r + 16, :] = packed_ref[f, MID_AT : MID_AT + 16, b * HID : (b + 1) * HID]
-                b = r // 16
-                wout_ref[k, f * share + r : f * share + r + 16, :] = packed_ref[
-                    f, OUT_AT : OUT_AT + 16, b * HID + k * LANE : b * HID + (k + 1) * LANE
-                ]
-            for r in range(0, FEAT_PAD, 16):
-                b = (share + k * FEAT_PAD + r) // 16
-                win_ref[k, f * FEAT_PAD + r : f * FEAT_PAD + r + 16, :] = packed_ref[
-                    f, OUT_AT : OUT_AT + 16, b * HID : (b + 1) * HID
-                ]
+            wmid_ref[k, rows_of(f, share), :] = packed_ref[at : at + share, :]
+            at += share
+        for k in range(2):
+            win_ref[k, rows_of(f, FEAT_PAD), :] = packed_ref[at : at + FEAT_PAD, :]
+            at += FEAT_PAD
+        halves = [widen(packed_ref[at : at + CLASS_HALF, h * LANE : (h + 1) * LANE]) for h in range(2)]
+        head = both(jnp.concatenate(halves, 0))
+        lane = iota(head.shape, 1)
+        heads[0] = heads[0] + pltpu.roll(jnp.where(lane < share, head, 0.0), f * share, 1)
+        heads[1] = heads[1] + pltpu.roll(jnp.where((lane >= LANE + share) & (lane < LANE + 2 * share), head, 0.0),
+                                         (f * share + LANE - share) & (HID - 1), 1)
+        part = jnp.zeros((8, HID), F32)
         for p in range(3):
-            part = dot_nn(pick, packed_ref[f, 0:FEAT_PAD, p * HID : (p + 1) * HID]).astype(BF)
-            norms = norms + dot_nn(part, place_back(share, f))
-    norm_ref[...] = norms
+            part = part + widen(packed_ref[p * FEAT_PAD + 16 : (p + 1) * FEAT_PAD, :])[8:16, :]
+        part = jnp.where((iota((8, HID), 0) >= NORM_AT - 24) & (iota((8, HID), 0) < NORM_AT - 20), part, 0.0)
+        norms = norms + pltpu.roll(part, f * share, 1)
+    for k in range(2):
+        wout_ref[k, 0 : 2 * CLASS_HALF, :] = heads[k].astype(BF)
+        wout_ref[k, 2 * CLASS_HALF :, :] = jnp.zeros((LANE - 2 * CLASS_HALF, HID), BF)
+    norm_ref[...] = pltpu.roll(norms, 8 - (NORM_AT - 24), 0)
 
 
 TILE = 1024
-
-
-def both(x):
-    return jnp.concatenate([x, x], 1)
 
 
 def loop(count, tile, body, carry=0):
@@ -221,14 +257,11 @@
     h_ref[s, :] = hidden.astype(BF)
 
 
-def first_kernel(adj_ref, edge_ref, recv_ref, packed_ref, ft_ref, sel_ref,
-                 row_ref, col_ref, wmid_ref, wout_ref, norm_ref,
+def first_kernel(adj_ref, edge_ref, recv_ref, own_ref, core_ref, chip_ref, far_ref, ft_ref, sel_ref, at_ref,
+                 wmid_ref, wout_ref, norm_ref,
                  mean_ref, xhat_ref, slope_ref, istd_ref, h_ref, invd_ref, send_ref, win_ref):
-    nodes, halo = edge_ref.shape
-    unpack(packed_ref, win_ref, wmid_ref, wout_ref, norm_ref)
-
-    row_ref[...] = dot_nn(edge_ref[...], jnp.ones((halo, LANE), BF))
-    col_ref[...] = dot_tn(edge_ref[...], jnp.ones((nodes, LANE), BF))
+    nodes = edge_ref.shape[0]
+    unpack((own_ref, core_ref, chip_ref, far_ref), at_ref, win_ref, wmid_ref, wout_ref, norm_ref)
 
     def gather(s, _):
         summed = dot_nt(adj_ref[s, :], ft_ref[...]) + dot_nn(edge_ref[s, :], recv_ref[...])
@@ -280,7 +313,7 @@
     gather_mean(adj_ref, hin_ref, edge_ref, halo_ref, invd_ref, mean_ref)
 
     def apply(s, _):
-        logits = dot_nn(hin_ref[s, :], w_ref[0]) + dot_nn(mean_ref[s, :], w_ref[1])
+        logits = dot_nt(hin_ref[s, :], w_ref[0]) + dot_nt(mean_ref[s, :], w_ref[1])
         logit_ref[s, :] = logits
         pred_ref[s, :] = logits.astype(BF)
         return 0
@@ -348,7 +381,7 @@
         back = dot_tn(sel_ref[:, s], ret_ref[...])
         grad = ((inv_count * weight) * (shifted * (1.0 / total) - hot) + scale * own + back).astype(BF)
         grad_ref[s, :] = grad
-        gs_ref[s, :] = (dot_nt(grad, w_ref[1]) * both(invd_ref[s, :])).astype(BF)
+        gs_ref[s, :] = (dot_nn(grad, w_ref[1]) * both(invd_ref[s, :])).astype(BF)
         return ce_sum, pen_sum
 
     zero = jnp.zeros((1, 1), F32)
@@ -359,14 +392,14 @@
     send_ref[...] = dot_tn(edge_ref[...], gs_ref[...]).astype(BF)
 
 
-BACK_TILE = 512
-
-
-def layer_back(adj_ref, gs_ref, grad_ref, w_ref, sel_ref, halo_ref, slope_ref, xhat_ref, istd_ref, norm_ref, layer, own_ref, gj_ref):
+BACK_TILE = 1024
+
+
+def layer_back(adj_ref, gs_ref, grad_ref, w_ref, sel_ref, halo_ref, slope_ref, xhat_ref, istd_ref, norm_ref, layer, own_ref, gj_ref, back):
     nodes = adj_ref.shape[0]
 
     def pull(s, _):
-        own_ref[s, :] = (dot_tn(adj_ref[:, s], gs_ref[...]) + dot_nt(grad_ref[s, :], w_ref[0])
+        own_ref[s, :] = (dot_tn(adj_ref[:, s], gs_ref[...]) + back(grad_ref[s, :], w_ref[0])
                          + dot_tn(sel_ref[:, s], halo_ref[...]))
         return 0
 
@@ -392,7 +425,7 @@
                        invd_ref, edge_ref, h_two_ref, mean_head_ref, h_one_ref, mean_two_ref, at_ref,
                        gj_ref, gs_ref, send_ref, sums_ref, own_ref, full_ref, head_ref, *, each):
     gain_sum, bias_sum = layer_back(
-        adj_ref, gsin_ref, grad_ref, wout_ref, sel_ref, recv_ref, slope_ref, xhat_ref, istd_ref, norm_ref, 1, own_ref, gj_ref
+        adj_ref, gsin_ref, grad_ref, wout_ref, sel_ref, recv_ref, slope_ref, xhat_ref, istd_ref, norm_ref, 1, own_ref, gj_ref, dot_nn
     )
     row = iota((8, HID), 0)
     sums_ref[...] = jnp.where(row == 2, gain_sum, 0.0) + jnp.where(row == 3, bias_sum, 0.0)
@@ -404,12 +437,13 @@
     loop(adj_ref.shape[0], TILE, body)
     parts = send_ref.shape[0]
     send_ref[:, 0:each, :] = dot_tn(edge_ref[...], gs_ref[...]).astype(BF).reshape(parts, each, HID)
-    head_ref[:, 0:LANE] = dot_tn(h_two_ref[...], grad_ref[...])
-    head_ref[:, LANE:] = dot_tn(mean_head_ref[...], grad_ref[...])
-    full_ref[0] = dot_tn(h_one_ref[...], gj_ref[...])
-    full_ref[1] = dot_tn(mean_two_ref[...], gj_ref[...])
     share = HID // FEATS
-    start = at_ref[0] * share
+    half = pl.ds(pl.multiple_of(at_ref[0] * share // LANE * LANE, LANE), LANE)
+    start = at_ref[0] * share % LANE
+    head_ref[:, 0:LANE] = dot_tn(h_two_ref[:, half], grad_ref[...])
+    head_ref[:, LANE:] = dot_tn(mean_head_ref[:, half], grad_ref[...])
+    full_ref[0] = dot_tn(h_one_ref[:, half], gj_ref[...])
+    full_ref[1] = dot_tn(mean_two_ref[:, half], gj_ref[...])
     for q in range(parts):
         if q * 16 < 2 * share:
             k, r = divmod(q * 16, share)
@@ -430,7 +464,7 @@
     parts = recv_ref.shape[0]
     halo_ref[...] = recv_ref[:, 0:each, :].reshape(halo_ref.shape)
     gain_sum, bias_sum = layer_back(
-        adj_ref, gsin_ref, grad_ref, w_ref, sel_ref, halo_ref, slope_ref, xhat_ref, istd_ref, norm_ref, 0, own_ref, gj_ref
+        adj_ref, gsin_ref, grad_ref, w_ref, sel_ref, halo_ref, slope_ref, xhat_ref, istd_ref, norm_ref, 0, own_ref, gj_ref, dot_nt
     )
     row = iota((8, HID), 0)
     sums = sums_ref[...] + jnp.where(row == 0, gain_sum, 0.0) + jnp.where(row == 1, bias_sum, 0.0)
@@ -446,41 +480,43 @@
     mid_high, mid_low = bf_parts(mid, 2)
     out_high, out_low = bf_parts(out, 2)
     out = jnp.where(iota((16, HID), 0) < 8, widen(out_high), widen(out_low))
-    high, low = bf_parts(sums, 2)
     lane = iota((8, HID), 1)
-    tail = jnp.zeros((8, HID), F32)
-    for which in range(2):
-        for p, part in enumerate(bf_parts(jnp.broadcast_to(loss_ref[which : which + 1, 0:1], (8, HID)), 3)):
-            tail = tail + jnp.where((lane == p) & (row == which), widen(part), 0.0)
-    message = jnp.concatenate(
-        [full_ref[0, at, :], full_ref[1, at, :], jnp.where(row < 4, widen(high), 0.0) + pltpu.roll(widen(low), 4, 0), tail,
-         widen(mid_high), widen(mid_low), out], 0
-    ).astype(BF)
+    blocks = []
+    for k, norm_part in enumerate(bf_parts(sums, 2)):
+        tail = jnp.zeros((8, HID), F32)
+        for p, part in enumerate(bf_parts(jnp.broadcast_to(loss_ref[k : k + 1, 0:1], (8, HID)), 3)):
+            tail = tail + jnp.where(lane == p, widen(part), 0.0)
+        rows = full_ref[k, at, :]
+        last = jnp.where(row == 0, rows[FEAT_PAD - 8 :, :], jnp.where(row == 3, tail, 0.0))
+        blocks += [rows[0 : FEAT_PAD - 8, :], jnp.where(row >= 4, pltpu.roll(widen(norm_part), 4, 0), last)]
+    message = jnp.concatenate([*blocks, widen(mid_high), widen(mid_low), out], 0).astype(BF)
     for q in range(parts):
         send_ref[q] = message
 
 
-NORM_ROW = 2 * FEAT_PAD
-CHUNK_ROW = NORM_ROW + 16
+CHUNK_ROW = 2 * FEAT_PAD
 MESSAGE_ROWS = CHUNK_ROW + 48
 
 
-def total_kernel(recv_ref, grads_ref, mid_ref, out_ref, square_ref, *, width):
+def total_kernel(recv_ref, grads_ref, norm_ref, loss_ref, mid_ref, out_ref, square_ref, *, width):
     parts = recv_ref.shape[0]
     grads = jnp.zeros((CHUNK_ROW, HID), F32)
     for q in range(parts):
         grads = grads + widen(recv_ref[q, 0:CHUNK_ROW, :])
-    norms = grads[NORM_ROW : NORM_ROW + 8, :]
-    norms = jnp.where(iota((8, HID), 0) < 4, norms + pltpu.roll(norms, 4, 0), 0.0)
     grads_ref[...] = grads
-    grads_ref[NORM_ROW : NORM_ROW + 8, :] = norms
+    tails = [grads[FEAT_PAD - 8 : FEAT_PAD, :], grads[2 * FEAT_PAD - 8 :, :]]
+    row = iota((8, HID), 0)
+    norms = jnp.where(row < 4, pltpu.roll(tails[0] + tails[1], 4, 0), 0.0)
+    norm_ref[...] = norms
+    sums = [jnp.sum(tail[3:4, :], keepdims=True) for tail in tails]
+    loss_ref[...] = jnp.broadcast_to(sums[0] + PEN_WEIGHT * sums[1], loss_ref.shape)
     for q in range(mid_ref.shape[0] // 16):
         at = CHUNK_ROW
         mid_ref[q * 16 : q * 16 + 16, :] = widen(recv_ref[q, at : at + 16, :]) + widen(recv_ref[q, at + 16 : at + 32, :])
         rows = widen(recv_ref[q, at + 32 : at + 48, :])
         out_ref[q * 8 : q * 8 + 8, :] = rows[0:8, :] + rows[8:16, :]
-    weight_row = (iota((NORM_ROW, HID), 0) & (FEAT_PAD - 1)) < width
-    first = jnp.where(weight_row, grads[0:NORM_ROW, :], 0.0)
+    weight_row = (iota((CHUNK_ROW, HID), 0) & (FEAT_PAD - 1)) < width
+    first = jnp.where(weight_row, grads, 0.0)
     square = jnp.sum(first * first, keepdims=True)
     square = square + jnp.sum(mid_ref[...] * mid_ref[...], keepdims=True)
     square = square + jnp.sum(out_ref[...] * out_ref[...], keepdims=True)
@@ -497,13 +533,12 @@
     return fresh, first_new, second_new
 
 
-def update_kernel(grads_ref, gmid_ref, gout_ref, sq0_ref, sq1_ref, sq2_ref, sq3_ref, loss_ref,
+def update_kernel(grads_ref, gnorm_ref, total_ref, gmid_ref, gout_ref, sq0_ref, sq1_ref, sq2_ref, sq3_ref, loss_ref,
                   w_in, w_mid, w_out, norm, m_in, m_mid, m_out, m_norm, v_in, v_mid, v_out, v_norm, at_ref,
                   loss_out, count_out, gnorm_out,
                   nw_in, nw_mid, nw_out, nnorm, nm_in, nm_mid, nm_out, nm_norm, nv_in, nv_mid, nv_out, nv_norm,
                   c_in, c_mid, c_out):
-    tail = jnp.sum(grads_ref[NORM_ROW + 8 : NORM_ROW + 16, :], 1, keepdims=True)
-    loss_out[...] = tail[0:1] + PEN_WEIGHT * tail[1:2]
+    loss_out[...] = total_ref[0:1, 0:1]
     count_out[...] = loss_ref[2:3, 0:1]
     square = (sq0_ref[0:1, 0:1] + sq1_ref[0:1, 0:1]) + (sq2_ref[0:1, 0:1] + sq3_ref[0:1, 0:1])
     grad_norm = jnp.sqrt(square + sq0_ref[1:2, 0:1])
@@ -524,7 +559,7 @@
         step(k, gmid_ref[k * share : (k + 1) * share, :], w_mid, m_mid, v_mid, nw_mid, nm_mid, nv_mid, c_mid)
         turned = jnp.transpose(gout_ref[:, k * LANE : (k + 1) * LANE])[0:classes, :]
         step((every, k, every), turned, w_out, m_out, v_out, nw_out, nm_out, nv_out, c_out)
-    whole = grads_ref[NORM_ROW : NORM_ROW + 8, :]
+    whole = gnorm_ref[...]
     mine = jnp.zeros((8, share), F32)
     for f in range(HID // share):
         mine = mine + jnp.where(at_ref[0] == f, whole[:, f * share : (f + 1) * share], 0.0)
@@ -574,7 +609,7 @@
     classes = w_out.shape[2]
     share = w_mid.shape[1]
     width = features.shape[1]
-    run = functools.partial(call, mib=24 if parts <= 16 else 48)
+    run = functools.partial(call, mib=16 if parts <= 16 else 48)
     labels = labels.reshape(nodes // LANE, LANE)
     mask = train_mask.reshape(nodes // LANE, LANE)
     params = native(w_in, w_mid, w_out, norm_params)
@@ -585,20 +620,35 @@
     def bf(*dims):
         return shape(*dims, dtype=BF)
 
-    sel, packed, at = run(
-        pack_kernel, [bf(halo, nodes), bf(PACK_ROWS, nodes), shape(1, dtype=jnp.int32)],
-        send_index, features.T, *params, feat_at, smem_in=(6,), smem_out=(2,),
-    )
-    packed = lax.all_gather(packed, "feat", axis=0)
-    adj, edge = convert(inner_adj, bound_adj, keep_slots, packed)
-    ft, send = run(spread_kernel, [bf(feats * FEAT_PAD, nodes), bf(halo, LANE)], packed, sel, adj, any_in=(2,))
+    loads = tuple(pltpu.with_memory_space_constraint(a, pltpu.HBM) for a in (features.T, *params))
+    own, at = run(
+        pack_kernel, [bf(pack_rows(nodes, share), HID), shape(1, dtype=jnp.int32)],
+        *loads, feat_at, smem_in=(5,), smem_out=(1,),  hbm_in=range(5),
+        scratch=[pltpu.VMEM(a.shape, a.dtype) for a in loads] + [pltpu.SemaphoreType.DMA((5,))],
+    )
+    chip = lax.ppermute(own, "feat", [(s, s ^ 2) for s in range(feats)])
+    core = lax.ppermute(own, "feat", [(s, s ^ 1) for s in range(feats)])
+    graph = tuple(pltpu.with_memory_space_constraint(a, pltpu.HBM) for a in (inner_adj, bound_adj, keep_slots, send_index))
+    adj, edge, row_deg, col_deg, sel = run(
+        convert_kernel, [bf(nodes, nodes), bf(nodes, halo), shape(nodes, LANE), shape(halo, LANE), bf(halo, nodes)],
+        *graph, hbm_in=range(4), flops=2 * nodes * nodes * HID,
+        scratch=[pltpu.VMEM((CONVERT_SLOTS, CONVERT_TILE, nodes), jnp.int32), pltpu.VMEM((CONVERT_SLOTS, CONVERT_TILE, halo), jnp.int32),
+                 pltpu.VMEM(keep_slots.shape, jnp.int32), pltpu.VMEM(send_index.shape, jnp.int32),
+                 pltpu.SemaphoreType.DMA((2, CONVERT_SLOTS)), pltpu.SemaphoreType.DMA((2,))],
+    )
+    chip, adj = lax.optimization_barrier((chip, adj))
+    far = lax.ppermute(chip, "feat", [(s, s ^ 1) for s in range(feats)])
+    packed = (own, core, chip, far)
+    ft, send = run(
+        spread_kernel, [bf(feats * FEAT_PAD, nodes), bf(halo, LANE)], *packed, sel, adj, at, any_in=(5,), smem_in=(6,)
+    )
     recv = exchange(send, parts).reshape(halo, LANE)
-    (row_deg, col_deg, wmid, wout, norms,
+    (wmid, wout, norms,
      mean_one, xhat_one, slope_one, istd_one, h_one, inv_deg, send) = run(
         first_kernel,
-        [shape(nodes, LANE), shape(halo, LANE), bf(2, HID, HID), bf(2, HID, LANE), shape(8, HID),
+        [bf(2, HID, HID), bf(2, LANE, HID), shape(8, HID),
          bf(nodes, LANE), shape(nodes, HID), shape(nodes, HID), shape(nodes, LANE), bf(nodes, HID), shape(nodes, LANE), bf(halo, HID)],
-        adj, edge, recv, packed, ft, sel,
+        adj, edge, recv, *packed, ft, sel, at, smem_in=(9,),
         scratch=[pltpu.VMEM((2, feats * FEAT_PAD, HID), BF)],
     )
     halo_one = exchange(send, parts).reshape(halo, HID)
@@ -626,7 +676,7 @@
         [bf(nodes, HID), bf(nodes, HID), bf(parts, each + 32, HID), shape(8, HID)],
         adj, grad_sum, grad, wout, recv, sel, slope_two, xhat_two, istd_two, norms, wmid, inv_deg, edge,
         h_two, mean_head, h_one, mean_two, at, smem_in=(17,),
-        scratch=[pltpu.VMEM((nodes, HID), F32), pltpu.VMEM((2, HID, HID), F32), pltpu.VMEM((HID, HID), F32)],
+        scratch=[pltpu.VMEM((nodes, HID), F32), pltpu.VMEM((2, LANE, HID), F32), pltpu.VMEM((LANE, HID), F32)],
     )
     recv = exchange(send, parts)
     send, = run(
@@ -637,15 +687,15 @@
                  pltpu.VMEM((halo, HID), BF)],
     )
     recv = exchange(send, parts)
-    grads, gmid, gout, square = run(
+    *grads, square = run(
         functools.partial(total_kernel, width=width),
-        [shape(CHUNK_ROW, HID), shape(2 * share, HID), shape(share, HID), shape(8, LANE)], recv,
+        [shape(CHUNK_ROW, HID), shape(8, HID), shape(8, LANE), shape(2 * share, HID), shape(share, HID), shape(8, LANE)], recv,
     )
     squares = [square]
     for k in range(1, feats):
         squares.append(lax.ppermute(square, "feat", [(s, s ^ k) for s in range(feats)]))
     outs = [shape(1, 1)] * 3 + [shape(*p.shape) for p in params] * 3 + [bf(*p.shape) for p in params[:3]]
-    result = run(update_kernel, outs, grads, gmid, gout, *squares, losses, *params, *firsts, *seconds, at, smem_in=(20,))
+    result = run(update_kernel, outs, *grads, *squares, losses, *params, *firsts, *seconds, at, smem_in=(22,))
     return (
         tuple(r.reshape(()) for r in result[:3])
         + restore(*result[3:7]) + restore(*result[7:11]) + restore(*result[11:15]) + restore(*result[15:])

time: 165 us -> 130 us (0.79)
  waiting for transfers between devices: 21.4 us -> 2.97 us
  local copies, waits for them, and re-layouts: 14.1 us -> 0.07 us
  between operations: 14.3 us -> 1.05 us
  Pallas kernels: 37.9 us -> 44.8 us
  starting transfers between devices: 1.96 us -> 5.49 us
    all_gather x1 -> x0, waiting for transfers between devices: 19.6 us -> none  [shards(): packed = lax.all_gather(packed, 'feat', axis=0)]
    unnamed x48 -> x28, local copies, waits for them, and re-layouts: 14.1 us -> 0.07 us
    pallas_call x10 -> x11, Pallas kernels: 36.8 us -> 44.8 us  [call(): pl.pallas_call(kernel, out_shape=outs, in_specs=[SMEM if i in smem_in els...]
    ppermute x0 -> x3, starting transfers between devices: none -> 3.57 us  [the longest x1 3 us: shards(): chip = lax.ppermute(own, 'feat', [(s, s ^ 2) for s in range(feats)])]
  transfers between devices with their start and end apart: 4 -> 6, of which waited for: 3 -> 3; matrix products, arithmetic and copies ran while one was open for 0% -> 0% of each run, Pallas kernels for 0% -> 6%
where the time goes in v2:
time: 130 us; the launch traced here: 129 us
  blocking collectives  74.7 us (57%)
  Pallas kernels  44.8 us (34%)
  starting transfers between devices  5.49 us (4%)
  waiting for transfers between devices  2.97 us (2%)
    all_to_all x7, blocking collectives, exchange(): lax.all_to_all(x.reshape(parts, -1, x.shape[-1]), 'dom', split_axis=0, co...  74.7 us
    pallas_call x11, Pallas kernels, call(): pl.pallas_call(kernel, out_shape=outs, in_specs=[SMEM if i in smem_in els...  44.8 us
    ppermute x1, starting transfers between devices, shards(): chip = lax.ppermute(own, 'feat', [(s, s ^ 2) for s in range(feats)])  3 us
  transfers between devices with their start and end apart: 6, of which 3 were waited for; matrix products, arithmetic and copies ran while one was open for 0% of the time, Pallas kernels for 6%

profile of v2, /device:TPU:0, one launch (start us, length us, event | category | flops | bytes accessed | tf_op | source)
XLA Modules:
  0.0 129.1 jit_solution(17710653699295228176)
XLA Ops:
  0.7 1.7 %shard_map.322 = (bf16[480,256]{1,0:T(8,128)(2,1)S(1)}, s32[1]{0:T(128)}) custom-call(f32[25,2048]{1,0:T(8,128)} %bitcast.52, f32[25,2,256]{2,1,0:T(2,128)} %bitcast.36, f32[2,64,256]{2,1,0:T(8,128)} %w_mid.1, f32[47,2,64]{2,1,0:T(2,128)} %bitcast.38, f32[2,2,64]{2,1,0:T(2,128)} %norm.1, s32[1]{0:T(128)} %bitcast.3.at_ref), custom_call_target="tpu_custom_call" | custom-call | bytes 164482 | tf_op jit(solution)/shard_map/pallas_call | solution.py:79
  2.3 3.0 %collective-permute-start = (bf16[480,256]{1,0:T(8,128)(2,1)S(1)}, bf16[480,256]{1,0:T(8,128)(2,1)S(1)}, u32[]{:S(2)}, u32[]{:S(2)}) collective-permute-start(bf16[480,256]{1,0:T(8,128)(2,1)S(1)} %get-tuple-element.83.own_ref), channel_id=1, source_target_pairs={{0,2},{1,3},{2,0},{3,1},{4,6},{5,7},{6,4},{7,5},{8,10},{9,11},{10,... | collective-permute-start | bytes 737288 | tf_op jit(solution)/shard_map/ppermute | solution.py:629
  5.3 0.0 collective-permute-start.1
  5.3 8.4 %shard_map.323 = (bf16[2048,2048]{1,0:T(8,128)(2,1)S(1)}, bf16[2048,256]{1,0:T(8,128)(2,1)S(1)}, f32[2048,128]{1,0:T(8,128)S(1)}, f32[256,128]{1,0:T(8,128)S(1)}, bf16[256,2048]{1,0:T(8,128)(2,1)S(1)}) custom-call(s32[2048,2048]{1,0:T(8,128)} %adj_hbm.1, s32[2048,256]{1,0:T(8,128)} %bound_hbm.1, s32[1,256]{1,0:T(1,128)} %keep_hbm.1, s32[1,8,32]{2,1,0:T(8,128)} %idx_hbm.1), custom_call_target="tpu_custom_call" | custom-call | flops 2147483648 | bytes 7635456 | tf_op jit(solution)/shard_map/pallas_call | solution.py:79
  13.7 0.0 collective-permute-done.chip_ref
  13.7 0.6 collective-permute-start.2
  14.3 0.0 collective-permute-done.1.core_ref
  14.3 1.1 collective-permute-done.2.far_ref
  15.4 1.1 shard_map.324
  16.6 12.6 %all_to_all.35 = bf16[8,32,128]{2,1,0:T(8,128)(2,1)S(1)} all-to-all(bf16[8,32,128]{2,1,0:T(8,128)(2,1)S(1)} %bitcast.44), channel_id=1, replica_groups=mesh['dom'=8,'feat'=4] {'dom'}, dimensions={0} | all-to-all | bytes 131072 | tf_op jit(solution)/shard_map/all_to_all | solution.py:571
  29.1 6.0 %shard_map.325 = (bf16[2,256,256]{2,1,0:T(8,128)(2,1)S(1)}, bf16[2,128,256]{2,1,0:T(8,128)(2,1)S(1)}, f32[8,256]{1,0:T(8,128)S(1)}, bf16[2048,128]{1,0:T(8,128)(...) custom-call(bf16[2048,2048]{1,0:T(8,128)(2,1)S(1)} %get-tuple-elemen, ...), custom_call_target="tpu_custom_call" | custom-call | bytes 5113857 | tf_op jit(solution)/shard_map/pallas_call | solution.py:79
  35.1 9.7 %all_to_all.36 = bf16[8,32,256]{2,1,0:T(8,128)(2,1)S(1)} all-to-all(bf16[8,32,256]{2,1,0:T(8,128)(2,1)S(1)} %bitcast.40), channel_id=1, replica_groups=mesh['dom'=8,'feat'=4] {'dom'}, dimensions={0} | all-to-all | bytes 262144 | tf_op jit(solution)/shard_map/all_to_all | solution.py:571
  44.9 5.0 %shard_map.326 = (bf16[2048,256]{1,0:T(8,128)(2,1)S(1)}, f32[2048,256]{1,0:T(8,128)S(1)}, f32[2048,256]{1,0:T(8,128)S(1)}, f32[2048,128]{1,0:T(8,128)S(1)}, bf16...) custom-call(bf16[2048,2048]{1,0:T(8,128)(2,1)S(1)} %get-tuple-element.85.after_ref.adj_ref, ...), custom_call_target="tpu_custom_call" | custom-call | bytes 5113856 | tf_op jit(solution)/shard_map/pallas_call | solution.py:79
  49.9 9.7 %all_to_all.37 = bf16[8,32,256]{2,1,0:T(8,128)(2,1)S(1)} all-to-all(bf16[8,32,256]{2,1,0:T(8,128)(2,1)S(1)} %bitcast.42), channel_id=1, replica_groups=mesh['dom'=8,'feat'=4] {'dom'}, dimensions={0} | all-to-all | bytes 262144 | tf_op jit(solution)/shard_map/all_to_all | solution.py:571
  59.6 0.0 copy-done.9
  59.6 4.5 %shard_map.327 = (bf16[2048,256]{1,0:T(8,128)(2,1)S(1)}, f32[2048,128]{1,0:T(8,128)S(1)}, bf16[2048,128]{1,0:T(8,128)(2,1)S(1)}, f32[256,128]{1,0:T(8,128)S(1)},...) custom-call(bf16[2048,2048]{1,0:T(8,128)(2,1)S(1)} %get-tuple-element.85.after_ref.adj_ref, ...), custom_call_target="tpu_custom_call" | custom-call | bytes 3999744 | tf_op jit(solution)/shard_map/pallas_call | solution.py:79
  64.1 9.7 %all_to_all.38 = bf16[8,32,256]{2,1,0:T(8,128)(2,1)S(1)} all-to-all(bf16[8,32,256]{2,1,0:T(8,128)(2,1)S(1)} %bitcast.43), channel_id=1, replica_groups=mesh['dom'=8,'feat'=4] {'dom'}, dimensions={0} | all-to-all | bytes 262144 | tf_op jit(solution)/shard_map/all_to_all | solution.py:571
  73.9 0.0 copy-done.10
  73.9 3.1 %shard_map.328 = (bf16[2048,128]{1,0:T(8,128)(2,1)S(1)}, bf16[2048,256]{1,0:T(8,128)(2,1)S(1)}, bf16[256,256]{1,0:T(8,128)(2,1)S(1)}, f32[8,128]{1,0:T(8,128)S(1)}) custom-call(f32[2048,128]{1,0:T(8,128)S(1)} %get-tuple-element.101.logit_ref, s32[16,128]{1,0:T(8,128)S(1)} %bitcast.51, s32[16,128]{1,0:T(8,128)S(1)} %bitcast.50, ...), custom_call_target="tpu_custom_call" | custom-call | bytes 2036736 | tf_op jit(solution)/shard_map/pallas_call | solution.py:79
  77.0 9.7 %all_to_all.39 = bf16[8,32,256]{2,1,0:T(8,128)(2,1)S(1)} all-to-all(bf16[8,32,256]{2,1,0:T(8,128)(2,1)S(1)} %bitcast.41), channel_id=1, replica_groups=mesh['dom'=8,'feat'=4] {'dom'}, dimensions={0} | all-to-all | bytes 262144 | tf_op jit(solution)/shard_map/all_to_all | solution.py:571
  86.7 6.8 %shard_map.329 = (bf16[2048,256]{1,0:T(8,128)(2,1)S(1)}, bf16[2048,256]{1,0:T(8,128)(2,1)S(1)}, bf16[8,64,256]{2,1,0:T(8,128)(2,1)S(1)}, f32[8,256]{1,0:T(8,128)S(1)}) custom-call(bf16[2048,2048]{1,0:T(8,128)(2,1)S(1)} %get-tuple-element.85.after_ref.adj_ref, bf16[2048,256]{1,0:T(8,128)(2,1)S(1)} %get-tuple-element.107.gsin_ref, ...), custom_call_target="tpu_custom_call" | custom-call | bytes 6361089 | tf_op jit(solution)/shard_map/pallas_call | solution.py:79
  93.6 10.6 %all_to_all.40.recv_ref = bf16[8,64,256]{2,1,0:T(8,128)(2,1)S(1)} all-to-all(bf16[8,64,256]{2,1,0:T(8,128)(2,1)S(1)} %get-tuple-element.117), channel_id=1, replica_groups=mesh['dom'=8,'feat'=4] {'dom'}, dimensions={0} | all-to-all | bytes 524288 | tf_op jit(solution)/shard_map/all_to_all | solution.py:571
  104.2 0.0 copy-start.4
  104.2 0.0 copy-start.5
  104.2 0.0 copy-start.6
  104.3 0.0 copy-start.7
  104.3 0.0 copy-start.8
  104.3 0.0 copy-start.11
  104.3 0.0 copy-start.12
  104.3 0.0 copy-start.13
  104.3 5.8 %shard_map.330 = bf16[8,112,256]{2,1,0:T(8,128)(2,1)S(1)} custom-call(bf16[2048,2048]{1,0:T(8,128)(2,1)S(1)} %get-tuple-element.85.after_ref.adj_ref, bf16[2048,256]{1,0:T(8,128)(2,1)S(1)} %get-tuple-element.115.gsin_ref, bf16[2048,256]{1,0:T(8,128)(2,1)S(1)} %get-tuple-element.116.grad_ref, bf16[2,256,256]{2,1,0:T(8,128)(2,1)S(1)} %get-tuple-element.94.w_ref, ...), custom_call_target="tpu_custom_call" | custom-call | bytes 4707329 | tf_op jit(solution)/shard_map/pallas_call | solution.py:79
  110.2 12.6 %all_to_all.41.recv_ref = bf16[8,112,256]{2,1,0:T(8,128)(2,1)S(1)} all-to-all(bf16[8,112,256]{2,1,0:T(8,128)(2,1)S(1)} %shard_map.330), channel_id=1, replica_groups=mesh['dom'=8,'feat'=4] {'dom'}, dimensions={0} | all-to-all | bytes 917504 | tf_op jit(solution)/shard_map/all_to_all | solution.py:571
  122.7 0.2 shard_map.331
  123.0 0.1 collective-permute-start.5
  123.0 0.6 collective-permute-start.4
  123.7 1.2 collective-permute-start.3
  124.9 1.2 collective-permute-done.5.sq3_ref
  126.1 0.7 collective-permute-done.4.sq2_ref
  126.7 0.0 collective-permute-done.3.sq1_ref
  126.7 0.0 copy-done
  126.7 0.0 copy-done.1
  126.7 0.0 copy-done.2
  126.7 0.0 copy-done.3
  126.7 0.0 copy-done.4
  126.7 0.0 copy-done.5
  126.8 0.0 copy-done.6
  126.8 0.0 copy-done.7
  126.8 2.1 %shard_map.332 = (f32[1,1]{1,0:T(1,128)}, f32[1,1]{1,0:T(1,128)}, f32[1,1]{1,0:T(1,128)}, f32[25,2,256]{2,1,0:T(2,128)}, f32[2,64,256]{2,1,0:T(8,128)}, /*index=...) custom-call(f32[64,256]{1,0:T(8,128)S(1)} %get-tuple-element.124.gra, ...), custom_call_target="tpu_custom_call" | custom-call | bytes 410564 | tf_op jit(solution)/shard_map/pallas_call | solution.py:79
  (10 shorter events, 0.0 us)
Async XLA Ops:
  2.3 11.4 %collective-permute-start = (bf16[480,256]{1,0:T(8,128)(2,1)S(1)}, bf16[480,256]{1,0:T(8,128)(2,1)S(1)}, u32[]{:S(2)}, u32[]{:S(2)}) collective-permute-start(bf16[480,256]{1,0:T(8,128)(2,1)S(1)} %get-tuple-element.83.own_ref), channel_id=1, source_target_pairs={{0,2},{1,3},{2,0},{3,1},{4,6},{5,7},{6,4},{7,5},{8,10},{9,11},{10,... | collective-permute-start | bytes 737288 | tf_op jit(solution)/shard_map/ppermute | solution.py:629
  5.3 9.0 %collective-permute-start.1 = (bf16[480,256]{1,0:T(8,128)(2,1)S(1)}, bf16[480,256]{1,0:T(8,128)(2,1)S(1)}, u32[]{:S(2)}, u32[]{:S(2)}) collective-permute-start(bf16[480,256]{1,0:T(8,128)(2,1)S(1)} %get-tuple-element.83.own_ref), channel_id=1, source_target_pairs={{0,1},{1,0},{2,3},{3,2},{4,5},{5,4},{6,7},{7,6},{8,9},{9,8},{10,11... | collective-permute-start | bytes 737288 | tf_op jit(solution)/shard_map/ppermute | solution.py:630
  13.7 1.7 %collective-permute-start.2 = (bf16[480,256]{1,0:T(8,128)(2,1)S(1)}, bf16[480,256]{1,0:T(8,128)(2,1)S(1)}, u32[]{:S(2)}, u32[]{:S(2)}) collective-permute-start(bf16[480,256]{1,0:T(8,128)(2,1)S(1)} %collective-permute-done.chip_ref), channel_id=1, source_target_pairs={{0,1},{1,0},{2,3},{3,2},{4,5},{5,4},{6,7},{7,6},{8,9},{9,8},{10,11... | collective-permute-start | bytes 737288 | tf_op jit(solution)/shard_map/ppermute | solution.py:640
  44.9 14.8 %copy-start.9 = (s32[2048]{0:T(1024)S(1)}, s32[2048]{0:T(1024)}, u32[]{:S(2)}) copy-start(s32[2048]{0:T(1024)} %param.25) | copy-start | bytes 24580
  59.6 14.2 %copy-start.10 = (s32[2048]{0:T(1024)S(1)}, s32[2048]{0:T(1024)}, u32[]{:S(2)}) copy-start(s32[2048]{0:T(1024)} %param.24) | copy-start | bytes 24580
  104.2 22.5 %copy-start = (f32[2,64,256]{2,1,0:T(8,128)S(1)}, f32[2,64,256]{2,1,0:T(8,128)}, u32[]{:S(2)}) copy-start(f32[2,64,256]{2,1,0:T(8,128)} %w_mid.1) | copy-start | bytes 393220
  104.2 22.5 %copy-start.1 = (f32[2,25,256]{2,0,1:T(2,128)S(1)}, f32[2,25,256]{2,0,1:T(2,128)}, u32[]{:S(2)}) copy-start(f32[2,25,256]{2,0,1:T(2,128)} %param.26) | copy-start | bytes 153604
  104.2 22.5 %copy-start.2 = (f32[2,64,47]{1,0,2:T(2,128)S(1)}, f32[2,64,47]{1,0,2:T(2,128)}, u32[]{:S(2)}) copy-start(f32[2,64,47]{1,0,2:T(2,128)} %param.28) | copy-start | bytes 72196
  104.2 22.5 %copy-start.3 = (f32[2,64,256]{2,1,0:T(8,128)S(1)}, f32[2,64,256]{2,1,0:T(8,128)}, u32[]{:S(2)}) copy-start(f32[2,64,256]{2,1,0:T(8,128)} %m_mid.1) | copy-start | bytes 393220
  104.2 22.5 %copy-start.4 = (f32[2,64,256]{2,1,0:T(8,128)S(1)}, f32[2,64,256]{2,1,0:T(8,128)}, u32[]{:S(2)}) copy-start(f32[2,64,256]{2,1,0:T(8,128)} %v_mid.1) | copy-start | bytes 393220
  104.2 22.5 %copy-start.5 = (f32[2,25,256]{2,0,1:T(2,128)S(1)}, f32[2,25,256]{2,0,1:T(2,128)}, u32[]{:S(2)}) copy-start(f32[2,25,256]{2,0,1:T(2,128)} %param.30) | copy-start | bytes 153604
  104.2 22.5 %copy-start.6 = (f32[2,25,256]{2,0,1:T(2,128)S(1)}, f32[2,25,256]{2,0,1:T(2,128)}, u32[]{:S(2)}) copy-start(f32[2,25,256]{2,0,1:T(2,128)} %param.34) | copy-start | bytes 153604
  104.3 22.5 %copy-start.7 = (f32[2,64,47]{1,0,2:T(2,128)S(1)}, f32[2,64,47]{1,0,2:T(2,128)}, u32[]{:S(2)}) copy-start(f32[2,64,47]{1,0,2:T(2,128)} %param.32) | copy-start | bytes 72196
  104.3 22.5 %copy-start.8 = (f32[2,64,47]{1,0,2:T(2,128)S(1)}, f32[2,64,47]{1,0,2:T(2,128)}, u32[]{:S(2)}) copy-start(f32[2,64,47]{1,0,2:T(2,128)} %param.36) | copy-start | bytes 72196
  104.3 22.5 %copy-start.11 = (f32[2,2,64]{2,1,0:T(2,128)S(1)}, f32[2,2,64]{2,1,0:T(2,128)}, u32[]{:S(2)}) copy-start(f32[2,2,64]{2,1,0:T(2,128)} %norm.1) | copy-start | bytes 3076
  104.3 22.5 %copy-start.12 = (f32[2,2,64]{2,1,0:T(2,128)S(1)}, f32[2,2,64]{2,1,0:T(2,128)}, u32[]{:S(2)}) copy-start(f32[2,2,64]{2,1,0:T(2,128)} %m_norm.1) | copy-start | bytes 3076
  104.3 22.5 %copy-start.13 = (f32[2,2,64]{2,1,0:T(2,128)S(1)}, f32[2,2,64]{2,1,0:T(2,128)}, u32[]{:S(2)}) copy-start(f32[2,2,64]{2,1,0:T(2,128)} %v_norm.1) | copy-start | bytes 3076
  123.0 3.1 %collective-permute-start.5 = (f32[8,128]{1,0:T(8,128)S(1)}, f32[8,128]{1,0:T(8,128)S(1)}, u32[]{:S(2)}, u32[]{:S(2)}) collective-permute-start(f32[8,128]{1,0:T(8,128)S(1)} %get-tuple-element.129.sq0_ref), channel_id=1, source_target_pairs={{0,3},{1,2},{2,1},{3,0},{4,7},{5,6},{6,5},{7,4},{8,11},{9,10},{10,... | collective-permute-start | bytes 12296 | tf_op jit(solution)/shard_map/ppermute | solution.py:696
  123.0 3.7 %collective-permute-start.4 = (f32[8,128]{1,0:T(8,128)S(1)}, f32[8,128]{1,0:T(8,128)S(1)}, u32[]{:S(2)}, u32[]{:S(2)}) collective-permute-start(f32[8,128]{1,0:T(8,128)S(1)} %get-tuple-element.129.sq0_ref), channel_id=1, source_target_pairs={{0,2},{1,3},{2,0},{3,1},{4,6},{5,7},{6,4},{7,5},{8,10},{9,11},{10,... | collective-permute-start | bytes 12296 | tf_op jit(solution)/shard_map/ppermute | solution.py:696
  123.7 3.0 %collective-permute-start.3 = (f32[8,128]{1,0:T(8,128)S(1)}, f32[8,128]{1,0:T(8,128)S(1)}, u32[]{:S(2)}, u32[]{:S(2)}) collective-permute-start(f32[8,128]{1,0:T(8,128)S(1)} %get-tuple-element.129.sq0_ref), channel_id=1, source_target_pairs={{0,1},{1,0},{2,3},{3,2},{4,5},{5,4},{6,7},{7,6},{8,9},{9,8},{10,11... | collective-permute-start | bytes 12296 | tf_op jit(solution)/shard_map/ppermute | solution.py:696

commit v3 on v2

--- a/solution.py
+++ b/solution.py
@@ -1,4 +1,5 @@
 import functools
+import math
 
 import jax
 import jax.numpy as jnp
@@ -74,13 +75,13 @@
     return pl.ds(pl.multiple_of(i * tile, tile), tile)
 
 
-def call(kernel, outs, *args, mib=24, flops=0, smem_in=(), any_in=(), hbm_in=(), smem_out=(), scratch=()):
-    size = sum(a.size * a.dtype.itemsize for a in (*args, *outs))
+def call(kernel, outs, *args, mib=24, flops=0, smem_in=(), any_in=(), hbm_in=(), smem_out=(), hbm_out=(), scratch=()):
+    size = sum(math.prod(a.shape) * a.dtype.itemsize for a in (*args, *outs))
     return pl.pallas_call(
         kernel,
         out_shape=outs,
         in_specs=[SMEM if i in smem_in else ANY if i in any_in else HBM if i in hbm_in else VMEM for i in range(len(args))],
-        out_specs=[SMEM if i in smem_out else VMEM for i in range(len(outs))],
+        out_specs=[SMEM if i in smem_out else HBM if i in hbm_out else VMEM for i in range(len(outs))],
         scratch_shapes=list(scratch),
         cost_estimate=pl.CostEstimate(flops=flops, bytes_accessed=size // 4, transcendentals=0),
         compiler_params=pltpu.CompilerParams(vmem_limit_bytes=mib * MIB),
@@ -91,20 +92,37 @@
     return jax.ShapeDtypeStruct(dims, dtype)
 
 
-def pack_kernel(feat_hbm, w_in_hbm, w_mid_hbm, w_out_hbm, norm_hbm, at_ref, pack_ref, at_out,
-                feat_ref, w_in_ref, w_mid_ref, w_out_ref, norm_ref, sems):
-    sources = (feat_hbm, w_mid_hbm, w_in_hbm, w_out_hbm, norm_hbm)
-    targets = (feat_ref, w_mid_ref, w_in_ref, w_out_ref, norm_ref)
+def select(idx_ref, sel_ref):
+    nodes = sel_ref.shape[1]
+    parts, each = idx_ref.shape[1:]
+    eye = iota((each, each), 0) == iota((each, each), 1)
+    for p in range(parts):
+        column = jnp.sum(jnp.where(eye, idx_ref[0, p : p + 1, :].astype(F32), 0.0), 1, keepdims=True)
+        hot = iota((each, nodes), 1) == column.astype(jnp.int32)
+        sel_ref[p * each : (p + 1) * each, :] = hot.astype(F32).astype(BF)
+
+
+def pack_kernel(idx_hbm, feat_hbm, w_in_hbm, w_mid_hbm, w_out_hbm, norm_hbm, at_ref, send_ref, pack_ref, at_out,
+                sel_ref, idx_ref, feat_ref, w_in_ref, w_mid_ref, w_out_ref, norm_ref, sems):
+    sources = (idx_hbm, feat_hbm, w_mid_hbm, w_in_hbm, w_out_hbm, norm_hbm)
+    targets = (idx_ref, feat_ref, w_mid_ref, w_in_ref, w_out_ref, norm_ref)
     copies = [pltpu.make_async_copy(src, dst, sems.at[i]) for i, (src, dst) in enumerate(zip(sources, targets))]
     for copy in copies:
         copy.start()
     at_out[0] = at_ref[0]
-    for copy in copies:
-        copy.wait()
+    copies[0].wait()
+    select(idx_ref, sel_ref)
+    wait_all(copies[1:])
     nodes = feat_ref.shape[1]
     width, share = feat_ref.shape[0], w_mid_ref.shape[1]
     classes = w_out_ref.shape[0]
     rows = dot_nn(place(FEAT_PAD, width, 0), feat_ref[...].astype(BF))
+    parts, copies, half, _ = send_ref.shape
+    sent = dot_nt(sel_ref[...], rows.astype(BF)).astype(BF)
+    left = dot_nn(sent, place(FEAT_PAD, LANE, 0)).reshape(parts, 2, half, LANE)[:, 0]
+    right = dot_nn(sent, place(FEAT_PAD, LANE, LANE // 2)).reshape(parts, 2, half, LANE)[:, 1]
+    for f in range(copies):
+        send_ref[:, f] = (left + right).astype(BF)
     ones = iota((FEAT_PAD, nodes), 0) == FEAT_PAD - 1
     blocks = [jnp.zeros((FEAT_PAD, HID), F32) for _ in range(3)]
     for layer in range(2):
@@ -140,66 +158,29 @@
     return nodes // HID * FEAT_PAD + 2 * share + 2 * FEAT_PAD + CLASS_HALF
 
 
-def convert_kernel(adj_hbm, bound_hbm, keep_hbm, idx_hbm, adj_ref, edge_ref, row_ref, col_ref, sel_ref,
-                   adj_buf, bound_buf, keep_ref, idx_ref, sems, small_sems):
-    slots, nodes = sel_ref.shape
-    parts, each = idx_ref.shape[1:]
-    steps = nodes // CONVERT_TILE
-
-    def fetch(step, slot):
-        s = rows_of(step, CONVERT_TILE)
-        return (pltpu.make_async_copy(adj_hbm.at[s], adj_buf.at[slot], sems.at[0, slot]),
-                pltpu.make_async_copy(bound_hbm.at[s], bound_buf.at[slot], sems.at[1, slot]))
-
-    small = (pltpu.make_async_copy(idx_hbm, idx_ref, small_sems.at[0]), pltpu.make_async_copy(keep_hbm, keep_ref, small_sems.at[1]))
-    for copy in small:
-        copy.start()
-    for step in range(CONVERT_SLOTS):
-        for copy in fetch(step, step):
-            copy.start()
-    for copy in small:
-        copy.wait()
-    eye = iota((each, each), 0) == iota((each, each), 1)
-    for p in range(parts):
-        column = jnp.sum(jnp.where(eye, idx_ref[0, p : p + 1, :].astype(F32), 0.0), 1, keepdims=True)
-        hot = iota((each, nodes), 1) == column.astype(jnp.int32)
-        sel_ref[p * each : (p + 1) * each, :] = hot.astype(F32).astype(BF)
-
-    def body(step, _):
-        slot = lax.rem(step, CONVERT_SLOTS)
-        s = rows_of(step, CONVERT_TILE)
-        for copy in fetch(step, slot):
-            copy.wait()
-        adj_ref[s, :] = adj_buf[slot].astype(F32).astype(BF)
-        edge = (bound_buf[slot] * keep_ref[...]).astype(F32).astype(BF)
-        edge_ref[s, :] = edge
-        row_ref[s, :] = dot_nn(edge, jnp.ones((slots, LANE), BF))
-        col_ref[...] += dot_tn(edge, jnp.ones((CONVERT_TILE, LANE), BF))
-
-        @pl.when(step + CONVERT_SLOTS < steps)
-        def _():
-            for copy in fetch(step + CONVERT_SLOTS, slot):
-                copy.start()
-
-        return 0
-
-    col_ref[...] = jnp.zeros(col_ref.shape, F32)
-    lax.fori_loop(0, steps, body, 0)
-
-
-CONVERT_SLOTS = 4
-
-
-def spread_kernel(own_ref, core_ref, chip_ref, far_ref, sel_ref, after_ref, at_ref, ft_ref, send_ref):
-    del after_ref
+def spread(packed_refs, at_ref, ft_ref):
     row = iota((FEAT_PAD, HID), 0)
     keep = (row < NORM_AT) | (row == FEAT_PAD - 1)
-    for k, packed_ref in enumerate((own_ref, core_ref, chip_ref, far_ref)):
+    for k, packed_ref in enumerate(packed_refs):
         at = rows_of(at_ref[0] ^ k, FEAT_PAD)
         for b in range(ft_ref.shape[1] // HID):
             rows = widen(packed_ref[b * FEAT_PAD : (b + 1) * FEAT_PAD, :])
             ft_ref[at, b * HID : (b + 1) * HID] = jnp.where(keep, rows, 0.0).astype(BF)
-    send_ref[...] = dot_nt(sel_ref[...], ft_ref[...]).astype(BF)
+
+
+def join_halo(recv_ref, halo_ref, width):
+    parts, feats, half, _ = recv_ref.shape
+    lane = iota((parts * half, LANE), 1)
+    sides = [jnp.where(lane == LANE - 1, 1.0, 0.0)] * 2
+    for f in range(feats):
+        rows = widen(recv_ref[:, f]).reshape(parts * half, LANE)
+        for g in range(2):
+            at = g * (LANE // 2)
+            side = jnp.where((lane >= at) & (lane < at + width), rows, 0.0)
+            shift = (f * FEAT_PAD - at) % LANE
+            sides[g] = sides[g] + (pltpu.roll(side, shift, 1) if shift else side)
+    sides = [side.astype(BF).reshape(parts, half, LANE) for side in sides]
+    halo_ref[...] = jnp.stack(sides, 1).reshape(halo_ref.shape)
 
 
 def unpack(packed_refs, at_ref, win_ref, wmid_ref, wout_ref, norm_ref):
@@ -257,20 +238,95 @@
     h_ref[s, :] = hidden.astype(BF)
 
 
-def first_kernel(adj_ref, edge_ref, recv_ref, own_ref, core_ref, chip_ref, far_ref, ft_ref, sel_ref, at_ref,
-                 wmid_ref, wout_ref, norm_ref,
-                 mean_ref, xhat_ref, slope_ref, istd_ref, h_ref, invd_ref, send_ref, win_ref):
+GATHER_PARTS = 2
+
+
+def start_all(copies):
+    for copy in copies:
+        copy.start()
+    return copies
+
+
+def wait_all(copies):
+    for copy in copies:
+        copy.wait()
+
+
+def side_kernel(own_hbm, chip_hbm, core_ref, far_ref, at_ref,
+                ft_out, win_out, wmid_out, wout_out, norm_out,
+                ft_ref, win_ref, wmid_ref, wout_ref, norm_ref, own_ref, chip_ref, in_sems, out_sems):
+    packed_refs = (own_ref, core_ref, chip_ref, far_ref)
+    loads = ((own_hbm, own_ref), (chip_hbm, chip_ref))
+    wait_all(start_all([pltpu.make_async_copy(src, dst, in_sems.at[i]) for i, (src, dst) in enumerate(loads)]))
+    pairs = ((ft_ref, ft_out), (win_ref, win_out), (wmid_ref, wmid_out), (wout_ref, wout_out), (norm_ref, norm_out))
+    stores = [pltpu.make_async_copy(src, dst, out_sems.at[i]) for i, (src, dst) in enumerate(pairs)]
+    spread(packed_refs, at_ref, ft_ref)
+    stores[0].start()
+    unpack(packed_refs, at_ref, win_ref, wmid_ref, wout_ref, norm_ref)
+    start_all(stores[1:])
+    wait_all(stores)
+
+
+def first_kernel(adj_hbm, bound_hbm, keep_hbm, idx_hbm, ft_hbm, win_hbm, norm_hbm, recv_ref,
+                 adj_ref, edge_ref, row_ref, sel_ref, mean_ref, xhat_ref, slope_ref, istd_ref, h_ref, invd_ref, send_ref,
+                 halo_ref, keep_ref, idx_ref, ft_ref, win_ref, norm_ref, adj_buf, bound_buf, ring_sems, sems, *, width):
     nodes = edge_ref.shape[0]
-    unpack((own_ref, core_ref, chip_ref, far_ref), at_ref, win_ref, wmid_ref, wout_ref, norm_ref)
-
-    def gather(s, _):
-        summed = dot_nt(adj_ref[s, :], ft_ref[...]) + dot_nn(edge_ref[s, :], recv_ref[...])
+    ring, tile = adj_buf.shape[0:2]
+
+    def fetch(step, slot):
+        return pltpu.make_async_copy(adj_hbm.at[rows_of(step, tile)], adj_buf.at[slot], ring_sems.at[0, slot])
+
+    def fetch_bound(step, slot):
+        return pltpu.make_async_copy(bound_hbm.at[rows_of(step, tile)], bound_buf.at[slot], ring_sems.at[1, slot])
+
+    sources, targets = (keep_hbm, idx_hbm, ft_hbm, win_hbm, norm_hbm), (keep_ref, idx_ref, ft_ref, win_ref, norm_ref)
+    small = [pltpu.make_async_copy(src, dst, sems.at[i]) for i, (src, dst) in enumerate(zip(sources, targets))]
+    start_all(small[0:2])
+    for step in range(bound_buf.shape[0]):
+        fetch_bound(step, step).start()
+    start_all(small[2:])
+    for step in range(ring):
+        fetch(step, step).start()
+    join_halo(recv_ref, halo_ref, width)
+    wait_all(small[0:2])
+    select(idx_ref, sel_ref)
+
+    def boundary(step, _):
+        slot = lax.rem(step, bound_buf.shape[0])
+        s = rows_of(step, tile)
+        fetch_bound(step, slot).wait()
+        edge_ref[s, :] = (bound_buf[slot] * keep_ref[...]).astype(F32).astype(BF)
+
+        @pl.when(step + bound_buf.shape[0] < nodes // tile)
+        def _():
+            fetch_bound(step + bound_buf.shape[0], slot).start()
+
+        return 0
+
+    lax.fori_loop(0, nodes // tile, boundary, 0)
+    wait_all(small[2:])
+
+    def gather(step, _):
+        for part in range(GATHER_PARTS):
+            chunk = step * GATHER_PARTS + part
+            slot = lax.rem(chunk, ring)
+            fetch(chunk, slot).wait()
+            adj_ref[rows_of(chunk, tile), :] = adj_buf[slot].astype(F32).astype(BF)
+
+            @pl.when(chunk + ring < nodes // tile)
+            def _():
+                fetch(chunk + ring, slot).start()
+
+        s = rows_of(step, GATHER_PARTS * tile)
+        far = dot_nn(edge_ref[s, :], halo_ref[...])
+        row_ref[s, :] = jnp.broadcast_to(far[:, LANE - 1 : LANE], far.shape)
+        summed = dot_nt(adj_ref[s, :], ft_ref[...]) + far
         inv_deg = 1.0 / jnp.maximum(summed[:, LANE - 1 : LANE], 1.0)
         invd_ref[s, :] = jnp.broadcast_to(inv_deg, summed.shape)
         mean_ref[s, :] = (summed * inv_deg).astype(BF)
         return 0
 
-    loop(nodes, TILE, gather)
+    lax.fori_loop(0, nodes // (GATHER_PARTS * tile), gather, 0)
 
     def apply(s, _):
         joined = dot_tn(ft_ref[:, s], win_ref[0]) + dot_nn(mean_ref[s, :], win_ref[1])
@@ -308,26 +364,27 @@
     return high, x - 256.0 * high
 
 
-def head_kernel(adj_ref, edge_ref, halo_ref, hin_ref, w_ref, invd_ref, sel_ref, mask_ref, col_ref,
+def head_kernel(adj_ref, edge_ref, halo_ref, hin_ref, w_ref, invd_ref, sel_ref, mask_ref,
                 mean_ref, logit_ref, pred_ref, cross_ref, mine_ref, send_ref):
     gather_mean(adj_ref, hin_ref, edge_ref, halo_ref, invd_ref, mean_ref)
 
     def apply(s, _):
         logits = dot_nt(hin_ref[s, :], w_ref[0]) + dot_nt(mean_ref[s, :], w_ref[1])
         logit_ref[s, :] = logits
-        pred_ref[s, :] = logits.astype(BF)
+        pred_ref[s, :] = jnp.where(iota(logits.shape, 1) == LANE - 1, 1.0, logits).astype(BF)
         return 0
 
     loop(adj_ref.shape[0], TILE, apply)
     mine = dot_nn(sel_ref[...], pred_ref[...])
+    lane = iota(mine.shape, 1)
+    mine = jnp.where(lane < 64, mine, 0.0)
     mine_ref[...] = mine
     cross = dot_tn(edge_ref[...], pred_ref[...])
     cross_ref[...] = cross
-    high, low = bf_parts(cross, 2)
+    high, low = bf_parts(jnp.where(lane < 64, cross, 0.0), 2)
     count = jnp.sum(mask_ref[...].astype(F32), keepdims=True)
-    lane = iota(mine.shape, 1)
     count_high, count_low = split_count(count)
-    col_high, col_low = split_count(col_ref[...])
+    col_high, col_low = split_count(cross[:, LANE - 1 : LANE])
     extra = jnp.where(lane == 64, count_high, 0.0) + jnp.where(lane == 65, count_low, 0.0)
     extra = extra + jnp.where(lane == 66, col_high, 0.0) + jnp.where(lane == 67, col_low, 0.0)
     send_ref[:, 0:LANE] = (mine + pltpu.roll(widen(low), 64, 1)).astype(BF)
@@ -339,7 +396,7 @@
     return dot_tn(values.astype(F32).astype(BF), pick)
 
 
-def logit_grad_kernel(logit_ref, label_ref, mask_ref, row_ref, pred_ref, edge_ref, recv_ref, mine_ref, cross_ref, col_ref,
+def logit_grad_kernel(logit_ref, label_ref, mask_ref, row_ref, pred_ref, edge_ref, recv_ref, mine_ref, cross_ref,
                       sel_ref, w_ref, invd_ref,
                       grad_ref, gs_ref, send_ref, loss_ref, hp_ref, ret_ref, lab_ref, wgt_ref, *, classes, each):
     slots = mine_ref.shape[0]
@@ -356,7 +413,7 @@
     inv_count = 1.0 / count
     hp_ref[...] = halo_pred.astype(BF)
     ret_ref[...] = (scale * (col_back * mine_ref[...] - back_cross)).astype(BF)
-    pen = jnp.sum(col_ref[...] * (halo_pred * halo_pred), keepdims=True)
+    pen = jnp.sum(cross_ref[:, LANE - 1 : LANE] * (halo_pred * halo_pred), keepdims=True)
     pen = pen - 2.0 * jnp.sum(halo_pred * cross_ref[...], keepdims=True)
     for r in range(nodes // LANE):
         lab_ref[r * LANE : (r + 1) * LANE, :] = spread_row(label_ref[...], r)
@@ -374,7 +431,7 @@
         target = jnp.sum(logits * hot, 1, keepdims=True)
         weight = wgt_ref[s, :]
         ce_sum = ce_sum + jnp.sum(weight[:, 0:1] * (top + jnp.log(total) - target), keepdims=True)
-        pred = widen(pred_ref[s, :])
+        pred = jnp.where(real, widen(pred_ref[s, :]), 0.0)
         drawn = row_ref[s, :] * pred
         pen_sum = pen_sum + jnp.sum(drawn * pred, keepdims=True)
         own = drawn - dot_nn(edge_ref[s, :], hp_ref[...])
@@ -609,7 +666,7 @@
     classes = w_out.shape[2]
     share = w_mid.shape[1]
     width = features.shape[1]
-    run = functools.partial(call, mib=16 if parts <= 16 else 48)
+    run = functools.partial(call, mib=16 if parts <= 16 else 52)
     labels = labels.reshape(nodes // LANE, LANE)
     mask = train_mask.reshape(nodes // LANE, LANE)
     params = native(w_in, w_mid, w_out, norm_params)
@@ -620,36 +677,39 @@
     def bf(*dims):
         return shape(*dims, dtype=BF)
 
-    loads = tuple(pltpu.with_memory_space_constraint(a, pltpu.HBM) for a in (features.T, *params))
-    own, at = run(
-        pack_kernel, [bf(pack_rows(nodes, share), HID), shape(1, dtype=jnp.int32)],
-        *loads, feat_at, smem_in=(5,), smem_out=(1,),  hbm_in=range(5),
-        scratch=[pltpu.VMEM(a.shape, a.dtype) for a in loads] + [pltpu.SemaphoreType.DMA((5,))],
-    )
+    def in_hbm(*arrays):
+        return tuple(pltpu.with_memory_space_constraint(a, pltpu.HBM) for a in arrays)
+
+    loads = in_hbm(send_index, features.T, *params)
+    send, own, at = run(
+        pack_kernel, [bf(parts, feats, each // 2, LANE), bf(pack_rows(nodes, share), HID), shape(1, dtype=jnp.int32)],
+        *loads, feat_at, smem_in=(6,), smem_out=(2,), hbm_in=range(6),
+        scratch=[pltpu.VMEM((halo, nodes), BF)] + [pltpu.VMEM(a.shape, a.dtype) for a in loads] + [pltpu.SemaphoreType.DMA((6,))],
+    )
+    recv = lax.all_to_all(
+        send.reshape(parts * feats, each // 2, LANE), ("dom", "feat"), split_axis=0, concat_axis=0, tiled=True
+    ).reshape(parts, feats, each // 2, LANE)
     chip = lax.ppermute(own, "feat", [(s, s ^ 2) for s in range(feats)])
     core = lax.ppermute(own, "feat", [(s, s ^ 1) for s in range(feats)])
-    graph = tuple(pltpu.with_memory_space_constraint(a, pltpu.HBM) for a in (inner_adj, bound_adj, keep_slots, send_index))
-    adj, edge, row_deg, col_deg, sel = run(
-        convert_kernel, [bf(nodes, nodes), bf(nodes, halo), shape(nodes, LANE), shape(halo, LANE), bf(halo, nodes)],
-        *graph, hbm_in=range(4), flops=2 * nodes * nodes * HID,
-        scratch=[pltpu.VMEM((CONVERT_SLOTS, CONVERT_TILE, nodes), jnp.int32), pltpu.VMEM((CONVERT_SLOTS, CONVERT_TILE, halo), jnp.int32),
-                 pltpu.VMEM(keep_slots.shape, jnp.int32), pltpu.VMEM(send_index.shape, jnp.int32),
-                 pltpu.SemaphoreType.DMA((2, CONVERT_SLOTS)), pltpu.SemaphoreType.DMA((2,))],
-    )
-    chip, adj = lax.optimization_barrier((chip, adj))
     far = lax.ppermute(chip, "feat", [(s, s ^ 1) for s in range(feats)])
-    packed = (own, core, chip, far)
-    ft, send = run(
-        spread_kernel, [bf(feats * FEAT_PAD, nodes), bf(halo, LANE)], *packed, sel, adj, at, any_in=(5,), smem_in=(6,)
-    )
-    recv = exchange(send, parts).reshape(halo, LANE)
-    (wmid, wout, norms,
-     mean_one, xhat_one, slope_one, istd_one, h_one, inv_deg, send) = run(
-        first_kernel,
-        [bf(2, HID, HID), bf(2, LANE, HID), shape(8, HID),
-         bf(nodes, LANE), shape(nodes, HID), shape(nodes, HID), shape(nodes, LANE), bf(nodes, HID), shape(nodes, LANE), bf(halo, HID)],
-        adj, edge, recv, *packed, ft, sel, at, smem_in=(9,),
-        scratch=[pltpu.VMEM((2, feats * FEAT_PAD, HID), BF)],
+    loads = in_hbm(own, chip)
+    results = [((feats * FEAT_PAD, nodes), BF), ((2, feats * FEAT_PAD, HID), BF), ((2, HID, HID), BF), ((2, LANE, HID), BF), ((8, HID), F32)]
+    ft, win, wmid, wout, norms = run(
+        side_kernel, [pltpu.HBM(*r) for r in results], *loads, core, far, at, hbm_in=range(2), smem_in=(4,), hbm_out=range(5),
+        scratch=[pltpu.VMEM(*r) for r in results] + [pltpu.VMEM(a.shape, a.dtype) for a in loads]
+        + [pltpu.SemaphoreType.DMA((2,)), pltpu.SemaphoreType.DMA((5,))],
+    )
+    loads = in_hbm(inner_adj, bound_adj, keep_slots, send_index, ft, win, norms)
+    ring, bound_ring = (4, 8) if parts <= 16 else (2, 2)
+    adj, edge, row_deg, sel, mean_one, xhat_one, slope_one, istd_one, h_one, inv_deg, send = run(
+        functools.partial(first_kernel, width=width),
+        [bf(nodes, nodes), bf(nodes, halo), shape(nodes, LANE), bf(halo, nodes), bf(nodes, LANE),
+         shape(nodes, HID), shape(nodes, HID), shape(nodes, LANE), bf(nodes, HID), shape(nodes, LANE), bf(halo, HID)],
+        *loads, recv, hbm_in=range(7),
+        scratch=[pltpu.VMEM((halo, LANE), BF), pltpu.VMEM(keep_slots.shape, jnp.int32), pltpu.VMEM(send_index.shape, jnp.int32)]
+        + [pltpu.VMEM(a.shape, a.dtype) for a in loads[4:]]
+        + [pltpu.VMEM((ring, CONVERT_TILE, nodes), jnp.int32), pltpu.VMEM((bound_ring, CONVERT_TILE, halo), jnp.int32),
+           pltpu.SemaphoreType.DMA((2, max(ring, bound_ring))), pltpu.SemaphoreType.DMA((5,))],
     )
     halo_one = exchange(send, parts).reshape(halo, HID)
     mean_two, xhat_two, slope_two, istd_two, h_two, send = run(
@@ -661,13 +721,13 @@
     mean_head, logits, pred, cross, mine, send = run(
         head_kernel,
         [bf(nodes, HID), shape(nodes, LANE), bf(nodes, LANE), shape(halo, LANE), shape(halo, LANE), bf(halo, HID)],
-        adj, edge, halo_two, h_two, wout, inv_deg, sel, mask, col_deg,
+        adj, edge, halo_two, h_two, wout, inv_deg, sel, mask,
     )
     recv = exchange(send, parts).reshape(halo, HID)
     grad, grad_sum, send, losses = run(
         functools.partial(logit_grad_kernel, classes=classes, each=each),
         [bf(nodes, LANE), bf(nodes, HID), bf(halo, HID), shape(8, LANE)],
-        logits, labels, mask, row_deg, pred, edge, recv, mine, cross, col_deg, sel, wout, inv_deg,
+        logits, labels, mask, row_deg, pred, edge, recv, mine, cross, sel, wout, inv_deg,
         scratch=[pltpu.VMEM((halo, LANE), BF), pltpu.VMEM((halo, LANE), BF), pltpu.VMEM((nodes, LANE), F32), pltpu.VMEM((nodes, LANE), F32)],
     )
     recv = exchange(send, parts).reshape(halo, HID)

time: 130 us -> 126 us (0.969)
  blocking collectives: 74.7 us -> 63.4 us
  starting transfers between devices: 5.49 us -> 10.2 us
  waiting for transfers between devices: 2.97 us -> 6.83 us
    all_to_all x7 -> x6, blocking collectives: 74.7 us -> 63.4 us  [exchange(): lax.all_to_all(x.reshape(parts, -1, x.shape[-1]), 'dom', split_axis=0, co...]
    all_to_all x0 -> x1, starting transfers between devices: none -> 4.92 us  [shards(): lax.all_to_all(send.reshape(parts * feats, each // 2, LANE), ('dom', 'fea...]
    all_to_all x0 -> x1, waiting for transfers between devices: none -> 2.79 us  [shards(): lax.all_to_all(send.reshape(parts * feats, each // 2, LANE), ('dom', 'fea...]
    pallas_call x11 -> x10, Pallas kernels: 44.8 us -> 44.1 us  [call(): pl.pallas_call(kernel, out_shape=outs, in_specs=[SMEM if i in smem_in els...]
  transfers between devices with their start and end apart: 6 -> 7, of which waited for: 3 -> 6; matrix products, arithmetic and copies ran while one was open for 0% -> 0% of each run, Pallas kernels for 6% -> 2%
where the time goes in v3:
time: 126 us
  blocking collectives  63.4 us (50%)
  Pallas kernels  44.1 us (35%)
  starting transfers between devices  10.2 us (8%)
  waiting for transfers between devices  6.83 us (5%)
    all_to_all x6, blocking collectives, exchange(): lax.all_to_all(x.reshape(parts, -1, x.shape[-1]), 'dom', split_axis=0, co...  63.4 us
    pallas_call x10, Pallas kernels, call(): pl.pallas_call(kernel, out_shape=outs, in_specs=[SMEM if i in smem_in els...  44.1 us
    all_to_all x1, starting transfers between devices, shards(): lax.all_to_all(send.reshape(parts * feats, each // 2, LANE), ('dom', 'fea...  4.92 us
    ppermute x1, starting transfers between devices, shards(): chip = lax.ppermute(own, 'feat', [(s, s ^ 2) for s in range(feats)])  3 us
    all_to_all x1, waiting for transfers between devices, shards(): lax.all_to_all(send.reshape(parts * feats, each // 2, LANE), ('dom', 'fea...  2.79 us
  transfers between devices with their start and end apart: 7, of which 6 were waited for; matrix products, arithmetic and copies ran while one was open for 0% of the time, Pallas kernels for 2%

profile of v3, /device:TPU:0, one launch (start us, length us, event | category | flops | bytes accessed | tf_op | source)
XLA Modules:
  0.0 125.7 jit_solution(13923768112268101384)
XLA Ops:
  0.7 2.6 %shard_map.322 = (bf16[8,4,16,128]{3,2,1,0:T(8,128)(2,1)}, bf16[480,256]{1,0:T(8,128)(2,1)S(1)}, s32[1]{0:T(128)}) custom-call(s32[1,8,32]{2,1,0:T(8,128)} %idx_hbm.3, f32[25,2048]{1,0:T(8,128)} %bitcast.51, f32[25,2,256]{2,1,0:T(2,128)} %bitcast.36, f32[2,64,256]{2,1,0:T(8,128)} %w_mid.1, f32[47,2,64]{2,1,0:T(2,128)} %bitcast.38, f32[2,2,64]{2,1,0:T(2,128)} %norm.1, ...), custom_call_target="tpu_custom_call" | custom-call | bytes 197506 | tf_op jit(solution)/shard_map/pallas_call | solution.py:80
  3.2 0.0 copy-start.4
  3.2 3.0 %collective-permute-start = (bf16[480,256]{1,0:T(8,128)(2,1)S(1)}, bf16[480,256]{1,0:T(8,128)(2,1)S(1)}, u32[]{:S(2)}, u32[]{:S(2)}) collective-permute-start(bf16[480,256]{1,0:T(8,128)(2,1)S(1)} %get-tuple-element.81.own_hbm), channel_id=1, source_target_pairs={{0,2},{1,3},{2,0},{3,1},{4,6},{5,7},{6,4},{7,5},{8,10},{9,11},{10,... | collective-permute-start | bytes 737288 | tf_op jit(solution)/shard_map/ppermute | solution.py:692
  6.2 4.9 %all-to-all-start = ((bf16[32,16,128]{2,1,0:T(8,128)(2,1)}), bf16[32,16,128]{2,1,0:T(8,128)(2,1)S(1)}, u32[]{:S(2)}, u32[]{:S(2)}) async-start(bf16[32,16,128]{2,1,0:T(8,128)(2,1)} %bitcast.4), calls=%async_computation | async-start | bytes 262144 | tf_op jit(solution)/shard_map/all_to_all | solution.py:689
  11.2 0.3 collective-permute-start.1
  11.5 0.7 collective-permute-done.chip_hbm
  12.2 0.0 collective-permute-start.2
  12.2 0.5 collective-permute-done.1.core_ref
  12.8 1.0 collective-permute-done.2.far_ref
  13.7 0.0 copy-done.4
  13.7 0.0 copy-done.19
  13.7 2.9 %shard_map.323 = (bf16[128,2048]{1,0:T(8,128)(2,1)}, bf16[2,128,256]{2,1,0:T(8,128)(2,1)}, bf16[2,256,256]{2,1,0:T(8,128)(2,1)}, bf16[2,128,256]{2,1,0:T(8,128)(2,1)}, f32[8,256]{1,0:T(8,128)}) custom-call(bf16[480,256]{1,0:T(8,128)(2,1)} %copy-done.4, bf16[480,256]{1,0:T(8,128)(2,1)} %copy-done.19, bf16[480,256]{1,0:T(8,128)(2,1)S(1)} %collective-permute-done.1.core_ref, ...), custom_call_target="tpu_custom_call" | custom-call | bytes 509953 | tf_op jit(solution)/shard_map/pallas_call | solution.py:80
  16.6 2.8 %all-to-all-done = bf16[32,16,128]{2,1,0:T(8,128)(2,1)S(1)} async-done(((bf16[32,16,128]{2,1,0:T(8,128)(2,1)}), bf16[32,16,128]{2,1,0:T(8,128)(2,1)S(1)}, u32[]{:S(2)}, u32[]{:S(2)}) %all-to-all-start) | async-done | bytes 131104 | tf_op jit(solution)/shard_map/all_to_all | solution.py:689
  19.4 10.7 %shard_map.324 = (bf16[2048,2048]{1,0:T(8,128)(2,1)S(1)}, bf16[2048,256]{1,0:T(8,128)(2,1)S(1)}, f32[2048,128]{1,0:T(8,128)S(1)}, bf16[256,2048]{1,0:T(8,128)(2,...) custom-call(s32[2048,2048]{1,0:T(8,128)} %adj_hbm.1, ...), custom_call_target="tpu_custom_call" | custom-call | bytes 9800192 | tf_op jit(solution)/shard_map/pallas_call | solution.py:80
  30.1 11.0 %all_to_all.35 = bf16[8,32,256]{2,1,0:T(8,128)(2,1)S(1)} all-to-all(bf16[8,32,256]{2,1,0:T(8,128)(2,1)S(1)} %bitcast.40), channel_id=1, replica_groups=mesh['dom'=8,'feat'=4] {'dom'}, dimensions={0} | all-to-all | bytes 262144 | tf_op jit(solution)/shard_map/all_to_all | solution.py:628
  41.1 0.0 copy-done
  41.1 0.0 copy-done.7
  41.1 5.1 %shard_map.325 = (bf16[2048,256]{1,0:T(8,128)(2,1)S(1)}, f32[2048,256]{1,0:T(8,128)S(1)}, f32[2048,256]{1,0:T(8,128)S(1)}, f32[2048,128]{1,0:T(8,128)S(1)}, bf16...) custom-call(bf16[2048,2048]{1,0:T(8,128)(2,1)S(1)} %get-tuple-element.87.adj_ref, ...), custom_call_target="tpu_custom_call" | custom-call | bytes 5113856 | tf_op jit(solution)/shard_map/pallas_call | solution.py:80
  46.1 9.8 %all_to_all.36 = bf16[8,32,256]{2,1,0:T(8,128)(2,1)S(1)} all-to-all(bf16[8,32,256]{2,1,0:T(8,128)(2,1)S(1)} %bitcast.42), channel_id=1, replica_groups=mesh['dom'=8,'feat'=4] {'dom'}, dimensions={0} | all-to-all | bytes 262144 | tf_op jit(solution)/shard_map/all_to_all | solution.py:628
  55.9 0.0 copy-done.2
  55.9 0.0 copy-done.14
  56.0 4.5 %shard_map.326 = (bf16[2048,256]{1,0:T(8,128)(2,1)S(1)}, f32[2048,128]{1,0:T(8,128)S(1)}, bf16[2048,128]{1,0:T(8,128)(2,1)S(1)}, f32[256,128]{1,0:T(8,128)S(1)},...) custom-call(bf16[2048,2048]{1,0:T(8,128)(2,1)S(1)} %get-tuple-element.87.adj_ref, ...), custom_call_target="tpu_custom_call" | custom-call | bytes 3966976 | tf_op jit(solution)/shard_map/pallas_call | solution.py:80
  60.5 9.7 %all_to_all.37 = bf16[8,32,256]{2,1,0:T(8,128)(2,1)S(1)} all-to-all(bf16[8,32,256]{2,1,0:T(8,128)(2,1)S(1)} %bitcast.43), channel_id=1, replica_groups=mesh['dom'=8,'feat'=4] {'dom'}, dimensions={0} | all-to-all | bytes 262144 | tf_op jit(solution)/shard_map/all_to_all | solution.py:628
  70.2 0.0 copy-done.15
  70.2 3.3 %shard_map.327 = (bf16[2048,128]{1,0:T(8,128)(2,1)S(1)}, bf16[2048,256]{1,0:T(8,128)(2,1)S(1)}, bf16[256,256]{1,0:T(8,128)(2,1)S(1)}, f32[8,128]{1,0:T(8,128)S(1)}) custom-call(f32[2048,128]{1,0:T(8,128)S(1)} %get-tuple-element.97.logit_ref, s32[16,128]{1,0:T(8,128)S(1)} %bitcast.50, s32[16,128]{1,0:T(8,128)S(1)} %bitcast.49, ...), custom_call_target="tpu_custom_call" | custom-call | bytes 2003968 | tf_op jit(solution)/shard_map/pallas_call | solution.py:80
  73.5 9.7 %all_to_all.38 = bf16[8,32,256]{2,1,0:T(8,128)(2,1)S(1)} all-to-all(bf16[8,32,256]{2,1,0:T(8,128)(2,1)S(1)} %bitcast.41), channel_id=1, replica_groups=mesh['dom'=8,'feat'=4] {'dom'}, dimensions={0} | all-to-all | bytes 262144 | tf_op jit(solution)/shard_map/all_to_all | solution.py:628
  83.2 6.9 %shard_map.328 = (bf16[2048,256]{1,0:T(8,128)(2,1)S(1)}, bf16[2048,256]{1,0:T(8,128)(2,1)S(1)}, bf16[8,64,256]{2,1,0:T(8,128)(2,1)S(1)}, f32[8,256]{1,0:T(8,128)S(1)}) custom-call(bf16[2048,2048]{1,0:T(8,128)(2,1)S(1)} %get-tuple-element.87.adj_ref, bf16[2048,256]{1,0:T(8,128)(2,1)S(1)} %get-tuple-element.103.gsin_ref, ...), custom_call_target="tpu_custom_call" | custom-call | bytes 6361089 | tf_op jit(solution)/shard_map/pallas_call | solution.py:80
  90.1 10.6 %all_to_all.39.recv_ref = bf16[8,64,256]{2,1,0:T(8,128)(2,1)S(1)} all-to-all(bf16[8,64,256]{2,1,0:T(8,128)(2,1)S(1)} %get-tuple-element.113), channel_id=1, replica_groups=mesh['dom'=8,'feat'=4] {'dom'}, dimensions={0} | all-to-all | bytes 524288 | tf_op jit(solution)/shard_map/all_to_all | solution.py:628
  100.8 0.0 copy-done.1
  100.8 0.0 copy-start.8
  100.8 0.0 copy-start.9
  100.8 0.0 copy-start.10
  100.8 0.0 copy-start.11
  100.8 0.0 copy-start.12
  100.8 0.0 copy-start.13
  100.9 0.0 copy-start.16
  100.9 0.0 copy-start.17
  100.9 0.0 copy-start.18
  100.9 5.9 %shard_map.329 = bf16[8,112,256]{2,1,0:T(8,128)(2,1)S(1)} custom-call(bf16[2048,2048]{1,0:T(8,128)(2,1)S(1)} %get-tuple-element.87.adj_ref, bf16[2048,256]{1,0:T(8,128)(2,1)S(1)} %get-tuple-element.111.gsin_ref, bf16[2048,256]{1,0:T(8,128)(2,1)S(1)} %get-tuple-element.112.grad_ref, bf16[2,256,256]{2,1,0:T(8,128)(2,1)S(1)} %copy-done, ...), custom_call_target="tpu_custom_call" | custom-call | bytes 4707329 | tf_op jit(solution)/shard_map/pallas_call | solution.py:80
  106.8 12.6 %all_to_all.40.recv_ref = bf16[8,112,256]{2,1,0:T(8,128)(2,1)S(1)} all-to-all(bf16[8,112,256]{2,1,0:T(8,128)(2,1)S(1)} %shard_map.329), channel_id=1, replica_groups=mesh['dom'=8,'feat'=4] {'dom'}, dimensions={0} | all-to-all | bytes 917504 | tf_op jit(solution)/shard_map/all_to_all | solution.py:628
  119.3 0.2 shard_map.330
  119.6 0.1 collective-permute-start.5
  119.6 1.6 %collective-permute-start.4 = (f32[8,128]{1,0:T(8,128)S(1)}, f32[8,128]{1,0:T(8,128)S(1)}, u32[]{:S(2)}, u32[]{:S(2)}) collective-permute-start(f32[8,128]{1,0:T(8,128)S(1)} %get-tuple-element.125.sq0_ref), channel_id=1, source_target_pairs={{0,2},{1,3},{2,0},{3,1},{4,6},{5,7},{6,4},{7,5},{8,10},{9,11},{10,... | collective-permute-start | bytes 12296 | tf_op jit(solution)/shard_map/ppermute | solution.py:756
  121.2 0.3 collective-permute-start.3
  121.5 1.2 collective-permute-done.5.sq3_ref
  122.7 0.7 collective-permute-done.4.sq2_ref
  123.3 0.0 collective-permute-done.3.sq1_ref
  123.4 2.1 %shard_map.331 = (f32[1,1]{1,0:T(1,128)}, f32[1,1]{1,0:T(1,128)}, f32[1,1]{1,0:T(1,128)}, f32[25,2,256]{2,1,0:T(2,128)}, f32[2,64,256]{2,1,0:T(8,128)}, /*index=...) custom-call(f32[64,256]{1,0:T(8,128)S(1)} %get-tuple-element.120.gra, ...), custom_call_target="tpu_custom_call" | custom-call | bytes 410564 | tf_op jit(solution)/shard_map/pallas_call | solution.py:80
  (22 shorter events, 0.0 us)
Async XLA Ops:
  3.2 10.5 %copy-start.4 = (bf16[480,256]{1,0:T(8,128)(2,1)}, bf16[480,256]{1,0:T(8,128)(2,1)S(1)}, u32[]{:S(2)}) copy-start(bf16[480,256]{1,0:T(8,128)(2,1)S(1)} %get-tuple-element.81.own_hbm) | copy-start | bytes 737284
  3.2 9.0 %collective-permute-start = (bf16[480,256]{1,0:T(8,128)(2,1)S(1)}, bf16[480,256]{1,0:T(8,128)(2,1)S(1)}, u32[]{:S(2)}, u32[]{:S(2)}) collective-permute-start(bf16[480,256]{1,0:T(8,128)(2,1)S(1)} %get-tuple-element.81.own_hbm), channel_id=1, source_target_pairs={{0,2},{1,3},{2,0},{3,1},{4,6},{5,7},{6,4},{7,5},{8,10},{9,11},{10,... | collective-permute-start | bytes 737288 | tf_op jit(solution)/shard_map/ppermute | solution.py:692
  6.2 13.2 %all-to-all-start = ((bf16[32,16,128]{2,1,0:T(8,128)(2,1)}), bf16[32,16,128]{2,1,0:T(8,128)(2,1)S(1)}, u32[]{:S(2)}, u32[]{:S(2)}) async-start(bf16[32,16,128]{2,1,0:T(8,128)(2,1)} %bitcast.4), calls=%async_computation | async-start | bytes 262144 | tf_op jit(solution)/shard_map/all_to_all | solution.py:689
  11.2 1.6 %collective-permute-start.1 = (bf16[480,256]{1,0:T(8,128)(2,1)S(1)}, bf16[480,256]{1,0:T(8,128)(2,1)S(1)}, u32[]{:S(2)}, u32[]{:S(2)}) collective-permute-start(bf16[480,256]{1,0:T(8,128)(2,1)S(1)} %get-tuple-element.81.own_hbm), channel_id=1, source_target_pairs={{0,1},{1,0},{2,3},{3,2},{4,5},{5,4},{6,7},{7,6},{8,9},{9,8},{10,11... | collective-permute-start | bytes 737288 | tf_op jit(solution)/shard_map/ppermute | solution.py:693
  12.2 1.5 %copy-start.19 = (bf16[480,256]{1,0:T(8,128)(2,1)}, bf16[480,256]{1,0:T(8,128)(2,1)S(1)}, u32[]{:S(2)}) copy-start(bf16[480,256]{1,0:T(8,128)(2,1)S(1)} %collective-permute-done.chip_hbm) | copy-start | bytes 737284
  12.2 1.5 %collective-permute-start.2 = (bf16[480,256]{1,0:T(8,128)(2,1)S(1)}, bf16[480,256]{1,0:T(8,128)(2,1)S(1)}, u32[]{:S(2)}, u32[]{:S(2)}) collective-permute-start(bf16[480,256]{1,0:T(8,128)(2,1)S(1)} %collective-permute-done.chip_hbm), channel_id=1, source_target_pairs={{0,1},{1,0},{2,3},{3,2},{4,5},{5,4},{6,7},{7,6},{8,9},{9,8},{10,11... | collective-permute-start | bytes 737288 | tf_op jit(solution)/shard_map/ppermute | solution.py:694
  19.4 21.7 %copy-start = (bf16[2,256,256]{2,1,0:T(8,128)(2,1)S(1)}, bf16[2,256,256]{2,1,0:T(8,128)(2,1)}, u32[]{:S(2)}) copy-start(bf16[2,256,256]{2,1,0:T(8,128)(2,1)} %get-tuple-element.91.w_ref) | copy-start | bytes 786436
  19.4 21.7 %copy-start.7 = (f32[8,256]{1,0:T(8,128)S(1)}, f32[8,256]{1,0:T(8,128)}, u32[]{:S(2)}) copy-start(f32[8,256]{1,0:T(8,128)} %get-tuple-element.85.norm_hbm.norm_ref) | copy-start | bytes 24580
  41.1 14.9 %copy-start.2 = (bf16[2,128,256]{2,1,0:T(8,128)(2,1)S(1)}, bf16[2,128,256]{2,1,0:T(8,128)(2,1)}, u32[]{:S(2)}) copy-start(bf16[2,128,256]{2,1,0:T(8,128)(2,1)} %get-tuple-element.96.w_ref.wout_ref) | copy-start | bytes 393220
  41.1 14.9 %copy-start.14 = (s32[2048]{0:T(1024)S(1)}, s32[2048]{0:T(1024)}, u32[]{:S(2)}) copy-start(s32[2048]{0:T(1024)} %param.25) | copy-start | bytes 24580
  55.9 14.3 %copy-start.15 = (s32[2048]{0:T(1024)S(1)}, s32[2048]{0:T(1024)}, u32[]{:S(2)}) copy-start(s32[2048]{0:T(1024)} %param.24) | copy-start | bytes 24580
  83.2 17.5 %copy-start.1 = (bf16[128,2048]{1,0:T(8,128)(2,1)S(1)}, bf16[128,2048]{1,0:T(8,128)(2,1)}, u32[]{:S(2)}) copy-start(bf16[128,2048]{1,0:T(8,128)(2,1)} %get-tuple-element.83.ft_hbm.ft_ref) | copy-start | bytes 1572868
  100.8 22.5 %copy-start.3 = (f32[2,64,256]{2,1,0:T(8,128)S(1)}, f32[2,64,256]{2,1,0:T(8,128)}, u32[]{:S(2)}) copy-start(f32[2,64,256]{2,1,0:T(8,128)} %w_mid.1) | copy-start | bytes 393220
  100.8 22.5 %copy-start.5 = (f32[2,25,256]{2,0,1:T(2,128)S(1)}, f32[2,25,256]{2,0,1:T(2,128)}, u32[]{:S(2)}) copy-start(f32[2,25,256]{2,0,1:T(2,128)} %param.26) | copy-start | bytes 153604
  100.8 22.5 %copy-start.6 = (f32[2,64,47]{1,0,2:T(2,128)S(1)}, f32[2,64,47]{1,0,2:T(2,128)}, u32[]{:S(2)}) copy-start(f32[2,64,47]{1,0,2:T(2,128)} %param.28) | copy-start | bytes 72196
  100.8 22.6 %copy-start.8 = (f32[2,64,256]{2,1,0:T(8,128)S(1)}, f32[2,64,256]{2,1,0:T(8,128)}, u32[]{:S(2)}) copy-start(f32[2,64,256]{2,1,0:T(8,128)} %m_mid.1) | copy-start | bytes 393220
  100.8 22.5 %copy-start.9 = (f32[2,64,256]{2,1,0:T(8,128)S(1)}, f32[2,64,256]{2,1,0:T(8,128)}, u32[]{:S(2)}) copy-start(f32[2,64,256]{2,1,0:T(8,128)} %v_mid.1) | copy-start | bytes 393220
  100.8 22.5 %copy-start.10 = (f32[2,25,256]{2,0,1:T(2,128)S(1)}, f32[2,25,256]{2,0,1:T(2,128)}, u32[]{:S(2)}) copy-start(f32[2,25,256]{2,0,1:T(2,128)} %param.30) | copy-start | bytes 153604
  100.8 22.5 %copy-start.11 = (f32[2,25,256]{2,0,1:T(2,128)S(1)}, f32[2,25,256]{2,0,1:T(2,128)}, u32[]{:S(2)}) copy-start(f32[2,25,256]{2,0,1:T(2,128)} %param.34) | copy-start | bytes 153604
  100.8 22.5 %copy-start.12 = (f32[2,64,47]{1,0,2:T(2,128)S(1)}, f32[2,64,47]{1,0,2:T(2,128)}, u32[]{:S(2)}) copy-start(f32[2,64,47]{1,0,2:T(2,128)} %param.32) | copy-start | bytes 72196
  100.8 22.5 %copy-start.13 = (f32[2,64,47]{1,0,2:T(2,128)S(1)}, f32[2,64,47]{1,0,2:T(2,128)}, u32[]{:S(2)}) copy-start(f32[2,64,47]{1,0,2:T(2,128)} %param.36) | copy-start | bytes 72196
  100.9 22.5 %copy-start.16 = (f32[2,2,64]{2,1,0:T(2,128)S(1)}, f32[2,2,64]{2,1,0:T(2,128)}, u32[]{:S(2)}) copy-start(f32[2,2,64]{2,1,0:T(2,128)} %norm.1) | copy-start | bytes 3076
  100.9 22.5 %copy-start.17 = (f32[2,2,64]{2,1,0:T(2,128)S(1)}, f32[2,2,64]{2,1,0:T(2,128)}, u32[]{:S(2)}) copy-start(f32[2,2,64]{2,1,0:T(2,128)} %m_norm.1) | copy-start | bytes 3076
  100.9 22.5 %copy-start.18 = (f32[2,2,64]{2,1,0:T(2,128)S(1)}, f32[2,2,64]{2,1,0:T(2,128)}, u32[]{:S(2)}) copy-start(f32[2,2,64]{2,1,0:T(2,128)} %v_norm.1) | copy-start | bytes 3076
  119.6 3.1 %collective-permute-start.5 = (f32[8,128]{1,0:T(8,128)S(1)}, f32[8,128]{1,0:T(8,128)S(1)}, u32[]{:S(2)}, u32[]{:S(2)}) collective-permute-start(f32[8,128]{1,0:T(8,128)S(1)} %get-tuple-element.125.sq0_ref), channel_id=1, source_target_pairs={{0,3},{1,2},{2,1},{3,0},{4,7},{5,6},{6,5},{7,4},{8,11},{9,10},{10,... | collective-permute-start | bytes 12296 | tf_op jit(solution)/shard_map/ppermute | solution.py:756
  119.6 3.7 %collective-permute-start.4 = (f32[8,128]{1,0:T(8,128)S(1)}, f32[8,128]{1,0:T(8,128)S(1)}, u32[]{:S(2)}, u32[]{:S(2)}) collective-permute-start(f32[8,128]{1,0:T(8,128)S(1)} %get-tuple-element.125.sq0_ref), channel_id=1, source_target_pairs={{0,2},{1,3},{2,0},{3,1},{4,6},{5,7},{6,4},{7,5},{8,10},{9,11},{10,... | collective-permute-start | bytes 12296 | tf_op jit(solution)/shard_map/ppermute | solution.py:756
  121.2 2.1 %collective-permute-start.3 = (f32[8,128]{1,0:T(8,128)S(1)}, f32[8,128]{1,0:T(8,128)S(1)}, u32[]{:S(2)}, u32[]{:S(2)}) collective-permute-start(f32[8,128]{1,0:T(8,128)S(1)} %get-tuple-element.125.sq0_ref), channel_id=1, source_target_pairs={{0,1},{1,0},{2,3},{3,2},{4,5},{5,4},{6,7},{7,6},{8,9},{9,8},{10,11... | collective-permute-start | bytes 12296 | tf_op jit(solution)/shard_map/ppermute | solution.py:756

commit v4 on v3

--- a/solution.py
+++ b/solution.py
@@ -227,7 +227,8 @@
     x_hat = (joined - center) * inv_std
     normed = x_hat * norm_ref[2 * layer : 2 * layer + 1, :] + norm_ref[2 * layer + 1 : 2 * layer + 2, :]
     gate = 0.5 * jnp.tanh(0.5 * normed) + 0.5
-    return inv_std, x_hat, normed * gate, gate * (1.0 + normed * (1.0 - gate))
+    hidden = normed * gate
+    return inv_std, x_hat, hidden, gate + hidden * (1.0 - gate)
 
 
 def keep_norm(s, parts, xhat_ref, slope_ref, istd_ref, h_ref):
@@ -343,7 +344,7 @@
         mean_ref[s, :] = (summed * both(invd_ref[s, :])).astype(BF)
         return 0
 
-    loop(adj_ref.shape[0], TILE, gather)
+    loop(adj_ref.shape[0], 2 * TILE, gather)
 
 
 def second_kernel(adj_ref, edge_ref, halo_ref, hin_ref, w_ref, norm_ref, invd_ref, sel_ref,
@@ -590,38 +591,33 @@
     return fresh, first_new, second_new
 
 
-def update_kernel(grads_ref, gnorm_ref, total_ref, gmid_ref, gout_ref, sq0_ref, sq1_ref, sq2_ref, sq3_ref, loss_ref,
-                  w_in, w_mid, w_out, norm, m_in, m_mid, m_out, m_norm, v_in, v_mid, v_out, v_norm, at_ref,
-                  loss_out, count_out, gnorm_out,
-                  nw_in, nw_mid, nw_out, nnorm, nm_in, nm_mid, nm_out, nm_norm, nv_in, nv_mid, nv_out, nv_norm,
-                  c_in, c_mid, c_out):
+def turn_kernel(grads_ref, gnorm_ref, gmid_ref, gout_ref, at_ref, in_ref, mid_ref, out_ref, norm_ref):
+    width, classes, share = in_ref.shape[0], out_ref.shape[0], mid_ref.shape[1]
+    whole = gnorm_ref[...]
+    mine = jnp.zeros((8, share), F32)
+    for f in range(HID // share):
+        mine = mine + jnp.where(at_ref[0] == f, whole[:, f * share : (f + 1) * share], 0.0)
+    for k in range(2):
+        in_ref[:, k, :] = grads_ref[k * FEAT_PAD : k * FEAT_PAD + width, :]
+        mid_ref[k] = gmid_ref[k * share : (k + 1) * share, :]
+        out_ref[:, k, :] = jnp.transpose(gout_ref[:, k * LANE : (k + 1) * LANE])[0:classes, :]
+        norm_ref[k] = mine[2 * k : 2 * k + 2, :]
+
+
+def update_kernel(total_ref, sq0_ref, sq1_ref, sq2_ref, sq3_ref, loss_ref, *refs):
+    grads, params, firsts, seconds = (refs[i : i + 4] for i in range(0, 16, 4))
+    loss_out, count_out, gnorm_out, *results = refs[16:]
     loss_out[...] = total_ref[0:1, 0:1]
     count_out[...] = loss_ref[2:3, 0:1]
     square = (sq0_ref[0:1, 0:1] + sq1_ref[0:1, 0:1]) + (sq2_ref[0:1, 0:1] + sq3_ref[0:1, 0:1])
     grad_norm = jnp.sqrt(square + sq0_ref[1:2, 0:1])
     gnorm_out[...] = grad_norm
-    factor = jnp.minimum(1.0, CLIP_LEVEL / (grad_norm + 1e-06))
-
-    def step(index, grad, w, m, v, nw, nm, nv, copy):
-        fresh, first, second = adam(w[index], grad * factor, m[index], v[index])
-        nw[index], nm[index], nv[index] = fresh, first, second
-        if copy is not None:
-            copy[index] = fresh.astype(BF)
-
-    every = slice(None)
-    width, _, share = w_in.shape[0], 2, w_mid.shape[1]
-    classes = w_out.shape[0]
-    for k in range(2):
-        step((every, k, every), grads_ref[k * FEAT_PAD : k * FEAT_PAD + width, :], w_in, m_in, v_in, nw_in, nm_in, nv_in, c_in)
-        step(k, gmid_ref[k * share : (k + 1) * share, :], w_mid, m_mid, v_mid, nw_mid, nm_mid, nv_mid, c_mid)
-        turned = jnp.transpose(gout_ref[:, k * LANE : (k + 1) * LANE])[0:classes, :]
-        step((every, k, every), turned, w_out, m_out, v_out, nw_out, nm_out, nv_out, c_out)
-    whole = gnorm_ref[...]
-    mine = jnp.zeros((8, share), F32)
-    for f in range(HID // share):
-        mine = mine + jnp.where(at_ref[0] == f, whole[:, f * share : (f + 1) * share], 0.0)
-    for layer in range(2):
-        step(layer, mine[2 * layer : 2 * layer + 2, :], norm, m_norm, v_norm, nnorm, nm_norm, nv_norm, None)
+    factor = jnp.minimum(1.0, CLIP_LEVEL / (grad_norm + 1e-06)).reshape(1, 1, 1)
+    for i in range(4):
+        fresh, first, second = adam(params[i][...], grads[i][...] * factor, firsts[i][...], seconds[i][...])
+        results[i][...], results[4 + i][...], results[8 + i][...] = fresh, first, second
+        if i < 3:
+            results[12 + i][...] = fresh.astype(BF)
 
 
 def exchange(x, parts):
@@ -747,7 +743,7 @@
                  pltpu.VMEM((halo, HID), BF)],
     )
     recv = exchange(send, parts)
-    *grads, square = run(
+    grads, gnorm, total, gmid, gout, square = run(
         functools.partial(total_kernel, width=width),
         [shape(CHUNK_ROW, HID), shape(8, HID), shape(8, LANE), shape(2 * share, HID), shape(share, HID), shape(8, LANE)], recv,
     )
@@ -755,7 +751,8 @@
     for k in range(1, feats):
         squares.append(lax.ppermute(square, "feat", [(s, s ^ k) for s in range(feats)]))
     outs = [shape(1, 1)] * 3 + [shape(*p.shape) for p in params] * 3 + [bf(*p.shape) for p in params[:3]]
-    result = run(update_kernel, outs, *grads, *squares, losses, *params, *firsts, *seconds, at, smem_in=(22,))
+    grads = run(turn_kernel, [shape(*p.shape) for p in params], grads, gnorm, gmid, gout, at, smem_in=(4,))
+    result = run(update_kernel, outs, total, *squares, losses, *grads, *params, *firsts, *seconds)
     return (
         tuple(r.reshape(()) for r in result[:3])
         + restore(*result[3:7]) + restore(*result[7:11]) + restore(*result[11:15]) + restore(*result[15:])

time: 126 us -> 125 us (level)
    pallas_call x10 -> x11, Pallas kernels: 44.1 us -> 44 us  [call(): pl.pallas_call(kernel, out_shape=outs, in_specs=[SMEM if i in smem_in els...]
  transfers between devices with their start and end apart: 7 -> 7, of which waited for: 6 -> 6; matrix products, arithmetic and copies ran while one was open for 0% -> 0% of each run, Pallas kernels for 2% -> 3%
where the time goes in v4:
time: 125 us
  blocking collectives  63.5 us (51%)
  Pallas kernels  44 us (35%)
  starting transfers between devices  10.2 us (8%)
  waiting for transfers between devices  6.05 us (5%)
    all_to_all x6, blocking collectives, exchange(): lax.all_to_all(x.reshape(parts, -1, x.shape[-1]), 'dom', split_axis=0, co...  63.5 us
    pallas_call x11, Pallas kernels, call(): pl.pallas_call(kernel, out_shape=outs, in_specs=[SMEM if i in smem_in els...  44 us
    all_to_all x1, starting transfers between devices, shards(): lax.all_to_all(send.reshape(parts * feats, each // 2, LANE), ('dom', 'fea...  4.92 us
    ppermute x1, starting transfers between devices, shards(): chip = lax.ppermute(own, 'feat', [(s, s ^ 2) for s in range(feats)])  3 us
    all_to_all x1, waiting for transfers between devices, shards(): lax.all_to_all(send.reshape(parts * feats, each // 2, LANE), ('dom', 'fea...  2.76 us
  transfers between devices with their start and end apart: 7, of which 6 were waited for; matrix products, arithmetic and copies ran while one was open for 0% of the time, Pallas kernels for 3%

profile of v4, /device:TPU:0, one launch (start us, length us, event | category | flops | bytes accessed | tf_op | source)
XLA Modules:
  0.0 124.8 jit_solution(15120143684389734925)
XLA Ops:
  0.7 2.6 %shard_map.322 = (bf16[8,4,16,128]{3,2,1,0:T(8,128)(2,1)}, bf16[480,256]{1,0:T(8,128)(2,1)S(1)}, s32[1]{0:T(128)}) custom-call(s32[1,8,32]{2,1,0:T(8,128)} %idx_hbm.3, f32[25,2048]{1,0:T(8,128)} %bitcast.51, f32[25,2,256]{2,1,0:T(2,128)} %bitcast.36, f32[2,64,256]{2,1,0:T(8,128)} %refs_5_.1, f32[47,2,64]{2,1,0:T(2,128)} %bitcast.38, f32[2,2,64]{2,1,0:T(2,128)} %refs_7_.1, ...), custom_call_target="tpu_custom_call" | custom-call | bytes 197506 | tf_op jit(solution)/shard_map/pallas_call | solution.py:80
  3.2 0.0 copy-start.4
  3.2 3.0 %collective-permute-start = (bf16[480,256]{1,0:T(8,128)(2,1)S(1)}, bf16[480,256]{1,0:T(8,128)(2,1)S(1)}, u32[]{:S(2)}, u32[]{:S(2)}) collective-permute-start(bf16[480,256]{1,0:T(8,128)(2,1)S(1)} %get-tuple-element.85.own_hbm), channel_id=1, source_target_pairs={{0,2},{1,3},{2,0},{3,1},{4,6},{5,7},{6,4},{7,5},{8,10},{9,11},{10,... | collective-permute-start | bytes 737288 | tf_op jit(solution)/shard_map/ppermute | solution.py:688
  6.2 4.9 %all-to-all-start = ((bf16[32,16,128]{2,1,0:T(8,128)(2,1)}), bf16[32,16,128]{2,1,0:T(8,128)(2,1)S(1)}, u32[]{:S(2)}, u32[]{:S(2)}) async-start(bf16[32,16,128]{2,1,0:T(8,128)(2,1)} %bitcast.4), calls=%async_computation | async-start | bytes 262144 | tf_op jit(solution)/shard_map/all_to_all | solution.py:685
  11.2 0.3 collective-permute-start.1
  11.5 0.7 collective-permute-done.chip_hbm
  12.2 0.0 collective-permute-start.2
  12.2 0.5 collective-permute-done.1.core_ref
  12.8 1.0 collective-permute-done.2.far_ref
  13.7 0.0 copy-done.4
  13.7 0.0 copy-done.19
  13.7 2.9 %shard_map.323 = (bf16[128,2048]{1,0:T(8,128)(2,1)}, bf16[2,128,256]{2,1,0:T(8,128)(2,1)}, bf16[2,256,256]{2,1,0:T(8,128)(2,1)}, bf16[2,128,256]{2,1,0:T(8,128)(2,1)}, f32[8,256]{1,0:T(8,128)}) custom-call(bf16[480,256]{1,0:T(8,128)(2,1)} %copy-done.4, bf16[480,256]{1,0:T(8,128)(2,1)} %copy-done.19, bf16[480,256]{1,0:T(8,128)(2,1)S(1)} %collective-permute-done.1.core_ref, ...), custom_call_target="tpu_custom_call" | custom-call | bytes 509953 | tf_op jit(solution)/shard_map/pallas_call | solution.py:80
  16.6 2.8 %all-to-all-done = bf16[32,16,128]{2,1,0:T(8,128)(2,1)S(1)} async-done(((bf16[32,16,128]{2,1,0:T(8,128)(2,1)}), bf16[32,16,128]{2,1,0:T(8,128)(2,1)S(1)}, u32[]{:S(2)}, u32[]{:S(2)}) %all-to-all-start) | async-done | bytes 131104 | tf_op jit(solution)/shard_map/all_to_all | solution.py:685
  19.4 10.7 %shard_map.324 = (bf16[2048,2048]{1,0:T(8,128)(2,1)S(1)}, bf16[2048,256]{1,0:T(8,128)(2,1)S(1)}, f32[2048,128]{1,0:T(8,128)S(1)}, bf16[256,2048]{1,0:T(8,128)(2,...) custom-call(s32[2048,2048]{1,0:T(8,128)} %adj_hbm.1, ...), custom_call_target="tpu_custom_call" | custom-call | bytes 9800192 | tf_op jit(solution)/shard_map/pallas_call | solution.py:80
  30.1 11.0 %all_to_all.35 = bf16[8,32,256]{2,1,0:T(8,128)(2,1)S(1)} all-to-all(bf16[8,32,256]{2,1,0:T(8,128)(2,1)S(1)} %bitcast.40), channel_id=1, replica_groups=mesh['dom'=8,'feat'=4] {'dom'}, dimensions={0} | all-to-all | bytes 262144 | tf_op jit(solution)/shard_map/all_to_all | solution.py:624
  41.1 0.0 copy-done
  41.1 0.0 copy-done.7
  41.1 5.0 %shard_map.325 = (bf16[2048,256]{1,0:T(8,128)(2,1)S(1)}, f32[2048,256]{1,0:T(8,128)S(1)}, f32[2048,256]{1,0:T(8,128)S(1)}, f32[2048,128]{1,0:T(8,128)S(1)}, bf16...) custom-call(bf16[2048,2048]{1,0:T(8,128)(2,1)S(1)} %get-tuple-element.91.adj_ref, ...), custom_call_target="tpu_custom_call" | custom-call | bytes 5113856 | tf_op jit(solution)/shard_map/pallas_call | solution.py:80
  46.0 9.8 %all_to_all.36 = bf16[8,32,256]{2,1,0:T(8,128)(2,1)S(1)} all-to-all(bf16[8,32,256]{2,1,0:T(8,128)(2,1)S(1)} %bitcast.42), channel_id=1, replica_groups=mesh['dom'=8,'feat'=4] {'dom'}, dimensions={0} | all-to-all | bytes 262144 | tf_op jit(solution)/shard_map/all_to_all | solution.py:624
  55.8 0.0 copy-done.2
  55.8 0.0 copy-done.14
  55.9 4.5 %shard_map.326 = (bf16[2048,256]{1,0:T(8,128)(2,1)S(1)}, f32[2048,128]{1,0:T(8,128)S(1)}, bf16[2048,128]{1,0:T(8,128)(2,1)S(1)}, f32[256,128]{1,0:T(8,128)S(1)},...) custom-call(bf16[2048,2048]{1,0:T(8,128)(2,1)S(1)} %get-tuple-element.91.adj_ref, ...), custom_call_target="tpu_custom_call" | custom-call | bytes 3966976 | tf_op jit(solution)/shard_map/pallas_call | solution.py:80
  60.3 9.7 %all_to_all.37 = bf16[8,32,256]{2,1,0:T(8,128)(2,1)S(1)} all-to-all(bf16[8,32,256]{2,1,0:T(8,128)(2,1)S(1)} %bitcast.43), channel_id=1, replica_groups=mesh['dom'=8,'feat'=4] {'dom'}, dimensions={0} | all-to-all | bytes 262144 | tf_op jit(solution)/shard_map/all_to_all | solution.py:624
  70.1 0.0 copy-done.15
  70.1 3.3 %shard_map.327 = (bf16[2048,128]{1,0:T(8,128)(2,1)S(1)}, bf16[2048,256]{1,0:T(8,128)(2,1)S(1)}, bf16[256,256]{1,0:T(8,128)(2,1)S(1)}, f32[8,128]{1,0:T(8,128)S(1)}) custom-call(f32[2048,128]{1,0:T(8,128)S(1)} %get-tuple-element.101.logit_ref, s32[16,128]{1,0:T(8,128)S(1)} %bitcast.50, s32[16,128]{1,0:T(8,128)S(1)} %bitcast.49, ...), custom_call_target="tpu_custom_call" | custom-call | bytes 2003968 | tf_op jit(solution)/shard_map/pallas_call | solution.py:80
  73.3 9.7 %all_to_all.38 = bf16[8,32,256]{2,1,0:T(8,128)(2,1)S(1)} all-to-all(bf16[8,32,256]{2,1,0:T(8,128)(2,1)S(1)} %bitcast.41), channel_id=1, replica_groups=mesh['dom'=8,'feat'=4] {'dom'}, dimensions={0} | all-to-all | bytes 262144 | tf_op jit(solution)/shard_map/all_to_all | solution.py:624
  83.1 6.9 %shard_map.328 = (bf16[2048,256]{1,0:T(8,128)(2,1)S(1)}, bf16[2048,256]{1,0:T(8,128)(2,1)S(1)}, bf16[8,64,256]{2,1,0:T(8,128)(2,1)S(1)}, f32[8,256]{1,0:T(8,128)S(1)}) custom-call(bf16[2048,2048]{1,0:T(8,128)(2,1)S(1)} %get-tuple-element.91.adj_ref, bf16[2048,256]{1,0:T(8,128)(2,1)S(1)} %get-tuple-element.107.gsin_ref, ...), custom_call_target="tpu_custom_call" | custom-call | bytes 6361089 | tf_op jit(solution)/shard_map/pallas_call | solution.py:80
  90.0 10.6 %all_to_all.39.recv_ref = bf16[8,64,256]{2,1,0:T(8,128)(2,1)S(1)} all-to-all(bf16[8,64,256]{2,1,0:T(8,128)(2,1)S(1)} %get-tuple-element.117), channel_id=1, replica_groups=mesh['dom'=8,'feat'=4] {'dom'}, dimensions={0} | all-to-all | bytes 524288 | tf_op jit(solution)/shard_map/all_to_all | solution.py:624
  100.6 0.0 copy-start.8
  100.7 0.0 copy-start.9
  100.7 0.0 copy-start.10
  100.7 0.0 copy-start.11
  100.7 0.0 copy-start.12
  100.7 0.0 copy-start.13
  100.7 0.0 copy-start.16
  100.7 0.0 copy-start.17
  100.7 0.0 copy-start.18
  100.8 5.9 %shard_map.329 = bf16[8,112,256]{2,1,0:T(8,128)(2,1)S(1)} custom-call(bf16[2048,2048]{1,0:T(8,128)(2,1)S(1)} %get-tuple-element.91.adj_ref, bf16[2048,256]{1,0:T(8,128)(2,1)S(1)} %get-tuple-element.115.gsin_ref, bf16[2048,256]{1,0:T(8,128)(2,1)S(1)} %get-tuple-element.116.grad_ref, bf16[2,256,256]{2,1,0:T(8,128)(2,1)S(1)} %copy-done, ...), custom_call_target="tpu_custom_call" | custom-call | bytes 4707329 | tf_op jit(solution)/shard_map/pallas_call | solution.py:80
  106.7 12.6 %all_to_all.40.recv_ref = bf16[8,112,256]{2,1,0:T(8,128)(2,1)S(1)} all-to-all(bf16[8,112,256]{2,1,0:T(8,128)(2,1)S(1)} %shard_map.329), channel_id=1, replica_groups=mesh['dom'=8,'feat'=4] {'dom'}, dimensions={0} | all-to-all | bytes 917504 | tf_op jit(solution)/shard_map/all_to_all | solution.py:624
  119.2 0.2 shard_map.330
  119.5 0.1 collective-permute-start.5
  119.5 1.6 %collective-permute-start.4 = (f32[8,128]{1,0:T(8,128)S(1)}, f32[8,128]{1,0:T(8,128)S(1)}, u32[]{:S(2)}, u32[]{:S(2)}) collective-permute-start(f32[8,128]{1,0:T(8,128)S(1)} %get-tuple-element.125.sq0_ref), channel_id=1, source_target_pairs={{0,2},{1,3},{2,0},{3,1},{4,6},{5,7},{6,4},{7,5},{8,10},{9,11},{10,... | collective-permute-start | bytes 12296 | tf_op jit(solution)/shard_map/ppermute | solution.py:752
  121.1 0.3 collective-permute-start.3
  121.4 0.7 shard_map.331
  122.1 0.4 collective-permute-done.5.sq3_ref
  122.6 0.7 collective-permute-done.4.sq2_ref
  123.2 0.0 collective-permute-done.3.sq1_ref
  123.3 1.4 %shard_map.332 = (f32[1,1]{1,0:T(1,128)}, f32[1,1]{1,0:T(1,128)}, f32[1,1]{1,0:T(1,128)}, f32[25,2,256]{2,1,0:T(2,128)}, f32[2,64,256]{2,1,0:T(8,128)}, /*index=...) custom-call(f32[8,128]{1,0:T(8,128)S(1)} %get-tuple-element.124.tota, ...), custom_call_target="tpu_custom_call" | custom-call | bytes 394819 | tf_op jit(solution)/shard_map/pallas_call | solution.py:80
  (23 shorter events, 0.0 us)
Async XLA Ops:
  3.2 10.5 %copy-start.4 = (bf16[480,256]{1,0:T(8,128)(2,1)}, bf16[480,256]{1,0:T(8,128)(2,1)S(1)}, u32[]{:S(2)}) copy-start(bf16[480,256]{1,0:T(8,128)(2,1)S(1)} %get-tuple-element.85.own_hbm) | copy-start | bytes 737284
  3.2 9.0 %collective-permute-start = (bf16[480,256]{1,0:T(8,128)(2,1)S(1)}, bf16[480,256]{1,0:T(8,128)(2,1)S(1)}, u32[]{:S(2)}, u32[]{:S(2)}) collective-permute-start(bf16[480,256]{1,0:T(8,128)(2,1)S(1)} %get-tuple-element.85.own_hbm), channel_id=1, source_target_pairs={{0,2},{1,3},{2,0},{3,1},{4,6},{5,7},{6,4},{7,5},{8,10},{9,11},{10,... | collective-permute-start | bytes 737288 | tf_op jit(solution)/shard_map/ppermute | solution.py:688
  6.2 13.2 %all-to-all-start = ((bf16[32,16,128]{2,1,0:T(8,128)(2,1)}), bf16[32,16,128]{2,1,0:T(8,128)(2,1)S(1)}, u32[]{:S(2)}, u32[]{:S(2)}) async-start(bf16[32,16,128]{2,1,0:T(8,128)(2,1)} %bitcast.4), calls=%async_computation | async-start | bytes 262144 | tf_op jit(solution)/shard_map/all_to_all | solution.py:685
  11.2 1.6 %collective-permute-start.1 = (bf16[480,256]{1,0:T(8,128)(2,1)S(1)}, bf16[480,256]{1,0:T(8,128)(2,1)S(1)}, u32[]{:S(2)}, u32[]{:S(2)}) collective-permute-start(bf16[480,256]{1,0:T(8,128)(2,1)S(1)} %get-tuple-element.85.own_hbm), channel_id=1, source_target_pairs={{0,1},{1,0},{2,3},{3,2},{4,5},{5,4},{6,7},{7,6},{8,9},{9,8},{10,11... | collective-permute-start | bytes 737288 | tf_op jit(solution)/shard_map/ppermute | solution.py:689
  12.2 1.5 %copy-start.19 = (bf16[480,256]{1,0:T(8,128)(2,1)}, bf16[480,256]{1,0:T(8,128)(2,1)S(1)}, u32[]{:S(2)}) copy-start(bf16[480,256]{1,0:T(8,128)(2,1)S(1)} %collective-permute-done.chip_hbm) | copy-start | bytes 737284
  12.2 1.5 %collective-permute-start.2 = (bf16[480,256]{1,0:T(8,128)(2,1)S(1)}, bf16[480,256]{1,0:T(8,128)(2,1)S(1)}, u32[]{:S(2)}, u32[]{:S(2)}) collective-permute-start(bf16[480,256]{1,0:T(8,128)(2,1)S(1)} %collective-permute-done.chip_hbm), channel_id=1, source_target_pairs={{0,1},{1,0},{2,3},{3,2},{4,5},{5,4},{6,7},{7,6},{8,9},{9,8},{10,11... | collective-permute-start | bytes 737288 | tf_op jit(solution)/shard_map/ppermute | solution.py:690
  19.4 21.7 %copy-start = (bf16[2,256,256]{2,1,0:T(8,128)(2,1)S(1)}, bf16[2,256,256]{2,1,0:T(8,128)(2,1)}, u32[]{:S(2)}) copy-start(bf16[2,256,256]{2,1,0:T(8,128)(2,1)} %get-tuple-element.95.w_ref) | copy-start | bytes 786436
  19.4 21.7 %copy-start.7 = (f32[8,256]{1,0:T(8,128)S(1)}, f32[8,256]{1,0:T(8,128)}, u32[]{:S(2)}) copy-start(f32[8,256]{1,0:T(8,128)} %get-tuple-element.89.norm_hbm.norm_ref) | copy-start | bytes 24580
  41.1 14.8 %copy-start.2 = (bf16[2,128,256]{2,1,0:T(8,128)(2,1)S(1)}, bf16[2,128,256]{2,1,0:T(8,128)(2,1)}, u32[]{:S(2)}) copy-start(bf16[2,128,256]{2,1,0:T(8,128)(2,1)} %get-tuple-element.100.w_ref.wout_ref) | copy-start | bytes 393220
  41.1 14.8 %copy-start.14 = (s32[2048]{0:T(1024)S(1)}, s32[2048]{0:T(1024)}, u32[]{:S(2)}) copy-start(s32[2048]{0:T(1024)} %param.25) | copy-start | bytes 24580
  55.8 14.2 %copy-start.15 = (s32[2048]{0:T(1024)S(1)}, s32[2048]{0:T(1024)}, u32[]{:S(2)}) copy-start(s32[2048]{0:T(1024)} %param.24) | copy-start | bytes 24580
  83.1 17.6 %copy-start.1 = (bf16[128,2048]{1,0:T(8,128)(2,1)S(1)}, bf16[128,2048]{1,0:T(8,128)(2,1)}, u32[]{:S(2)}) copy-start(bf16[128,2048]{1,0:T(8,128)(2,1)} %get-tuple-element.87.ft_hbm.ft_ref) | copy-start | bytes 1572868
  100.6 22.6 %copy-start.3 = (f32[2,64,256]{2,1,0:T(8,128)S(1)}, f32[2,64,256]{2,1,0:T(8,128)}, u32[]{:S(2)}) copy-start(f32[2,64,256]{2,1,0:T(8,128)} %refs_5_.1) | copy-start | bytes 393220
  100.6 22.6 %copy-start.5 = (f32[2,25,256]{2,0,1:T(2,128)S(1)}, f32[2,25,256]{2,0,1:T(2,128)}, u32[]{:S(2)}) copy-start(f32[2,25,256]{2,0,1:T(2,128)} %param.26) | copy-start | bytes 153604
  100.6 22.6 %copy-start.6 = (f32[2,64,47]{1,0,2:T(2,128)S(1)}, f32[2,64,47]{1,0,2:T(2,128)}, u32[]{:S(2)}) copy-start(f32[2,64,47]{1,0,2:T(2,128)} %param.28) | copy-start | bytes 72196
  100.6 22.6 %copy-start.8 = (f32[2,64,256]{2,1,0:T(8,128)S(1)}, f32[2,64,256]{2,1,0:T(8,128)}, u32[]{:S(2)}) copy-start(f32[2,64,256]{2,1,0:T(8,128)} %refs_9_.1) | copy-start | bytes 393220
  100.7 22.6 %copy-start.9 = (f32[2,64,256]{2,1,0:T(8,128)S(1)}, f32[2,64,256]{2,1,0:T(8,128)}, u32[]{:S(2)}) copy-start(f32[2,64,256]{2,1,0:T(8,128)} %refs_13_.1) | copy-start | bytes 393220
  100.7 22.6 %copy-start.10 = (f32[2,25,256]{2,0,1:T(2,128)S(1)}, f32[2,25,256]{2,0,1:T(2,128)}, u32[]{:S(2)}) copy-start(f32[2,25,256]{2,0,1:T(2,128)} %param.30) | copy-start | bytes 153604
  100.7 22.6 %copy-start.11 = (f32[2,25,256]{2,0,1:T(2,128)S(1)}, f32[2,25,256]{2,0,1:T(2,128)}, u32[]{:S(2)}) copy-start(f32[2,25,256]{2,0,1:T(2,128)} %param.34) | copy-start | bytes 153604
  100.7 22.6 %copy-start.12 = (f32[2,64,47]{1,0,2:T(2,128)S(1)}, f32[2,64,47]{1,0,2:T(2,128)}, u32[]{:S(2)}) copy-start(f32[2,64,47]{1,0,2:T(2,128)} %param.32) | copy-start | bytes 72196
  100.7 22.6 %copy-start.13 = (f32[2,64,47]{1,0,2:T(2,128)S(1)}, f32[2,64,47]{1,0,2:T(2,128)}, u32[]{:S(2)}) copy-start(f32[2,64,47]{1,0,2:T(2,128)} %param.36) | copy-start | bytes 72196
  100.7 22.6 %copy-start.16 = (f32[2,2,64]{2,1,0:T(2,128)S(1)}, f32[2,2,64]{2,1,0:T(2,128)}, u32[]{:S(2)}) copy-start(f32[2,2,64]{2,1,0:T(2,128)} %refs_7_.1) | copy-start | bytes 3076
  100.7 22.6 %copy-start.17 = (f32[2,2,64]{2,1,0:T(2,128)S(1)}, f32[2,2,64]{2,1,0:T(2,128)}, u32[]{:S(2)}) copy-start(f32[2,2,64]{2,1,0:T(2,128)} %refs_11_.1) | copy-start | bytes 3076
  100.7 22.6 %copy-start.18 = (f32[2,2,64]{2,1,0:T(2,128)S(1)}, f32[2,2,64]{2,1,0:T(2,128)}, u32[]{:S(2)}) copy-start(f32[2,2,64]{2,1,0:T(2,128)} %refs_15_.1) | copy-start | bytes 3076
  119.5 3.1 %collective-permute-start.5 = (f32[8,128]{1,0:T(8,128)S(1)}, f32[8,128]{1,0:T(8,128)S(1)}, u32[]{:S(2)}, u32[]{:S(2)}) collective-permute-start(f32[8,128]{1,0:T(8,128)S(1)} %get-tuple-element.125.sq0_ref), channel_id=1, source_target_pairs={{0,3},{1,2},{2,1},{3,0},{4,7},{5,6},{6,5},{7,4},{8,11},{9,10},{10,... | collective-permute-start | bytes 12296 | tf_op jit(solution)/shard_map/ppermute | solution.py:752
  119.5 3.7 %collective-permute-start.4 = (f32[8,128]{1,0:T(8,128)S(1)}, f32[8,128]{1,0:T(8,128)S(1)}, u32[]{:S(2)}, u32[]{:S(2)}) collective-permute-start(f32[8,128]{1,0:T(8,128)S(1)} %get-tuple-element.125.sq0_ref), channel_id=1, source_target_pairs={{0,2},{1,3},{2,0},{3,1},{4,6},{5,7},{6,4},{7,5},{8,10},{9,11},{10,... | collective-permute-start | bytes 12296 | tf_op jit(solution)/shard_map/ppermute | solution.py:752
  121.1 2.1 %collective-permute-start.3 = (f32[8,128]{1,0:T(8,128)S(1)}, f32[8,128]{1,0:T(8,128)S(1)}, u32[]{:S(2)}, u32[]{:S(2)}) collective-permute-start(f32[8,128]{1,0:T(8,128)S(1)} %get-tuple-element.125.sq0_ref), channel_id=1, source_target_pairs={{0,1},{1,0},{2,3},{3,2},{4,5},{5,4},{6,7},{7,6},{8,9},{9,8},{10,11... | collective-permute-start | bytes 12296 | tf_op jit(solution)/shard_map/ppermute | solution.py:752

commit v5 on v4

--- a/solution.py
+++ b/solution.py
@@ -25,7 +25,6 @@
 LANE = 128
 FEAT_PAD = 32
 MIB = 1 << 20
-CONVERT_TILE = 256
 
 VMEM = pl.BlockSpec(memory_space=pltpu.VMEM)
 SMEM = pl.BlockSpec(memory_space=pltpu.SMEM)
@@ -239,7 +238,7 @@
     h_ref[s, :] = hidden.astype(BF)
 
 
-GATHER_PARTS = 2
+GATHER_ROWS = 512
 
 
 def start_all(copies):
@@ -308,8 +307,8 @@
     wait_all(small[2:])
 
     def gather(step, _):
-        for part in range(GATHER_PARTS):
-            chunk = step * GATHER_PARTS + part
+        for part in range(GATHER_ROWS // tile):
+            chunk = step * (GATHER_ROWS // tile) + part
             slot = lax.rem(chunk, ring)
             fetch(chunk, slot).wait()
             adj_ref[rows_of(chunk, tile), :] = adj_buf[slot].astype(F32).astype(BF)
@@ -318,7 +317,7 @@
             def _():
                 fetch(chunk + ring, slot).start()
 
-        s = rows_of(step, GATHER_PARTS * tile)
+        s = rows_of(step, GATHER_ROWS)
         far = dot_nn(edge_ref[s, :], halo_ref[...])
         row_ref[s, :] = jnp.broadcast_to(far[:, LANE - 1 : LANE], far.shape)
         summed = dot_nt(adj_ref[s, :], ft_ref[...]) + far
@@ -327,7 +326,7 @@
         mean_ref[s, :] = (summed * inv_deg).astype(BF)
         return 0
 
-    lax.fori_loop(0, nodes // (GATHER_PARTS * tile), gather, 0)
+    lax.fori_loop(0, nodes // GATHER_ROWS, gather, 0)
 
     def apply(s, _):
         joined = dot_tn(ft_ref[:, s], win_ref[0]) + dot_nn(mean_ref[s, :], win_ref[1])
@@ -696,15 +695,15 @@
         + [pltpu.SemaphoreType.DMA((2,)), pltpu.SemaphoreType.DMA((5,))],
     )
     loads = in_hbm(inner_adj, bound_adj, keep_slots, send_index, ft, win, norms)
-    ring, bound_ring = (4, 8) if parts <= 16 else (2, 2)
+    tile, ring, bound_ring = (512, 3, 4) if parts <= 16 else (256, 2, 2)
     adj, edge, row_deg, sel, mean_one, xhat_one, slope_one, istd_one, h_one, inv_deg, send = run(
         functools.partial(first_kernel, width=width),
         [bf(nodes, nodes), bf(nodes, halo), shape(nodes, LANE), bf(halo, nodes), bf(nodes, LANE),
          shape(nodes, HID), shape(nodes, HID), shape(nodes, LANE), bf(nodes, HID), shape(nodes, LANE), bf(halo, HID)],
-        *loads, recv, hbm_in=range(7),
+        *loads, recv, hbm_in=range(7), mib=24 if parts <= 16 else 52,
         scratch=[pltpu.VMEM((halo, LANE), BF), pltpu.VMEM(keep_slots.shape, jnp.int32), pltpu.VMEM(send_index.shape, jnp.int32)]
         + [pltpu.VMEM(a.shape, a.dtype) for a in loads[4:]]
-        + [pltpu.VMEM((ring, CONVERT_TILE, nodes), jnp.int32), pltpu.VMEM((bound_ring, CONVERT_TILE, halo), jnp.int32),
+        + [pltpu.VMEM((ring, tile, nodes), jnp.int32), pltpu.VMEM((bound_ring, tile, halo), jnp.int32),
            pltpu.SemaphoreType.DMA((2, max(ring, bound_ring))), pltpu.SemaphoreType.DMA((5,))],
     )
     halo_one = exchange(send, parts).reshape(halo, HID)

time: 125 us -> 124 us (level)
  Pallas kernels: 44 us -> 42.7 us
    pallas_call x11, Pallas kernels: 44 us -> 42.7 us  [call(): pl.pallas_call(kernel, out_shape=outs, in_specs=[SMEM if i in smem_in els...]
where the time goes in v5:
time: 124 us
  blocking collectives  63.8 us (51%)
  Pallas kernels  42.7 us (34%)
  starting transfers between devices  10.2 us (8%)
  waiting for transfers between devices  6.05 us (5%)
    all_to_all x6, blocking collectives, exchange(): lax.all_to_all(x.reshape(parts, -1, x.shape[-1]), 'dom', split_axis=0, co...  63.8 us
    pallas_call x11, Pallas kernels, call(): pl.pallas_call(kernel, out_shape=outs, in_specs=[SMEM if i in smem_in els...  42.7 us
    all_to_all x1, starting transfers between devices, shards(): lax.all_to_all(send.reshape(parts * feats, each // 2, LANE), ('dom', 'fea...  4.92 us
    ppermute x1, starting transfers between devices, shards(): chip = lax.ppermute(own, 'feat', [(s, s ^ 2) for s in range(feats)])  3 us
    all_to_all x1, waiting for transfers between devices, shards(): lax.all_to_all(send.reshape(parts * feats, each // 2, LANE), ('dom', 'fea...  2.76 us
  transfers between devices with their start and end apart: 7, of which 6 were waited for; matrix products, arithmetic and copies ran while one was open for 0% of the time, Pallas kernels for 3%

profile of v5, /device:TPU:0, one launch (start us, length us, event | category | flops | bytes accessed | tf_op | source)
XLA Modules:
  0.0 123.9 jit_solution(13454244895818584218)
XLA Ops:
  0.7 2.6 %shard_map.322 = (bf16[8,4,16,128]{3,2,1,0:T(8,128)(2,1)}, bf16[480,256]{1,0:T(8,128)(2,1)S(1)}, s32[1]{0:T(128)}) custom-call(s32[1,8,32]{2,1,0:T(8,128)} %idx_hbm.3, f32[25,2048]{1,0:T(8,128)} %bitcast.51, f32[25,2,256]{2,1,0:T(2,128)} %bitcast.36, f32[2,64,256]{2,1,0:T(8,128)} %refs_5_.1, f32[47,2,64]{2,1,0:T(2,128)} %bitcast.38, f32[2,2,64]{2,1,0:T(2,128)} %refs_7_.1, ...), custom_call_target="tpu_custom_call" | custom-call | bytes 197506 | tf_op jit(solution)/shard_map/pallas_call | solution.py:79
  3.2 0.0 copy-start.4
  3.2 3.0 %collective-permute-start = (bf16[480,256]{1,0:T(8,128)(2,1)S(1)}, bf16[480,256]{1,0:T(8,128)(2,1)S(1)}, u32[]{:S(2)}, u32[]{:S(2)}) collective-permute-start(bf16[480,256]{1,0:T(8,128)(2,1)S(1)} %get-tuple-element.85.own_hbm), channel_id=1, source_target_pairs={{0,2},{1,3},{2,0},{3,1},{4,6},{5,7},{6,4},{7,5},{8,10},{9,11},{10,... | collective-permute-start | bytes 737288 | tf_op jit(solution)/shard_map/ppermute | solution.py:687
  6.2 4.9 %all-to-all-start = ((bf16[32,16,128]{2,1,0:T(8,128)(2,1)}), bf16[32,16,128]{2,1,0:T(8,128)(2,1)S(1)}, u32[]{:S(2)}, u32[]{:S(2)}) async-start(bf16[32,16,128]{2,1,0:T(8,128)(2,1)} %bitcast.4), calls=%async_computation | async-start | bytes 262144 | tf_op jit(solution)/shard_map/all_to_all | solution.py:684
  11.2 0.3 collective-permute-start.1
  11.5 0.7 collective-permute-done.chip_hbm
  12.2 0.0 collective-permute-start.2
  12.2 0.5 collective-permute-done.1.core_ref
  12.8 1.0 collective-permute-done.2.far_ref
  13.7 0.0 copy-done.4
  13.7 0.0 copy-done.19
  13.7 2.9 %shard_map.323 = (bf16[128,2048]{1,0:T(8,128)(2,1)}, bf16[2,128,256]{2,1,0:T(8,128)(2,1)}, bf16[2,256,256]{2,1,0:T(8,128)(2,1)}, bf16[2,128,256]{2,1,0:T(8,128)(2,1)}, f32[8,256]{1,0:T(8,128)}) custom-call(bf16[480,256]{1,0:T(8,128)(2,1)} %copy-done.4, bf16[480,256]{1,0:T(8,128)(2,1)} %copy-done.19, bf16[480,256]{1,0:T(8,128)(2,1)S(1)} %collective-permute-done.1.core_ref, ...), custom_call_target="tpu_custom_call" | custom-call | bytes 509953 | tf_op jit(solution)/shard_map/pallas_call | solution.py:79
  16.6 2.8 %all-to-all-done = bf16[32,16,128]{2,1,0:T(8,128)(2,1)S(1)} async-done(((bf16[32,16,128]{2,1,0:T(8,128)(2,1)}), bf16[32,16,128]{2,1,0:T(8,128)(2,1)S(1)}, u32[]{:S(2)}, u32[]{:S(2)}) %all-to-all-start) | async-done | bytes 131104 | tf_op jit(solution)/shard_map/all_to_all | solution.py:684
  19.4 10.2 %shard_map.324 = (bf16[2048,2048]{1,0:T(8,128)(2,1)S(1)}, bf16[2048,256]{1,0:T(8,128)(2,1)S(1)}, f32[2048,128]{1,0:T(8,128)S(1)}, bf16[256,2048]{1,0:T(8,128)(2,...) custom-call(s32[2048,2048]{1,0:T(8,128)} %adj_hbm.1, ...), custom_call_target="tpu_custom_call" | custom-call | bytes 9800192 | tf_op jit(solution)/shard_map/pallas_call | solution.py:79
  29.7 11.3 %all_to_all.35 = bf16[8,32,256]{2,1,0:T(8,128)(2,1)S(1)} all-to-all(bf16[8,32,256]{2,1,0:T(8,128)(2,1)S(1)} %bitcast.40), channel_id=1, replica_groups=mesh['dom'=8,'feat'=4] {'dom'}, dimensions={0} | all-to-all | bytes 262144 | tf_op jit(solution)/shard_map/all_to_all | solution.py:623
  41.0 0.0 copy-done
  41.0 0.0 copy-done.7
  41.0 4.8 %shard_map.325 = (bf16[2048,256]{1,0:T(8,128)(2,1)S(1)}, f32[2048,256]{1,0:T(8,128)S(1)}, f32[2048,256]{1,0:T(8,128)S(1)}, f32[2048,128]{1,0:T(8,128)S(1)}, bf16...) custom-call(bf16[2048,2048]{1,0:T(8,128)(2,1)S(1)} %get-tuple-element.91.adj_ref, ...), custom_call_target="tpu_custom_call" | custom-call | bytes 5113856 | tf_op jit(solution)/shard_map/pallas_call | solution.py:79
  45.8 9.8 %all_to_all.36 = bf16[8,32,256]{2,1,0:T(8,128)(2,1)S(1)} all-to-all(bf16[8,32,256]{2,1,0:T(8,128)(2,1)S(1)} %bitcast.42), channel_id=1, replica_groups=mesh['dom'=8,'feat'=4] {'dom'}, dimensions={0} | all-to-all | bytes 262144 | tf_op jit(solution)/shard_map/all_to_all | solution.py:623
  55.6 4.3 %shard_map.326 = (bf16[2048,256]{1,0:T(8,128)(2,1)S(1)}, f32[2048,128]{1,0:T(8,128)S(1)}, bf16[2048,128]{1,0:T(8,128)(2,1)S(1)}, f32[256,128]{1,0:T(8,128)S(1)},...) custom-call(bf16[2048,2048]{1,0:T(8,128)(2,1)S(1)} %get-tuple-element.91.adj_ref, ...), custom_call_target="tpu_custom_call" | custom-call | bytes 3966976 | tf_op jit(solution)/shard_map/pallas_call | solution.py:79
  60.0 9.7 %all_to_all.37 = bf16[8,32,256]{2,1,0:T(8,128)(2,1)S(1)} all-to-all(bf16[8,32,256]{2,1,0:T(8,128)(2,1)S(1)} %bitcast.43), channel_id=1, replica_groups=mesh['dom'=8,'feat'=4] {'dom'}, dimensions={0} | all-to-all | bytes 262144 | tf_op jit(solution)/shard_map/all_to_all | solution.py:623
  69.7 0.0 copy-done.15
  69.7 3.2 %shard_map.327 = (bf16[2048,128]{1,0:T(8,128)(2,1)S(1)}, bf16[2048,256]{1,0:T(8,128)(2,1)S(1)}, bf16[256,256]{1,0:T(8,128)(2,1)S(1)}, f32[8,128]{1,0:T(8,128)S(1)}) custom-call(f32[2048,128]{1,0:T(8,128)S(1)} %get-tuple-element.101.logit_ref, s32[16,128]{1,0:T(8,128)S(1)} %bitcast.50, s32[16,128]{1,0:T(8,128)S(1)} %bitcast.49, ...), custom_call_target="tpu_custom_call" | custom-call | bytes 2003968 | tf_op jit(solution)/shard_map/pallas_call | solution.py:79
  72.9 9.7 %all_to_all.38 = bf16[8,32,256]{2,1,0:T(8,128)(2,1)S(1)} all-to-all(bf16[8,32,256]{2,1,0:T(8,128)(2,1)S(1)} %bitcast.41), channel_id=1, replica_groups=mesh['dom'=8,'feat'=4] {'dom'}, dimensions={0} | all-to-all | bytes 262144 | tf_op jit(solution)/shard_map/all_to_all | solution.py:623
  82.7 6.8 %shard_map.328 = (bf16[2048,256]{1,0:T(8,128)(2,1)S(1)}, bf16[2048,256]{1,0:T(8,128)(2,1)S(1)}, bf16[8,64,256]{2,1,0:T(8,128)(2,1)S(1)}, f32[8,256]{1,0:T(8,128)S(1)}) custom-call(bf16[2048,2048]{1,0:T(8,128)(2,1)S(1)} %get-tuple-element.91.adj_ref, bf16[2048,256]{1,0:T(8,128)(2,1)S(1)} %get-tuple-element.107.gsin_ref, ...), custom_call_target="tpu_custom_call" | custom-call | bytes 6361089 | tf_op jit(solution)/shard_map/pallas_call | solution.py:79
  89.4 10.6 %all_to_all.39.recv_ref = bf16[8,64,256]{2,1,0:T(8,128)(2,1)S(1)} all-to-all(bf16[8,64,256]{2,1,0:T(8,128)(2,1)S(1)} %get-tuple-element.117), channel_id=1, replica_groups=mesh['dom'=8,'feat'=4] {'dom'}, dimensions={0} | all-to-all | bytes 524288 | tf_op jit(solution)/shard_map/all_to_all | solution.py:623
  100.1 0.0 copy-done.1
  100.1 0.0 copy-start.8
  100.1 0.0 copy-start.9
  100.1 0.0 copy-start.10
  100.1 0.0 copy-start.11
  100.1 0.0 copy-start.12
  100.2 0.0 copy-start.13
  100.2 0.0 copy-start.16
  100.2 0.0 copy-start.17
  100.2 0.0 copy-start.18
  100.2 5.5 %shard_map.329 = bf16[8,112,256]{2,1,0:T(8,128)(2,1)S(1)} custom-call(bf16[2048,2048]{1,0:T(8,128)(2,1)S(1)} %get-tuple-element.91.adj_ref, bf16[2048,256]{1,0:T(8,128)(2,1)S(1)} %get-tuple-element.115.gsin_ref, bf16[2048,256]{1,0:T(8,128)(2,1)S(1)} %get-tuple-element.116.grad_ref, bf16[2,256,256]{2,1,0:T(8,128)(2,1)S(1)} %copy-done, ...), custom_call_target="tpu_custom_call" | custom-call | bytes 4707329 | tf_op jit(solution)/shard_map/pallas_call | solution.py:79
  105.7 12.6 %all_to_all.40.recv_ref = bf16[8,112,256]{2,1,0:T(8,128)(2,1)S(1)} all-to-all(bf16[8,112,256]{2,1,0:T(8,128)(2,1)S(1)} %shard_map.329), channel_id=1, replica_groups=mesh['dom'=8,'feat'=4] {'dom'}, dimensions={0} | all-to-all | bytes 917504 | tf_op jit(solution)/shard_map/all_to_all | solution.py:623
  118.3 0.2 shard_map.330
  118.5 0.1 collective-permute-start.5
  118.6 1.6 %collective-permute-start.4 = (f32[8,128]{1,0:T(8,128)S(1)}, f32[8,128]{1,0:T(8,128)S(1)}, u32[]{:S(2)}, u32[]{:S(2)}) collective-permute-start(f32[8,128]{1,0:T(8,128)S(1)} %get-tuple-element.125.sq0_ref), channel_id=1, source_target_pairs={{0,2},{1,3},{2,0},{3,1},{4,6},{5,7},{6,4},{7,5},{8,10},{9,11},{10,... | collective-permute-start | bytes 12296 | tf_op jit(solution)/shard_map/ppermute | solution.py:751
  120.2 0.2 collective-permute-start.3
  120.4 0.7 shard_map.331
  121.2 0.4 collective-permute-done.5.sq3_ref
  121.6 0.7 collective-permute-done.4.sq2_ref
  122.2 0.0 collective-permute-done.3.sq1_ref
  122.3 0.0 copy-done.5
  122.4 1.4 %shard_map.332 = (f32[1,1]{1,0:T(1,128)}, f32[1,1]{1,0:T(1,128)}, f32[1,1]{1,0:T(1,128)}, f32[25,2,256]{2,1,0:T(2,128)}, f32[2,64,256]{2,1,0:T(8,128)}, /*index=...) custom-call(f32[8,128]{1,0:T(8,128)S(1)} %get-tuple-element.124.tota, ...), custom_call_target="tpu_custom_call" | custom-call | bytes 394819 | tf_op jit(solution)/shard_map/pallas_call | solution.py:79
  (23 shorter events, 0.0 us)
Async XLA Ops:
  3.2 10.5 %copy-start.4 = (bf16[480,256]{1,0:T(8,128)(2,1)}, bf16[480,256]{1,0:T(8,128)(2,1)S(1)}, u32[]{:S(2)}) copy-start(bf16[480,256]{1,0:T(8,128)(2,1)S(1)} %get-tuple-element.85.own_hbm) | copy-start | bytes 737284
  3.2 9.0 %collective-permute-start = (bf16[480,256]{1,0:T(8,128)(2,1)S(1)}, bf16[480,256]{1,0:T(8,128)(2,1)S(1)}, u32[]{:S(2)}, u32[]{:S(2)}) collective-permute-start(bf16[480,256]{1,0:T(8,128)(2,1)S(1)} %get-tuple-element.85.own_hbm), channel_id=1, source_target_pairs={{0,2},{1,3},{2,0},{3,1},{4,6},{5,7},{6,4},{7,5},{8,10},{9,11},{10,... | collective-permute-start | bytes 737288 | tf_op jit(solution)/shard_map/ppermute | solution.py:687
  6.2 13.2 %all-to-all-start = ((bf16[32,16,128]{2,1,0:T(8,128)(2,1)}), bf16[32,16,128]{2,1,0:T(8,128)(2,1)S(1)}, u32[]{:S(2)}, u32[]{:S(2)}) async-start(bf16[32,16,128]{2,1,0:T(8,128)(2,1)} %bitcast.4), calls=%async_computation | async-start | bytes 262144 | tf_op jit(solution)/shard_map/all_to_all | solution.py:684
  11.2 1.6 %collective-permute-start.1 = (bf16[480,256]{1,0:T(8,128)(2,1)S(1)}, bf16[480,256]{1,0:T(8,128)(2,1)S(1)}, u32[]{:S(2)}, u32[]{:S(2)}) collective-permute-start(bf16[480,256]{1,0:T(8,128)(2,1)S(1)} %get-tuple-element.85.own_hbm), channel_id=1, source_target_pairs={{0,1},{1,0},{2,3},{3,2},{4,5},{5,4},{6,7},{7,6},{8,9},{9,8},{10,11... | collective-permute-start | bytes 737288 | tf_op jit(solution)/shard_map/ppermute | solution.py:688
  12.2 1.5 %copy-start.19 = (bf16[480,256]{1,0:T(8,128)(2,1)}, bf16[480,256]{1,0:T(8,128)(2,1)S(1)}, u32[]{:S(2)}) copy-start(bf16[480,256]{1,0:T(8,128)(2,1)S(1)} %collective-permute-done.chip_hbm) | copy-start | bytes 737284
  12.2 1.5 %collective-permute-start.2 = (bf16[480,256]{1,0:T(8,128)(2,1)S(1)}, bf16[480,256]{1,0:T(8,128)(2,1)S(1)}, u32[]{:S(2)}, u32[]{:S(2)}) collective-permute-start(bf16[480,256]{1,0:T(8,128)(2,1)S(1)} %collective-permute-done.chip_hbm), channel_id=1, source_target_pairs={{0,1},{1,0},{2,3},{3,2},{4,5},{5,4},{6,7},{7,6},{8,9},{9,8},{10,11... | collective-permute-start | bytes 737288 | tf_op jit(solution)/shard_map/ppermute | solution.py:689
  19.4 21.6 %copy-start = (bf16[2,256,256]{2,1,0:T(8,128)(2,1)S(1)}, bf16[2,256,256]{2,1,0:T(8,128)(2,1)}, u32[]{:S(2)}) copy-start(bf16[2,256,256]{2,1,0:T(8,128)(2,1)} %get-tuple-element.95.w_ref) | copy-start | bytes 786436
  19.4 21.6 %copy-start.7 = (f32[8,256]{1,0:T(8,128)S(1)}, f32[8,256]{1,0:T(8,128)}, u32[]{:S(2)}) copy-start(f32[8,256]{1,0:T(8,128)} %get-tuple-element.89.norm_hbm.norm_ref) | copy-start | bytes 24580
  41.0 14.6 %copy-start.2 = (bf16[2,128,256]{2,1,0:T(8,128)(2,1)S(1)}, bf16[2,128,256]{2,1,0:T(8,128)(2,1)}, u32[]{:S(2)}) copy-start(bf16[2,128,256]{2,1,0:T(8,128)(2,1)} %get-tuple-element.100.w_ref.wout_ref) | copy-start | bytes 393220
  41.0 14.6 %copy-start.14 = (s32[2048]{0:T(1024)S(1)}, s32[2048]{0:T(1024)}, u32[]{:S(2)}) copy-start(s32[2048]{0:T(1024)} %param.25) | copy-start | bytes 24580
  55.6 14.1 %copy-start.15 = (s32[2048]{0:T(1024)S(1)}, s32[2048]{0:T(1024)}, u32[]{:S(2)}) copy-start(s32[2048]{0:T(1024)} %param.24) | copy-start | bytes 24580
  82.7 17.4 %copy-start.1 = (bf16[128,2048]{1,0:T(8,128)(2,1)S(1)}, bf16[128,2048]{1,0:T(8,128)(2,1)}, u32[]{:S(2)}) copy-start(bf16[128,2048]{1,0:T(8,128)(2,1)} %get-tuple-element.87.ft_hbm.ft_ref) | copy-start | bytes 1572868
  100.1 22.2 %copy-start.3 = (f32[2,64,256]{2,1,0:T(8,128)S(1)}, f32[2,64,256]{2,1,0:T(8,128)}, u32[]{:S(2)}) copy-start(f32[2,64,256]{2,1,0:T(8,128)} %refs_5_.1) | copy-start | bytes 393220
  100.1 22.2 %copy-start.5 = (f32[2,25,256]{2,0,1:T(2,128)S(1)}, f32[2,25,256]{2,0,1:T(2,128)}, u32[]{:S(2)}) copy-start(f32[2,25,256]{2,0,1:T(2,128)} %param.26) | copy-start | bytes 153604
  100.1 22.2 %copy-start.6 = (f32[2,64,47]{1,0,2:T(2,128)S(1)}, f32[2,64,47]{1,0,2:T(2,128)}, u32[]{:S(2)}) copy-start(f32[2,64,47]{1,0,2:T(2,128)} %param.28) | copy-start | bytes 72196
  100.1 22.2 %copy-start.8 = (f32[2,64,256]{2,1,0:T(8,128)S(1)}, f32[2,64,256]{2,1,0:T(8,128)}, u32[]{:S(2)}) copy-start(f32[2,64,256]{2,1,0:T(8,128)} %refs_9_.1) | copy-start | bytes 393220
  100.1 22.2 %copy-start.9 = (f32[2,64,256]{2,1,0:T(8,128)S(1)}, f32[2,64,256]{2,1,0:T(8,128)}, u32[]{:S(2)}) copy-start(f32[2,64,256]{2,1,0:T(8,128)} %refs_13_.1) | copy-start | bytes 393220
  100.1 22.2 %copy-start.10 = (f32[2,25,256]{2,0,1:T(2,128)S(1)}, f32[2,25,256]{2,0,1:T(2,128)}, u32[]{:S(2)}) copy-start(f32[2,25,256]{2,0,1:T(2,128)} %param.30) | copy-start | bytes 153604
  100.1 22.2 %copy-start.11 = (f32[2,25,256]{2,0,1:T(2,128)S(1)}, f32[2,25,256]{2,0,1:T(2,128)}, u32[]{:S(2)}) copy-start(f32[2,25,256]{2,0,1:T(2,128)} %param.34) | copy-start | bytes 153604
  100.1 22.2 %copy-start.12 = (f32[2,64,47]{1,0,2:T(2,128)S(1)}, f32[2,64,47]{1,0,2:T(2,128)}, u32[]{:S(2)}) copy-start(f32[2,64,47]{1,0,2:T(2,128)} %param.32) | copy-start | bytes 72196
  100.2 22.2 %copy-start.13 = (f32[2,64,47]{1,0,2:T(2,128)S(1)}, f32[2,64,47]{1,0,2:T(2,128)}, u32[]{:S(2)}) copy-start(f32[2,64,47]{1,0,2:T(2,128)} %param.36) | copy-start | bytes 72196
  100.2 22.2 %copy-start.16 = (f32[2,2,64]{2,1,0:T(2,128)S(1)}, f32[2,2,64]{2,1,0:T(2,128)}, u32[]{:S(2)}) copy-start(f32[2,2,64]{2,1,0:T(2,128)} %refs_7_.1) | copy-start | bytes 3076
  100.2 22.2 %copy-start.17 = (f32[2,2,64]{2,1,0:T(2,128)S(1)}, f32[2,2,64]{2,1,0:T(2,128)}, u32[]{:S(2)}) copy-start(f32[2,2,64]{2,1,0:T(2,128)} %refs_11_.1) | copy-start | bytes 3076
  100.2 22.2 %copy-start.18 = (f32[2,2,64]{2,1,0:T(2,128)S(1)}, f32[2,2,64]{2,1,0:T(2,128)}, u32[]{:S(2)}) copy-start(f32[2,2,64]{2,1,0:T(2,128)} %refs_15_.1) | copy-start | bytes 3076
  118.5 3.1 %collective-permute-start.5 = (f32[8,128]{1,0:T(8,128)S(1)}, f32[8,128]{1,0:T(8,128)S(1)}, u32[]{:S(2)}, u32[]{:S(2)}) collective-permute-start(f32[8,128]{1,0:T(8,128)S(1)} %get-tuple-element.125.sq0_ref), channel_id=1, source_target_pairs={{0,3},{1,2},{2,1},{3,0},{4,7},{5,6},{6,5},{7,4},{8,11},{9,10},{10,... | collective-permute-start | bytes 12296 | tf_op jit(solution)/shard_map/ppermute | solution.py:751
  118.6 3.7 %collective-permute-start.4 = (f32[8,128]{1,0:T(8,128)S(1)}, f32[8,128]{1,0:T(8,128)S(1)}, u32[]{:S(2)}, u32[]{:S(2)}) collective-permute-start(f32[8,128]{1,0:T(8,128)S(1)} %get-tuple-element.125.sq0_ref), channel_id=1, source_target_pairs={{0,2},{1,3},{2,0},{3,1},{4,6},{5,7},{6,4},{7,5},{8,10},{9,11},{10,... | collective-permute-start | bytes 12296 | tf_op jit(solution)/shard_map/ppermute | solution.py:751
  120.2 2.1 %collective-permute-start.3 = (f32[8,128]{1,0:T(8,128)S(1)}, f32[8,128]{1,0:T(8,128)S(1)}, u32[]{:S(2)}, u32[]{:S(2)}) collective-permute-start(f32[8,128]{1,0:T(8,128)S(1)} %get-tuple-element.125.sq0_ref), channel_id=1, source_target_pairs={{0,1},{1,0},{2,3},{3,2},{4,5},{5,4},{6,7},{7,6},{8,9},{9,8},{10,11... | collective-permute-start | bytes 12296 | tf_op jit(solution)/shard_map/ppermute | solution.py:751

commit v6 on v5

--- a/solution.py
+++ b/solution.py
@@ -212,7 +212,7 @@
     norm_ref[...] = pltpu.roll(norms, 8 - (NORM_AT - 24), 0)
 
 
-TILE = 1024
+TILE = 2048
 
 
 def loop(count, tile, body, carry=0):
@@ -343,7 +343,7 @@
         mean_ref[s, :] = (summed * both(invd_ref[s, :])).astype(BF)
         return 0
 
-    loop(adj_ref.shape[0], 2 * TILE, gather)
+    loop(adj_ref.shape[0], TILE, gather)
 
 
 def second_kernel(adj_ref, edge_ref, halo_ref, hin_ref, w_ref, norm_ref, invd_ref, sel_ref,

time: 124 us -> 125 us (level)
  no operation moved by 1% of the time
where the time goes in v6:
time: 125 us; the launch traced here: 124 us
  blocking collectives  63.8 us (51%)
  Pallas kernels  43.2 us (35%)
  starting transfers between devices  10.2 us (8%)
  waiting for transfers between devices  6.05 us (5%)
    all_to_all x6, blocking collectives, exchange(): lax.all_to_all(x.reshape(parts, -1, x.shape[-1]), 'dom', split_axis=0, co...  63.8 us
    pallas_call x11, Pallas kernels, call(): pl.pallas_call(kernel, out_shape=outs, in_specs=[SMEM if i in smem_in els...  43.2 us
    all_to_all x1, starting transfers between devices, shards(): lax.all_to_all(send.reshape(parts * feats, each // 2, LANE), ('dom', 'fea...  4.92 us
    ppermute x1, starting transfers between devices, shards(): chip = lax.ppermute(own, 'feat', [(s, s ^ 2) for s in range(feats)])  3 us
    all_to_all x1, waiting for transfers between devices, shards(): lax.all_to_all(send.reshape(parts * feats, each // 2, LANE), ('dom', 'fea...  2.76 us
  transfers between devices with their start and end apart: 7, of which 6 were waited for; matrix products, arithmetic and copies ran while one was open for 0% of the time, Pallas kernels for 3%

profile of v6, /device:TPU:0, one launch (start us, length us, event | category | flops | bytes accessed | tf_op | source)
XLA Modules:
  0.0 124.4 jit_solution(3191434666600456520)
XLA Ops:
  0.7 2.6 %shard_map.322 = (bf16[8,4,16,128]{3,2,1,0:T(8,128)(2,1)}, bf16[480,256]{1,0:T(8,128)(2,1)S(1)}, s32[1]{0:T(128)}) custom-call(s32[1,8,32]{2,1,0:T(8,128)} %idx_hbm.3, f32[25,2048]{1,0:T(8,128)} %bitcast.51, f32[25,2,256]{2,1,0:T(2,128)} %bitcast.36, f32[2,64,256]{2,1,0:T(8,128)} %refs_5_.1, f32[47,2,64]{2,1,0:T(2,128)} %bitcast.38, f32[2,2,64]{2,1,0:T(2,128)} %refs_7_.1, ...), custom_call_target="tpu_custom_call" | custom-call | bytes 197506 | tf_op jit(solution)/shard_map/pallas_call | solution.py:79
  3.2 3.0 %collective-permute-start = (bf16[480,256]{1,0:T(8,128)(2,1)S(1)}, bf16[480,256]{1,0:T(8,128)(2,1)S(1)}, u32[]{:S(2)}, u32[]{:S(2)}) collective-permute-start(bf16[480,256]{1,0:T(8,128)(2,1)S(1)} %get-tuple-element.85.own_hbm), channel_id=1, source_target_pairs={{0,2},{1,3},{2,0},{3,1},{4,6},{5,7},{6,4},{7,5},{8,10},{9,11},{10,... | collective-permute-start | bytes 737288 | tf_op jit(solution)/shard_map/ppermute | solution.py:687
  6.2 4.9 %all-to-all-start = ((bf16[32,16,128]{2,1,0:T(8,128)(2,1)}), bf16[32,16,128]{2,1,0:T(8,128)(2,1)S(1)}, u32[]{:S(2)}, u32[]{:S(2)}) async-start(bf16[32,16,128]{2,1,0:T(8,128)(2,1)} %bitcast.4), calls=%async_computation | async-start | bytes 262144 | tf_op jit(solution)/shard_map/all_to_all | solution.py:684
  11.2 0.3 collective-permute-start.1
  11.5 0.7 collective-permute-done.chip_hbm
  12.2 0.0 collective-permute-start.2
  12.2 0.5 collective-permute-done.1.core_ref
  12.8 1.0 collective-permute-done.2.far_ref
  13.7 0.0 copy-done.4
  13.7 2.9 %shard_map.323 = (bf16[128,2048]{1,0:T(8,128)(2,1)}, bf16[2,128,256]{2,1,0:T(8,128)(2,1)}, bf16[2,256,256]{2,1,0:T(8,128)(2,1)}, bf16[2,128,256]{2,1,0:T(8,128)(2,1)}, f32[8,256]{1,0:T(8,128)}) custom-call(bf16[480,256]{1,0:T(8,128)(2,1)} %copy-done.4, bf16[480,256]{1,0:T(8,128)(2,1)} %copy-done.19, bf16[480,256]{1,0:T(8,128)(2,1)S(1)} %collective-permute-done.1.core_ref, ...), custom_call_target="tpu_custom_call" | custom-call | bytes 509953 | tf_op jit(solution)/shard_map/pallas_call | solution.py:79
  16.6 2.8 %all-to-all-done = bf16[32,16,128]{2,1,0:T(8,128)(2,1)S(1)} async-done(((bf16[32,16,128]{2,1,0:T(8,128)(2,1)}), bf16[32,16,128]{2,1,0:T(8,128)(2,1)S(1)}, u32[]{:S(2)}, u32[]{:S(2)}) %all-to-all-start) | async-done | bytes 131104 | tf_op jit(solution)/shard_map/all_to_all | solution.py:684
  19.4 10.0 %shard_map.324 = (bf16[2048,2048]{1,0:T(8,128)(2,1)S(1)}, bf16[2048,256]{1,0:T(8,128)(2,1)S(1)}, f32[2048,128]{1,0:T(8,128)S(1)}, bf16[256,2048]{1,0:T(8,128)(2,...) custom-call(s32[2048,2048]{1,0:T(8,128)} %adj_hbm.1, ...), custom_call_target="tpu_custom_call" | custom-call | bytes 9800192 | tf_op jit(solution)/shard_map/pallas_call | solution.py:79
  29.4 11.3 %all_to_all.35 = bf16[8,32,256]{2,1,0:T(8,128)(2,1)S(1)} all-to-all(bf16[8,32,256]{2,1,0:T(8,128)(2,1)S(1)} %bitcast.40), channel_id=1, replica_groups=mesh['dom'=8,'feat'=4] {'dom'}, dimensions={0} | all-to-all | bytes 262144 | tf_op jit(solution)/shard_map/all_to_all | solution.py:623
  40.8 0.0 copy-done
  40.8 5.3 %shard_map.325 = (bf16[2048,256]{1,0:T(8,128)(2,1)S(1)}, f32[2048,256]{1,0:T(8,128)S(1)}, f32[2048,256]{1,0:T(8,128)S(1)}, f32[2048,128]{1,0:T(8,128)S(1)}, bf16...) custom-call(bf16[2048,2048]{1,0:T(8,128)(2,1)S(1)} %get-tuple-element.91.adj_ref, ...), custom_call_target="tpu_custom_call" | custom-call | bytes 5113856 | tf_op jit(solution)/shard_map/pallas_call | solution.py:79
  46.2 9.8 %all_to_all.36 = bf16[8,32,256]{2,1,0:T(8,128)(2,1)S(1)} all-to-all(bf16[8,32,256]{2,1,0:T(8,128)(2,1)S(1)} %bitcast.42), channel_id=1, replica_groups=mesh['dom'=8,'feat'=4] {'dom'}, dimensions={0} | all-to-all | bytes 262144 | tf_op jit(solution)/shard_map/all_to_all | solution.py:623
  56.0 5.6 %shard_map.326 = (bf16[2048,256]{1,0:T(8,128)(2,1)S(1)}, f32[2048,128]{1,0:T(8,128)S(1)}, bf16[2048,128]{1,0:T(8,128)(2,1)S(1)}, f32[256,128]{1,0:T(8,128)S(1)},...) custom-call(bf16[2048,2048]{1,0:T(8,128)(2,1)S(1)} %get-tuple-element.91.adj_ref, ...), custom_call_target="tpu_custom_call" | custom-call | bytes 3966976 | tf_op jit(solution)/shard_map/pallas_call | solution.py:79
  61.6 9.7 %all_to_all.37 = bf16[8,32,256]{2,1,0:T(8,128)(2,1)S(1)} all-to-all(bf16[8,32,256]{2,1,0:T(8,128)(2,1)S(1)} %bitcast.43), channel_id=1, replica_groups=mesh['dom'=8,'feat'=4] {'dom'}, dimensions={0} | all-to-all | bytes 262144 | tf_op jit(solution)/shard_map/all_to_all | solution.py:623
  71.3 2.9 %shard_map.327 = (bf16[2048,128]{1,0:T(8,128)(2,1)S(1)}, bf16[2048,256]{1,0:T(8,128)(2,1)S(1)}, bf16[256,256]{1,0:T(8,128)(2,1)S(1)}, f32[8,128]{1,0:T(8,128)S(1)}) custom-call(f32[2048,128]{1,0:T(8,128)S(1)} %get-tuple-element.101.logit_ref, s32[16,128]{1,0:T(8,128)S(1)} %bitcast.50, s32[16,128]{1,0:T(8,128)S(1)} %bitcast.49, ...), custom_call_target="tpu_custom_call" | custom-call | bytes 2003968 | tf_op jit(solution)/shard_map/pallas_call | solution.py:79
  74.2 9.7 %all_to_all.38 = bf16[8,32,256]{2,1,0:T(8,128)(2,1)S(1)} all-to-all(bf16[8,32,256]{2,1,0:T(8,128)(2,1)S(1)} %bitcast.41), channel_id=1, replica_groups=mesh['dom'=8,'feat'=4] {'dom'}, dimensions={0} | all-to-all | bytes 262144 | tf_op jit(solution)/shard_map/all_to_all | solution.py:623
  83.9 6.2 %shard_map.328 = (bf16[2048,256]{1,0:T(8,128)(2,1)S(1)}, bf16[2048,256]{1,0:T(8,128)(2,1)S(1)}, bf16[8,64,256]{2,1,0:T(8,128)(2,1)S(1)}, f32[8,256]{1,0:T(8,128)S(1)}) custom-call(bf16[2048,2048]{1,0:T(8,128)(2,1)S(1)} %get-tuple-element.91.adj_ref, bf16[2048,256]{1,0:T(8,128)(2,1)S(1)} %get-tuple-element.107.gsin_ref, ...), custom_call_target="tpu_custom_call" | custom-call | bytes 6361089 | tf_op jit(solution)/shard_map/pallas_call | solution.py:79
  90.1 10.6 %all_to_all.39.recv_ref = bf16[8,64,256]{2,1,0:T(8,128)(2,1)S(1)} all-to-all(bf16[8,64,256]{2,1,0:T(8,128)(2,1)S(1)} %get-tuple-element.117), channel_id=1, replica_groups=mesh['dom'=8,'feat'=4] {'dom'}, dimensions={0} | all-to-all | bytes 524288 | tf_op jit(solution)/shard_map/all_to_all | solution.py:623
  100.7 0.0 copy-start.8
  100.7 0.0 copy-start.9
  100.8 0.0 copy-start.10
  100.8 0.0 copy-start.11
  100.8 0.0 copy-start.12
  100.8 0.0 copy-start.13
  100.8 0.0 copy-start.16
  100.8 0.0 copy-start.17
  100.8 0.0 copy-start.18
  100.8 5.4 %shard_map.329 = bf16[8,112,256]{2,1,0:T(8,128)(2,1)S(1)} custom-call(bf16[2048,2048]{1,0:T(8,128)(2,1)S(1)} %get-tuple-element.91.adj_ref, bf16[2048,256]{1,0:T(8,128)(2,1)S(1)} %get-tuple-element.115.gsin_ref, bf16[2048,256]{1,0:T(8,128)(2,1)S(1)} %get-tuple-element.116.grad_ref, bf16[2,256,256]{2,1,0:T(8,128)(2,1)S(1)} %copy-done, ...), custom_call_target="tpu_custom_call" | custom-call | bytes 4707329 | tf_op jit(solution)/shard_map/pallas_call | solution.py:79
  106.2 12.6 %all_to_all.40.recv_ref = bf16[8,112,256]{2,1,0:T(8,128)(2,1)S(1)} all-to-all(bf16[8,112,256]{2,1,0:T(8,128)(2,1)S(1)} %shard_map.329), channel_id=1, replica_groups=mesh['dom'=8,'feat'=4] {'dom'}, dimensions={0} | all-to-all | bytes 917504 | tf_op jit(solution)/shard_map/all_to_all | solution.py:623
  118.8 0.2 shard_map.330
  119.0 0.1 collective-permute-start.5
  119.1 1.6 %collective-permute-start.4 = (f32[8,128]{1,0:T(8,128)S(1)}, f32[8,128]{1,0:T(8,128)S(1)}, u32[]{:S(2)}, u32[]{:S(2)}) collective-permute-start(f32[8,128]{1,0:T(8,128)S(1)} %get-tuple-element.125.sq0_ref), channel_id=1, source_target_pairs={{0,2},{1,3},{2,0},{3,1},{4,6},{5,7},{6,4},{7,5},{8,10},{9,11},{10,... | collective-permute-start | bytes 12296 | tf_op jit(solution)/shard_map/ppermute | solution.py:751
  120.7 0.3 collective-permute-start.3
  120.9 0.7 shard_map.331
  121.7 0.4 collective-permute-done.5.sq3_ref
  122.1 0.7 collective-permute-done.4.sq2_ref
  122.8 0.0 collective-permute-done.3.sq1_ref
  122.8 0.0 copy-done.6
  122.8 0.0 copy-done.8
  122.8 0.0 copy-done.9
  122.8 0.0 copy-done.10
  122.8 0.0 copy-done.11
  122.8 0.0 copy-done.12
  122.9 1.4 %shard_map.332 = (f32[1,1]{1,0:T(1,128)}, f32[1,1]{1,0:T(1,128)}, f32[1,1]{1,0:T(1,128)}, f32[25,2,256]{2,1,0:T(2,128)}, f32[2,64,256]{2,1,0:T(8,128)}, /*index=...) custom-call(f32[8,128]{1,0:T(8,128)S(1)} %get-tuple-element.124.tota, ...), custom_call_target="tpu_custom_call" | custom-call | bytes 394819 | tf_op jit(solution)/shard_map/pallas_call | solution.py:79
  (23 shorter events, 0.0 us)
Async XLA Ops:
  3.2 10.5 %copy-start.4 = (bf16[480,256]{1,0:T(8,128)(2,1)}, bf16[480,256]{1,0:T(8,128)(2,1)S(1)}, u32[]{:S(2)}) copy-start(bf16[480,256]{1,0:T(8,128)(2,1)S(1)} %get-tuple-element.85.own_hbm) | copy-start | bytes 737284
  3.2 9.0 %collective-permute-start = (bf16[480,256]{1,0:T(8,128)(2,1)S(1)}, bf16[480,256]{1,0:T(8,128)(2,1)S(1)}, u32[]{:S(2)}, u32[]{:S(2)}) collective-permute-start(bf16[480,256]{1,0:T(8,128)(2,1)S(1)} %get-tuple-element.85.own_hbm), channel_id=1, source_target_pairs={{0,2},{1,3},{2,0},{3,1},{4,6},{5,7},{6,4},{7,5},{8,10},{9,11},{10,... | collective-permute-start | bytes 737288 | tf_op jit(solution)/shard_map/ppermute | solution.py:687
  6.2 13.2 %all-to-all-start = ((bf16[32,16,128]{2,1,0:T(8,128)(2,1)}), bf16[32,16,128]{2,1,0:T(8,128)(2,1)S(1)}, u32[]{:S(2)}, u32[]{:S(2)}) async-start(bf16[32,16,128]{2,1,0:T(8,128)(2,1)} %bitcast.4), calls=%async_computation | async-start | bytes 262144 | tf_op jit(solution)/shard_map/all_to_all | solution.py:684
  11.2 1.6 %collective-permute-start.1 = (bf16[480,256]{1,0:T(8,128)(2,1)S(1)}, bf16[480,256]{1,0:T(8,128)(2,1)S(1)}, u32[]{:S(2)}, u32[]{:S(2)}) collective-permute-start(bf16[480,256]{1,0:T(8,128)(2,1)S(1)} %get-tuple-element.85.own_hbm), channel_id=1, source_target_pairs={{0,1},{1,0},{2,3},{3,2},{4,5},{5,4},{6,7},{7,6},{8,9},{9,8},{10,11... | collective-permute-start | bytes 737288 | tf_op jit(solution)/shard_map/ppermute | solution.py:688
  12.2 1.5 %copy-start.19 = (bf16[480,256]{1,0:T(8,128)(2,1)}, bf16[480,256]{1,0:T(8,128)(2,1)S(1)}, u32[]{:S(2)}) copy-start(bf16[480,256]{1,0:T(8,128)(2,1)S(1)} %collective-permute-done.chip_hbm) | copy-start | bytes 737284
  12.2 1.5 %collective-permute-start.2 = (bf16[480,256]{1,0:T(8,128)(2,1)S(1)}, bf16[480,256]{1,0:T(8,128)(2,1)S(1)}, u32[]{:S(2)}, u32[]{:S(2)}) collective-permute-start(bf16[480,256]{1,0:T(8,128)(2,1)S(1)} %collective-permute-done.chip_hbm), channel_id=1, source_target_pairs={{0,1},{1,0},{2,3},{3,2},{4,5},{5,4},{6,7},{7,6},{8,9},{9,8},{10,11... | collective-permute-start | bytes 737288 | tf_op jit(solution)/shard_map/ppermute | solution.py:689
  19.4 21.4 %copy-start = (bf16[2,256,256]{2,1,0:T(8,128)(2,1)S(1)}, bf16[2,256,256]{2,1,0:T(8,128)(2,1)}, u32[]{:S(2)}) copy-start(bf16[2,256,256]{2,1,0:T(8,128)(2,1)} %get-tuple-element.95.w_ref) | copy-start | bytes 786436
  19.4 21.4 %copy-start.7 = (f32[8,256]{1,0:T(8,128)S(1)}, f32[8,256]{1,0:T(8,128)}, u32[]{:S(2)}) copy-start(f32[8,256]{1,0:T(8,128)} %get-tuple-element.89.norm_hbm.norm_ref) | copy-start | bytes 24580
  40.8 15.2 %copy-start.2 = (bf16[2,128,256]{2,1,0:T(8,128)(2,1)S(1)}, bf16[2,128,256]{2,1,0:T(8,128)(2,1)}, u32[]{:S(2)}) copy-start(bf16[2,128,256]{2,1,0:T(8,128)(2,1)} %get-tuple-element.100.w_ref.wout_ref) | copy-start | bytes 393220
  40.8 15.2 %copy-start.14 = (s32[2048]{0:T(1024)S(1)}, s32[2048]{0:T(1024)}, u32[]{:S(2)}) copy-start(s32[2048]{0:T(1024)} %param.25) | copy-start | bytes 24580
  56.0 15.3 %copy-start.15 = (s32[2048]{0:T(1024)S(1)}, s32[2048]{0:T(1024)}, u32[]{:S(2)}) copy-start(s32[2048]{0:T(1024)} %param.24) | copy-start | bytes 24580
  83.9 16.8 %copy-start.1 = (bf16[128,2048]{1,0:T(8,128)(2,1)S(1)}, bf16[128,2048]{1,0:T(8,128)(2,1)}, u32[]{:S(2)}) copy-start(bf16[128,2048]{1,0:T(8,128)(2,1)} %get-tuple-element.87.ft_hbm.ft_ref) | copy-start | bytes 1572868
  100.7 22.0 %copy-start.3 = (f32[2,64,256]{2,1,0:T(8,128)S(1)}, f32[2,64,256]{2,1,0:T(8,128)}, u32[]{:S(2)}) copy-start(f32[2,64,256]{2,1,0:T(8,128)} %refs_5_.1) | copy-start | bytes 393220
  100.7 22.1 %copy-start.5 = (f32[2,25,256]{2,0,1:T(2,128)S(1)}, f32[2,25,256]{2,0,1:T(2,128)}, u32[]{:S(2)}) copy-start(f32[2,25,256]{2,0,1:T(2,128)} %param.26) | copy-start | bytes 153604
  100.7 22.1 %copy-start.6 = (f32[2,64,47]{1,0,2:T(2,128)S(1)}, f32[2,64,47]{1,0,2:T(2,128)}, u32[]{:S(2)}) copy-start(f32[2,64,47]{1,0,2:T(2,128)} %param.28) | copy-start | bytes 72196
  100.7 22.1 %copy-start.8 = (f32[2,64,256]{2,1,0:T(8,128)S(1)}, f32[2,64,256]{2,1,0:T(8,128)}, u32[]{:S(2)}) copy-start(f32[2,64,256]{2,1,0:T(8,128)} %refs_9_.1) | copy-start | bytes 393220
  100.7 22.1 %copy-start.9 = (f32[2,64,256]{2,1,0:T(8,128)S(1)}, f32[2,64,256]{2,1,0:T(8,128)}, u32[]{:S(2)}) copy-start(f32[2,64,256]{2,1,0:T(8,128)} %refs_13_.1) | copy-start | bytes 393220
  100.8 22.1 %copy-start.10 = (f32[2,25,256]{2,0,1:T(2,128)S(1)}, f32[2,25,256]{2,0,1:T(2,128)}, u32[]{:S(2)}) copy-start(f32[2,25,256]{2,0,1:T(2,128)} %param.30) | copy-start | bytes 153604
  100.8 22.0 %copy-start.11 = (f32[2,25,256]{2,0,1:T(2,128)S(1)}, f32[2,25,256]{2,0,1:T(2,128)}, u32[]{:S(2)}) copy-start(f32[2,25,256]{2,0,1:T(2,128)} %param.34) | copy-start | bytes 153604
  100.8 22.0 %copy-start.12 = (f32[2,64,47]{1,0,2:T(2,128)S(1)}, f32[2,64,47]{1,0,2:T(2,128)}, u32[]{:S(2)}) copy-start(f32[2,64,47]{1,0,2:T(2,128)} %param.32) | copy-start | bytes 72196
  100.8 22.0 %copy-start.13 = (f32[2,64,47]{1,0,2:T(2,128)S(1)}, f32[2,64,47]{1,0,2:T(2,128)}, u32[]{:S(2)}) copy-start(f32[2,64,47]{1,0,2:T(2,128)} %param.36) | copy-start | bytes 72196
  100.8 22.0 %copy-start.16 = (f32[2,2,64]{2,1,0:T(2,128)S(1)}, f32[2,2,64]{2,1,0:T(2,128)}, u32[]{:S(2)}) copy-start(f32[2,2,64]{2,1,0:T(2,128)} %refs_7_.1) | copy-start | bytes 3076
  100.8 22.0 %copy-start.17 = (f32[2,2,64]{2,1,0:T(2,128)S(1)}, f32[2,2,64]{2,1,0:T(2,128)}, u32[]{:S(2)}) copy-start(f32[2,2,64]{2,1,0:T(2,128)} %refs_11_.1) | copy-start | bytes 3076
  100.8 22.0 %copy-start.18 = (f32[2,2,64]{2,1,0:T(2,128)S(1)}, f32[2,2,64]{2,1,0:T(2,128)}, u32[]{:S(2)}) copy-start(f32[2,2,64]{2,1,0:T(2,128)} %refs_15_.1) | copy-start | bytes 3076
  119.0 3.1 %collective-permute-start.5 = (f32[8,128]{1,0:T(8,128)S(1)}, f32[8,128]{1,0:T(8,128)S(1)}, u32[]{:S(2)}, u32[]{:S(2)}) collective-permute-start(f32[8,128]{1,0:T(8,128)S(1)} %get-tuple-element.125.sq0_ref), channel_id=1, source_target_pairs={{0,3},{1,2},{2,1},{3,0},{4,7},{5,6},{6,5},{7,4},{8,11},{9,10},{10,... | collective-permute-start | bytes 12296 | tf_op jit(solution)/shard_map/ppermute | solution.py:751
  119.1 3.7 %collective-permute-start.4 = (f32[8,128]{1,0:T(8,128)S(1)}, f32[8,128]{1,0:T(8,128)S(1)}, u32[]{:S(2)}, u32[]{:S(2)}) collective-permute-start(f32[8,128]{1,0:T(8,128)S(1)} %get-tuple-element.125.sq0_ref), channel_id=1, source_target_pairs={{0,2},{1,3},{2,0},{3,1},{4,6},{5,7},{6,4},{7,5},{8,10},{9,11},{10,... | collective-permute-start | bytes 12296 | tf_op jit(solution)/shard_map/ppermute | solution.py:751
  120.7 2.1 %collective-permute-start.3 = (f32[8,128]{1,0:T(8,128)S(1)}, f32[8,128]{1,0:T(8,128)S(1)}, u32[]{:S(2)}, u32[]{:S(2)}) collective-permute-start(f32[8,128]{1,0:T(8,128)S(1)} %get-tuple-element.125.sq0_ref), channel_id=1, source_target_pairs={{0,1},{1,0},{2,3},{3,2},{4,5},{5,4},{6,7},{7,6},{8,9},{9,8},{10,11... | collective-permute-start | bytes 12296 | tf_op jit(solution)/shard_map/ppermute | solution.py:751
